TPU v7x, 512 devices: a whole 4x8x8 slice. The times are simulated.
512 devices in a mesh: grp: 8 (over x, core), col: 64 (over z, y).
Axes of the slice: x: 4, y: 8, z: 8, core: 2. Of those that a mesh axis runs over, the one named last changes fastest.
Arguments:
- panel_blocks: bfloat16 [1024, 128, 128], P(('grp', 'col')), may hold values from -6 to 6
- panel_rows: int32 [1024], P(('grp', 'col')), may hold values from 0 to 7, as said below
- panel_inner: int32 [1024], P(('grp', 'col')), may hold values from 0 to 63, as said below
- right_blocks: bfloat16 [64, 256, 128, 128], P('grp', 'col'), may hold values from -0.1875 to 0.1875
- right_columns: int32 [64, 256], P('grp', 'col'), may hold values from 0 to 7, as said below
Outputs:
- product: bfloat16 [8192, 65536], P('grp', 'col')
Inputs may be any that keep to these rules, and one draw needn't show every extreme that they name: Within one group the pairs (panel_rows, panel_inner) are distinct, and every block row of a group has exactly 16 blocks. Within one group the pairs (panel_rows, panel_inner) are distinct. `right_columns`: the 4 block columns listed for one block row and one column set are distinct.
All inputs are finite; a program needn't handle non-finite values.
Results may differ from a plain program's by a relative error of at most 0.001.
Values may be sent and summed in bfloat16 or wider, within the bound.
No kernel may reach another device: no remote copies, remote signals or barrier semaphores. Data moves between devices by JAX's collectives and lax.ppermute only.
A program may use at most 128 MiB of HBM per device.

v0:
```python
import jax
import jax.numpy as jnp
from jax import lax
from jax.sharding import PartitionSpec as P

BS = 128
RG = 8
JB = 8
NBR = 4


def dense_strips(section_blocks, section_columns):
    section_count = section_blocks.shape[0]
    hits = (
        section_columns[:, :, None] == lax.broadcasted_iota(jnp.int32, (section_count, NBR, JB), 2)
    ).astype(jnp.bfloat16)
    placed = jnp.einsum("kmj,kmab->kajb", hits, section_blocks, preferred_element_type=jnp.float32)
    return placed.astype(jnp.bfloat16).reshape(section_count, BS, JB * BS)


def body(panel_blocks, panel_rows, panel_inner, right_blocks, right_columns):
    section_blocks, section_columns = (
        lax.all_gather(right_blocks, "grp", axis=0, tiled=True),
        lax.all_gather(right_columns, "grp", axis=0, tiled=True),
    )
    strips = dense_strips(section_blocks, section_columns)
    blocks, row_ids, inner_ids = (
        lax.all_gather(panel_blocks, "col", axis=0, tiled=True),
        lax.all_gather(panel_rows, "col", axis=0, tiled=True),
        lax.all_gather(panel_inner, "col", axis=0, tiled=True),
    )
    count = blocks.shape[0]
    per_row = count // RG
    order = jnp.argsort(row_ids, stable=True)
    sorted_blocks = blocks[order].reshape(RG, per_row, BS, BS)
    sorted_inner = inner_ids[order].reshape(RG, per_row)

    def one_row(pieces):
        chosen = strips[pieces[1]]
        return jnp.einsum("pab,pbn->an", pieces[0], chosen, preferred_element_type=jnp.float32)

    running = lax.map(one_row, (sorted_blocks, sorted_inner))
    return running.reshape(RG * BS, JB * BS).astype(jnp.bfloat16)


def solution(mesh):
    placed = (
        P(("grp", "col"), None, None),
        P(("grp", "col")),
        P(("grp", "col")),
        P("grp", "col", None, None),
        P("grp", "col"),
    )
    return jax.shard_map(
        body, mesh=mesh, in_specs=placed, out_specs=P("grp", "col"), check_vma=False
    )
```

profile of v0, /device:TPU:6, one launch (start us, length us, event | category | flops | bytes accessed | tf_op | source)
XLA Modules:
  0.0 300.5 jit_solution(5207696284654952855)
XLA Ops:
  6.5 0.0 all-gather.4.cloned.1.call-start
  6.5 0.7 all-gather.4.cloned.1.call-update
  7.3 0.0 all-gather.6.cloned.1.call-start
  7.3 0.7 all-gather.6.cloned.1.call-update
  8.0 1.3 dynamic-slice
  9.9 0.9 dynamic-update-slice
  10.8 0.8 dynamic-update-slice.1
  11.6 31.7 %all-reduce.2 = (s32[128]{0:T(128)S(1)}, s32[128]{0:T(128)S(1)}) all-reduce(s32[128]{0:T(128)S(1)} %dynamic-update-slice, s32[128]{0:T(128)S(1)} %dynamic-update-slice.1), channel_id=1, replica_groups=mesh['grp'=8,'col'=64] {'col'}, use_global_device_ids=true, to_apply=%add | all-reduce | flops 256 | bytes 2048
  43.4 2.6 sort.17
  46.0 1.2 gather_fusion.2
  47.2 0.1 reshape.41
  47.3 11.1 %all-gather = s32[8,8,4]{1,2,0:T(4,128)S(1)} all-gather(s32[1,8,4]{1,2,0:T(4,128)} %bitcast.43), channel_id=1, replica_groups=mesh['grp'=8,'col'=64] {'grp'}, dimensions={0}, use_global_device_ids=true | all-gather | bytes 1152 | tf_op jit(solution)/shard_map/all_gather | solution.py:24
  58.4 0.1 copy.14
  58.5 45.0 %all-gather.4.cloned.1.call-done = bf16[128,128,128]{2,1,0:T(8,128)(2,1)} async-done(((bf16[2,128,128]{2,1,0:T(8,128)(2,1)}), bf16[128,128,128]{2,1,0:T(8,128)(2,1)}) %all-gather.4.cloned.1.call-update) | async-done | bytes 4194320 | tf_op jit(solution)/shard_map/all_gather | solution.py:28
  103.5 5.3 %gather_fusion.1 = bf16[128,128,128]{2,1,0:T(8,128)(2,1)} fusion(bf16[128,128,128]{2,1,0:T(8,128)(2,1)} %all-gather.4.cloned.1.call-done, s32[1024]{0:T(1024)S(1)} %pad_clamp_fusion.1), kind=kCustom, calls=%fused_computation.1 | custom fusion | bytes 8389120 | tf_op jit(solution)/shard_map/gather | solution.py:35
  108.8 46.8 %all-gather.6.cloned.1.call-done = bf16[64,4,128,128]{3,2,1,0:T(8,128)(2,1)} async-done(((bf16[8,4,128,128]{3,2,1,0:T(8,128)(2,1)}), bf16[64,4,128,128]{3,2,1,0:T(8,128)(2,1)}) %all-gather.6.cloned.1.call-update) | async-done | bytes 8388624 | tf_op jit(solution)/shard_map/all_gather | solution.py:23
  155.6 14.3 %convert_bitcast_fusion = bf16[64,128,8,128]{3,2,1,0:T(8,128)(2,1)} fusion(bf16[64,4,128,128]{3,2,1,0:T(8,128)(2,1)} %all-gather.6.cloned.1.call-done, s32[64,4]{1,0:T(8,128)S(1)} %bitcast.42), kind=kOutput, calls=%fused_computation.13 | convolution fusion | flops 75499520 | bytes 25166848 | tf_op jit(solution)/shard_map/kmj,kmab->kajb/dot_general | solution.py:17
  170.0 25.3 %reshape.42 = bf16[64,128,1024]{2,1,0:T(8,128)(2,1)} reshape(bf16[64,128,8,128]{3,2,1,0:T(8,128)(2,1)} %convert_bitcast_fusion) | data formatting | bytes 33554432 | tf_op jit(solution)/shard_map/reshape | solution.py:18
  195.3 98.4 %while.10 = (s32[]{:T(128)}, bf16[8,128,1024]{2,1,0:T(8,128)(2,1)}, bf16[8,16,128,128]{3,2,1,0:T(8,128)(2,1)}, s32[8,16]{1,0:T(8,128)S(1)}, bf16[64,128,1024]{2,1,0:T(8,128)(2,1)}, /*index=5*/s32[]{:T(128)}) while((s32[]{:T(128)}, bf16[8,128,1024]{2,1,0:T(8,128)(2,1)}, bf16[8,16,128,128]{3,2,1,0:T(8,128)(2,1)}, s32[8,16]{1,0:T(8,128)S(1)}, ...), condition=%wide.region_2.3_spmd, body=%wide.region_1.2_spmd.sunk | while | flops 536872000 | bytes 13636937 | solution.py:42
  195.3 8.5 %gather_fusion = bf16[16,128,1024]{2,1,0:T(8,128)(2,1)} fusion(bf16[64,128,1024]{2,1,0:T(8,128)(2,1)} %get-tuple-element.94, s32[1024]{0:T(1024)S(1)} %pad_clamp_fusion.3), kind=kCustom, calls=%fused_computation.clone.1 | custom fusion | bytes 8388672 | tf_op jit(solution)/shard_map/while/body/eval_jaxpr/gather | solution.py:39
  203.8 3.8 %fusion.18 = bf16[8,128,1024]{2,1,0:T(8,128)(2,1)} fusion(bf16[8,128,1024]{2,1,0:T(8,128)(2,1)} %get-tuple-element.85, s32[]{:T(128)} %get-tuple-element.84, bf16[16,128,1024]{2,1,0:T(8,128)(2,1)} %gather_fusion, bf16[8,16,128,128]{3,2,1,0:T(8,128)(2,1)} %get-tuple-element.92), kind=kOutput, calls=%fused_computation.4.clone.1 | convolution fusion | flops 536870912 | bytes 5243904 | tf_op jit(solution)/shard_map/while/body/eval_jaxpr/pab,pbn->an/dot_general | solution.py:40
  207.6 8.5 %gather_fusion = bf16[16,128,1024]{2,1,0:T(8,128)(2,1)} fusion(bf16[64,128,1024]{2,1,0:T(8,128)(2,1)} %get-tuple-element.94, s32[1024]{0:T(1024)S(1)} %pad_clamp_fusion.3), kind=kCustom, calls=%fused_computation.clone.1 | custom fusion | bytes 8388672 | tf_op jit(solution)/shard_map/while/body/eval_jaxpr/gather | solution.py:39
  216.1 3.8 %fusion.18 = bf16[8,128,1024]{2,1,0:T(8,128)(2,1)} fusion(bf16[8,128,1024]{2,1,0:T(8,128)(2,1)} %get-tuple-element.85, s32[]{:T(128)} %get-tuple-element.84, bf16[16,128,1024]{2,1,0:T(8,128)(2,1)} %gather_fusion, bf16[8,16,128,128]{3,2,1,0:T(8,128)(2,1)} %get-tuple-element.92), kind=kOutput, calls=%fused_computation.4.clone.1 | convolution fusion | flops 536870912 | bytes 5243904 | tf_op jit(solution)/shard_map/while/body/eval_jaxpr/pab,pbn->an/dot_general | solution.py:40
  219.9 8.5 %gather_fusion = bf16[16,128,1024]{2,1,0:T(8,128)(2,1)} fusion(bf16[64,128,1024]{2,1,0:T(8,128)(2,1)} %get-tuple-element.94, s32[1024]{0:T(1024)S(1)} %pad_clamp_fusion.3), kind=kCustom, calls=%fused_computation.clone.1 | custom fusion | bytes 8388672 | tf_op jit(solution)/shard_map/while/body/eval_jaxpr/gather | solution.py:39
  228.4 3.8 %fusion.18 = bf16[8,128,1024]{2,1,0:T(8,128)(2,1)} fusion(bf16[8,128,1024]{2,1,0:T(8,128)(2,1)} %get-tuple-element.85, s32[]{:T(128)} %get-tuple-element.84, bf16[16,128,1024]{2,1,0:T(8,128)(2,1)} %gather_fusion, bf16[8,16,128,128]{3,2,1,0:T(8,128)(2,1)} %get-tuple-element.92), kind=kOutput, calls=%fused_computation.4.clone.1 | convolution fusion | flops 536870912 | bytes 5243904 | tf_op jit(solution)/shard_map/while/body/eval_jaxpr/pab,pbn->an/dot_general | solution.py:40
  232.2 8.5 %gather_fusion = bf16[16,128,1024]{2,1,0:T(8,128)(2,1)} fusion(bf16[64,128,1024]{2,1,0:T(8,128)(2,1)} %get-tuple-element.94, s32[1024]{0:T(1024)S(1)} %pad_clamp_fusion.3), kind=kCustom, calls=%fused_computation.clone.1 | custom fusion | bytes 8388672 | tf_op jit(solution)/shard_map/while/body/eval_jaxpr/gather | solution.py:39
  240.7 3.8 %fusion.18 = bf16[8,128,1024]{2,1,0:T(8,128)(2,1)} fusion(bf16[8,128,1024]{2,1,0:T(8,128)(2,1)} %get-tuple-element.85, s32[]{:T(128)} %get-tuple-element.84, bf16[16,128,1024]{2,1,0:T(8,128)(2,1)} %gather_fusion, bf16[8,16,128,128]{3,2,1,0:T(8,128)(2,1)} %get-tuple-element.92), kind=kOutput, calls=%fused_computation.4.clone.1 | convolution fusion | flops 536870912 | bytes 5243904 | tf_op jit(solution)/shard_map/while/body/eval_jaxpr/pab,pbn->an/dot_general | solution.py:40
  244.5 8.5 %gather_fusion = bf16[16,128,1024]{2,1,0:T(8,128)(2,1)} fusion(bf16[64,128,1024]{2,1,0:T(8,128)(2,1)} %get-tuple-element.94, s32[1024]{0:T(1024)S(1)} %pad_clamp_fusion.3), kind=kCustom, calls=%fused_computation.clone.1 | custom fusion | bytes 8388672 | tf_op jit(solution)/shard_map/while/body/eval_jaxpr/gather | solution.py:39
  253.0 3.8 %fusion.18 = bf16[8,128,1024]{2,1,0:T(8,128)(2,1)} fusion(bf16[8,128,1024]{2,1,0:T(8,128)(2,1)} %get-tuple-element.85, s32[]{:T(128)} %get-tuple-element.84, bf16[16,128,1024]{2,1,0:T(8,128)(2,1)} %gather_fusion, bf16[8,16,128,128]{3,2,1,0:T(8,128)(2,1)} %get-tuple-element.92), kind=kOutput, calls=%fused_computation.4.clone.1 | convolution fusion | flops 536870912 | bytes 5243904 | tf_op jit(solution)/shard_map/while/body/eval_jaxpr/pab,pbn->an/dot_general | solution.py:40
  256.8 8.5 %gather_fusion = bf16[16,128,1024]{2,1,0:T(8,128)(2,1)} fusion(bf16[64,128,1024]{2,1,0:T(8,128)(2,1)} %get-tuple-element.94, s32[1024]{0:T(1024)S(1)} %pad_clamp_fusion.3), kind=kCustom, calls=%fused_computation.clone.1 | custom fusion | bytes 8388672 | tf_op jit(solution)/shard_map/while/body/eval_jaxpr/gather | solution.py:39
  265.3 3.8 %fusion.18 = bf16[8,128,1024]{2,1,0:T(8,128)(2,1)} fusion(bf16[8,128,1024]{2,1,0:T(8,128)(2,1)} %get-tuple-element.85, s32[]{:T(128)} %get-tuple-element.84, bf16[16,128,1024]{2,1,0:T(8,128)(2,1)} %gather_fusion, bf16[8,16,128,128]{3,2,1,0:T(8,128)(2,1)} %get-tuple-element.92), kind=kOutput, calls=%fused_computation.4.clone.1 | convolution fusion | flops 536870912 | bytes 5243904 | tf_op jit(solution)/shard_map/while/body/eval_jaxpr/pab,pbn->an/dot_general | solution.py:40
  269.1 8.5 %gather_fusion = bf16[16,128,1024]{2,1,0:T(8,128)(2,1)} fusion(bf16[64,128,1024]{2,1,0:T(8,128)(2,1)} %get-tuple-element.94, s32[1024]{0:T(1024)S(1)} %pad_clamp_fusion.3), kind=kCustom, calls=%fused_computation.clone.1 | custom fusion | bytes 8388672 | tf_op jit(solution)/shard_map/while/body/eval_jaxpr/gather | solution.py:39
  277.6 3.8 %fusion.18 = bf16[8,128,1024]{2,1,0:T(8,128)(2,1)} fusion(bf16[8,128,1024]{2,1,0:T(8,128)(2,1)} %get-tuple-element.85, s32[]{:T(128)} %get-tuple-element.84, bf16[16,128,1024]{2,1,0:T(8,128)(2,1)} %gather_fusion, bf16[8,16,128,128]{3,2,1,0:T(8,128)(2,1)} %get-tuple-element.92), kind=kOutput, calls=%fused_computation.4.clone.1 | convolution fusion | flops 536870912 | bytes 5243904 | tf_op jit(solution)/shard_map/while/body/eval_jaxpr/pab,pbn->an/dot_general | solution.py:40
  281.4 8.5 %gather_fusion = bf16[16,128,1024]{2,1,0:T(8,128)(2,1)} fusion(bf16[64,128,1024]{2,1,0:T(8,128)(2,1)} %get-tuple-element.94, s32[1024]{0:T(1024)S(1)} %pad_clamp_fusion.3), kind=kCustom, calls=%fused_computation.clone.1 | custom fusion | bytes 8388672 | tf_op jit(solution)/shard_map/while/body/eval_jaxpr/gather | solution.py:39
  289.9 3.8 %fusion.18 = bf16[8,128,1024]{2,1,0:T(8,128)(2,1)} fusion(bf16[8,128,1024]{2,1,0:T(8,128)(2,1)} %get-tuple-element.85, s32[]{:T(128)} %get-tuple-element.84, bf16[16,128,1024]{2,1,0:T(8,128)(2,1)} %gather_fusion, bf16[8,16,128,128]{3,2,1,0:T(8,128)(2,1)} %get-tuple-element.92), kind=kOutput, calls=%fused_computation.4.clone.1 | convolution fusion | flops 536870912 | bytes 5243904 | tf_op jit(solution)/shard_map/while/body/eval_jaxpr/pab,pbn->an/dot_general | solution.py:40
  (22 shorter events, 0.1 us)
Async XLA Ops:
  6.5 97.0 %all-gather.4.cloned.1.call-start = ((), (), s32[]{:S(2)}) async-start(), calls=%async_computation | async-start | bytes 4259840 | tf_op jit(solution)/shard_map/all_gather | solution.py:28
  7.3 148.3 %all-gather.6.cloned.1.call-start = ((), (), s32[]{:S(2)}) async-start(), calls=%async_computation.1 | async-start | bytes 9437184 | tf_op jit(solution)/shard_map/all_gather | solution.py:23
Sparse Core Ops, SparseCore 0:
  10.4 93.0 all-gather.3
  105.7 49.8 all-gather.5
where the time goes:
time: 305 us; the launch traced here: 300 us
  local copies, waits for them, and re-layouts  103 us (34%)
  waiting for transfers between devices  93.2 us (31%)
  matrix products  44.6 us (15%)
  blocking collectives  42.8 us (14%)
  between operations  14.1 us (5%)
    gather x8, local copies, waits for them, and re-layouts, one_row(): chosen = strips[pieces[1]]  68.1 us
    all_gather x1, waiting for transfers between devices, body(): lax.all_gather(right_blocks, 'grp', axis=0, tiled=True)  46.8 us
    all_gather x1, waiting for transfers between devices, body(): lax.all_gather(panel_blocks, 'col', axis=0, tiled=True)  45 us
    unnamed x1, blocking collectives  31.7 us
    dot_general x8, matrix products, one_row(): jnp.einsum('pab,pbn->an', pieces[0], chosen, preferred_element_type=jnp.f...  30.2 us
    reshape x1, local copies, waits for them, and re-layouts, dense_strips(): return placed.astype(jnp.bfloat16).reshape(section_count, BS, JB * BS)  25.3 us
    dot_general x1, matrix products, dense_strips(): jnp.einsum('kmj,kmab->kajb', hits, section_blocks, preferred_element_type...  14.3 us
    all_gather x1, blocking collectives, body(): lax.all_gather(right_columns, 'grp', axis=0, tiled=True)  11.1 us
  transfers between devices with their start and end apart: 2, of which 2 were waited for; matrix products, arithmetic and copies ran while one was open for 4% of the time, Pallas kernels for 0%

commit v1 on v0

v1 whole, which is shorter than its diff:
```python
import jax
import jax.numpy as jnp
from jax import lax
from jax.experimental import pallas as pl
from jax.experimental.pallas import tpu as pltpu
from jax.sharding import PartitionSpec as P

BS = 128
RG = 8
KS = 64
JB = 8
NBR = 4
PER_ROW = 16
N_X = 4
N_Y = 8
N_Z = 8
PAD = 16
OWN_K = 8
R_ROWS = OWN_K * NBR * BS
L_ROWS = 2 * BS
N_LEFT = 128
N_RIGHT = KS * NBR


def shift_x(step):
    return [(x * 2 + c, ((x + step) % N_X) * 2 + c) for x in range(N_X) for c in range(2)]


SWAP_CORES = [(g, g ^ 1) for g in range(2 * N_X)]
Y_LINES = [[z * N_Y + y for y in range(N_Y)] for z in range(N_Z)]
Z_LINES = [[z * N_Y + y for z in range(N_Z)] for y in range(N_Y)]


def multiply_kernel(place, columns, ids, left, *refs):
    pieces, (out, left_buf, right_buf, table, order, filled, sem) = refs[:10], refs[10:]
    row = pl.program_id(0)

    @pl.when(row == 0)
    def load():
        copies = [pltpu.make_async_copy(left, left_buf, sem.at[0])]
        slot = 0
        for i, piece in enumerate(pieces):
            rows = piece.shape[0]
            blocks = rows // BS
            copies.append(
                pltpu.make_async_copy(
                    piece.at[pl.ds(0, blocks * BS)],
                    right_buf.at[pl.ds(slot * BS, blocks * BS)],
                    sem.at[i + 1],
                )
            )
            slot += blocks
        for copy in copies:
            copy.start()
        right_buf[pl.ds(N_RIGHT * BS, BS), :] = jnp.zeros((BS, BS), jnp.bfloat16)
        own_x, own_core = place[0] // 2, place[0] % 2
        for r in range(RG):
            filled[r] = 0

        def list_row(i, carry):
            device, b = i // 2, i % 2
            r = ids[device * 4 + b]
            n = filled[r]
            order[(r * PER_ROW + n) * 2] = device * (L_ROWS + PAD) + b * BS
            order[(r * PER_ROW + n) * 2 + 1] = ids[device * 4 + 2 + b]
            filled[r] = n + 1
            return carry

        lax.fori_loop(0, N_LEFT, list_row, 0, unroll=4)

        def clear(i, carry):
            table[i] = N_RIGHT * BS
            return carry

        lax.fori_loop(0, KS * JB, clear, 0, unroll=16)

        def fill(k, carry):
            g = k // OWN_K
            s = ((g + own_core) % 2) * N_X + (g // 2 + N_X - own_x) % N_X
            first = (s * OWN_K + k % OWN_K) * NBR
            for m in range(NBR):
                table[k * JB + columns[first + m]] = (first + m) * BS
            return carry

        lax.fori_loop(0, KS, fill, 0, unroll=2)
        for copy in copies:
            copy.wait()

    starts = [pl.multiple_of(order[(row * PER_ROW + p) * 2], BS // 8) for p in range(PER_ROW)]
    inner = [order[(row * PER_ROW + p) * 2 + 1] * JB for p in range(PER_ROW)]
    lhs = jnp.concatenate([left_buf[pl.ds(s, BS), :] for s in starts], axis=1)
    for j in range(0, JB, 2):
        rhs = jnp.concatenate(
            [
                jnp.concatenate(
                    [right_buf[pl.ds(pl.multiple_of(table[k + j + h], BS), BS), :] for h in range(2)],
                    axis=1,
                )
                for k in inner
            ],
            axis=0,
        )
        out[:, j * BS : (j + 2) * BS] = jnp.dot(lhs, rhs, preferred_element_type=jnp.float32).astype(out.dtype)


def multiply(place, columns, ids, left, pieces):
    smem = pl.BlockSpec(memory_space=pltpu.SMEM)
    hbm = pl.BlockSpec(memory_space=pl.ANY)
    return pl.pallas_call(
        multiply_kernel,
        grid=(RG,),
        out_shape=jax.ShapeDtypeStruct((RG * BS, JB * BS), jnp.bfloat16),
        in_specs=[smem] * 3 + [hbm] * (1 + len(pieces)),
        out_specs=pl.BlockSpec((BS, JB * BS), lambda r: (r, 0)),
        scratch_shapes=[
            pltpu.VMEM(left.shape, jnp.bfloat16),
            pltpu.VMEM(((N_RIGHT + 1) * BS, BS), jnp.bfloat16),
            pltpu.SMEM((KS * JB,), jnp.int32),
            pltpu.SMEM((N_LEFT * 2,), jnp.int32),
            pltpu.SMEM((RG,), jnp.int32),
            pltpu.SemaphoreType.DMA((1 + len(pieces),)),
        ],
        compiler_params=pltpu.CompilerParams(vmem_limit_bytes=32 * 2**20),
        cost_estimate=pl.CostEstimate(flops=4 * 2**30, bytes_accessed=14 * 2**20, transcendentals=0),
    )(place, columns, ids, left, *pieces)


def tail(values):
    flat = values.astype(jnp.bfloat16).reshape(1, -1)
    return jnp.pad(flat, ((0, PAD - 1), (0, BS - flat.shape[1])))


def gather_right(own):
    after = lax.ppermute(own, "grp", shift_x(-1))
    before = lax.ppermute(own, "grp", shift_x(1))
    far_head = lax.ppermute(before[: R_ROWS // 2], "grp", shift_x(1))
    far_tail = lax.ppermute(after[R_ROWS // 2 :], "grp", shift_x(-1))
    mine = [own, after, far_head, far_tail, before]
    return mine + [lax.ppermute(v, "grp", SWAP_CORES) for v in mine]


def gather_left(own):
    copies = jnp.broadcast_to(own[None], (N_Y,) + own.shape)
    line = lax.all_to_all(copies, "col", 0, 0, axis_index_groups=Y_LINES)
    return lax.all_gather(line, "col", axis=0, tiled=True, axis_index_groups=Z_LINES)


def body(panel_blocks, panel_rows, panel_inner, right_blocks, right_columns):
    right = jnp.concatenate([right_blocks.reshape(R_ROWS, BS), tail(right_columns)])
    left = jnp.concatenate(
        [panel_blocks.reshape(L_ROWS, BS), tail(jnp.concatenate([panel_rows, panel_inner]))]
    )
    pieces = gather_right(right)
    lefts = gather_left(left)
    columns = jnp.concatenate(
        [v[-PAD, : OWN_K * NBR] for v in pieces if v.shape[0] % BS == PAD]
    ).astype(jnp.int32)
    ids = lefts[:, L_ROWS, :4].astype(jnp.int32).reshape(-1)
    place = lax.axis_index("grp").reshape(1)
    return multiply(place, columns, ids, lefts.reshape(-1, BS), pieces)


def solution(mesh):
    placed = (
        P(("grp", "col"), None, None),
        P(("grp", "col")),
        P(("grp", "col")),
        P("grp", "col", None, None),
        P("grp", "col"),
    )
    return jax.shard_map(
        body, mesh=mesh, in_specs=placed, out_specs=P("grp", "col"), check_vma=False
    )
```

time: 305 us -> 121 us (0.40)
  local copies, waits for them, and re-layouts: 103 us -> 10.1 us
  waiting for transfers between devices: 93.2 us -> 34.3 us
  matrix products: 44.6 us -> 0 us
  starting transfers between devices: 0.04 us -> 21.3 us
  blocking collectives: 42.8 us -> 25.3 us
  Pallas kernels: 0 us -> 11.9 us
    all_gather x2 -> x1, waiting for transfers between devices: 91.8 us -> 6.95 us  [gather_left(): lax.all_gather(line, 'col', axis=0, tiled=True, axis_index_groups=Z_LINES)]
    gather x10 -> x0, local copies, waits for them, and re-layouts: 74.6 us -> none  [the longest x8 68.1 us: one_row(): chosen = strips[pieces[1]]]
    dot_general x9 -> x0, matrix products: 44.6 us -> none  [the longest x8 30.2 us: one_row(): jnp.einsum('pab,pbn->an', pieces[0], chosen, preferred_element_type=jnp.f...]
    unnamed x1 -> x0, blocking collectives: 31.7 us -> none
    ppermute x0 -> x9, waiting for transfers between devices: none -> 27.3 us  [the longest x1 17.1 us: gather_right(): before = lax.ppermute(own, 'grp', shift_x(1))]
    all_to_all x0 -> x1, blocking collectives: none -> 25.3 us  [gather_left(): line = lax.all_to_all(copies, 'col', 0, 0, axis_index_groups=Y_LINES)]
    reshape x2 -> x1, local copies, waits for them, and re-layouts: 25.4 us -> 0.09 us  [tail(): flat = values.astype(jnp.bfloat16).reshape(1, -1)]
    ppermute x0 -> x9, starting transfers between devices: none -> 21.3 us  [the longest x5 9.57 us: gather_right(): return mine + [lax.ppermute(v, 'grp', SWAP_CORES) for v in mine]]
  transfers between devices with their start and end apart: 2 -> 10, of which waited for: 2 -> 4; matrix products, arithmetic and copies ran while one was open for 4% -> 2% of each run, Pallas kernels for 0% -> 0%
where the time goes in v1:
time: 121 us; the launch traced here: 119 us
  waiting for transfers between devices  34.3 us (28%)
  blocking collectives  25.3 us (21%)
  starting transfers between devices  21.3 us (18%)
  between operations  13.6 us (11%)
  Pallas kernels  11.9 us (10%)
  local copies, waits for them, and re-layouts  10.1 us (8%)
  other arithmetic  2.69 us (2%)
    all_to_all x1, blocking collectives, gather_left(): line = lax.all_to_all(copies, 'col', 0, 0, axis_index_groups=Y_LINES)  25.3 us
    ppermute x1, waiting for transfers between devices, gather_right(): before = lax.ppermute(own, 'grp', shift_x(1))  17.1 us
    pallas_call x1, Pallas kernels, multiply(): pl.pallas_call(multiply_kernel, grid=(RG,), out_shape=jax.ShapeDtypeStruc...  11.9 us
    ppermute x5, starting transfers between devices, gather_right(): return mine + [lax.ppermute(v, 'grp', SWAP_CORES) for v in mine]  9.57 us
    unnamed x18, local copies, waits for them, and re-layouts  8.18 us
    ppermute x1, waiting for transfers between devices, gather_right(): far_head = lax.ppermute(before[:R_ROWS // 2], 'grp', shift_x(1))  7.78 us
    all_gather x1, waiting for transfers between devices, gather_left(): lax.all_gather(line, 'col', axis=0, tiled=True, axis_index_groups=Z_LINES)  6.95 us
    ppermute x1, starting transfers between devices, gather_right(): after = lax.ppermute(own, 'grp', shift_x(-1))  3.46 us
  transfers between devices with their start and end apart: 10, of which 4 were waited for; matrix products, arithmetic and copies ran while one was open for 2% of the time, Pallas kernels for 0%

profile of v1, /device:TPU:6, one launch (start us, length us, event | category | flops | bytes accessed | tf_op | source)
XLA Modules:
  0.0 119.2 jit_solution(5806909116886095162)
XLA Ops:
  6.5 0.0 all-gather.2.cloned.1.call-start
  6.5 0.7 convert_bitcast_fusion
  7.2 0.1 fusion.8
  7.3 0.8 pad_maximum_fusion
  8.1 0.0 copy-start.8
  8.1 0.0 copy-start.7
  8.1 0.1 broadcast_in_dim.2
  8.2 25.3 %all_to_all.5 = bf16[8,272,128]{2,1,0:T(8,128)(2,1)} all-to-all(bf16[8,272,128]{2,1,0:T(8,128)(2,1)S(1)} %broadcast_in_dim.2), channel_id=1, replica_groups={{0,1,2,3,4,5,6,7},{8,9,10,11,12,13,14,15},{16,17,18,19,20,21,22,23},{24..., dimensions={0} | all-to-all | bytes 1114112 | tf_op jit(solution)/shard_map/all_to_all | solution.py:144
  33.6 0.0 all-gather.2.cloned.1.call-update
  33.6 0.0 copy-done.8
  33.6 0.1 copy.13
  33.7 0.1 reshape.55
  33.8 0.0 copy-done.7
  33.8 0.1 fusion.1.refs_0_
  33.9 2.4 %collective-permute-start.2 = (bf16[4112,128]{1,0:T(8,128)(2,1)S(1)}, bf16[4112,128]{1,0:T(8,128)(2,1)S(1)}, u32[]{:S(2)}, u32[]{:S(2)}) collective-permute-start(bf16[4112,128]{1,0:T(8,128)(2,1)S(1)} %fusion.1.refs_0_), channel_id=1, source_target_pairs={{0,128},{64,192},{128,256},{192,320},{256,384},{320,448},{384,0},{... | collective-permute-start | bytes 3158024 | tf_op jit(solution)/shard_map/ppermute | solution.py:135
  36.3 3.5 %collective-permute-start = (bf16[4112,128]{1,0:T(8,128)(2,1)S(1)}, bf16[4112,128]{1,0:T(8,128)(2,1)S(1)}, u32[]{:S(2)}, u32[]{:S(2)}) collective-permute-start(bf16[4112,128]{1,0:T(8,128)(2,1)S(1)} %fusion.1.refs_0_), channel_id=1, source_target_pairs={{0,384},{64,448},{128,0},{192,64},{256,128},{320,192},{384,256},{4... | collective-permute-start | bytes 3158024 | tf_op jit(solution)/shard_map/ppermute | solution.py:134
  39.7 1.9 %collective-permute-start.3 = (bf16[4112,128]{1,0:T(8,128)(2,1)S(1)}, bf16[4112,128]{1,0:T(8,128)(2,1)}, u32[]{:S(2)}, u32[]{:S(2)}) collective-permute-start(bf16[4112,128]{1,0:T(8,128)(2,1)S(1)} %fusion.1.refs_0_), channel_id=1, source_target_pairs={{0,64},{64,0},{128,192},{192,128},{256,320},{320,256},{384,448},{4... | collective-permute-start | bytes 3158024 | tf_op jit(solution)/shard_map/ppermute | solution.py:139
  41.7 17.1 %collective-permute-done.2.refs_4_ = bf16[4112,128]{1,0:T(8,128)(2,1)S(1)} collective-permute-done((bf16[4112,128]{1,0:T(8,128)(2,1)S(1)}, bf16[4112,128]{1,0:T(8,128)(2,1)S(1)}, u32[]{:S(2)}, u32[]{:S(2)}) %collective-permute-start.2) | collective-permute-done | bytes 1052704 | tf_op jit(solution)/shard_map/ppermute | solution.py:135
  58.7 1.9 %collective-permute-start.6 = (bf16[4112,128]{1,0:T(8,128)(2,1)S(1)}, bf16[4112,128]{1,0:T(8,128)(2,1)}, u32[]{:S(2)}, u32[]{:S(2)}) collective-permute-start(bf16[4112,128]{1,0:T(8,128)(2,1)S(1)} %collective-permute-done.2.refs_4_), channel_id=1, source_target_pairs={{0,64},{64,0},{128,192},{192,128},{256,320},{320,256},{384,448},{4... | collective-permute-start | bytes 3158024 | tf_op jit(solution)/shard_map/ppermute | solution.py:139
  60.7 0.1 squeeze.25
  60.8 3.4 %collective-permute-start.7 = (bf16[2048,128]{1,0:T(8,128)(2,1)S(1)}, bf16[2048,128]{1,0:T(8,128)(2,1)}, u32[]{:S(2)}, u32[]{:S(2)}) collective-permute-start(bf16[2048,128]{1,0:T(8,128)(2,1)S(1)} %slice.50), channel_id=1, source_target_pairs={{0,128},{64,192},{128,256},{192,320},{256,384},{320,448},{384,0},{... | collective-permute-start | bytes 1572872 | tf_op jit(solution)/shard_map/ppermute | solution.py:136
  64.2 0.0 collective-permute-done.refs_1_
  64.3 2.4 %collective-permute-start.1 = (bf16[2064,128]{1,0:T(8,128)(2,1)S(1)}, bf16[2064,128]{1,0:T(8,128)(2,1)S(1)}, u32[]{:S(2)}, u32[]{:S(2)}) collective-permute-start(bf16[2064,128]{1,0:T(8,128)(2,1)S(1)} %slice.42), channel_id=1, source_target_pairs={{0,384},{64,448},{128,0},{192,64},{256,128},{320,192},{384,256},{4... | collective-permute-start | bytes 1585160 | tf_op jit(solution)/shard_map/ppermute | solution.py:137
  66.7 1.9 %collective-permute-start.4 = (bf16[4112,128]{1,0:T(8,128)(2,1)S(1)}, bf16[4112,128]{1,0:T(8,128)(2,1)S(1)}, u32[]{:S(2)}, u32[]{:S(2)}) collective-permute-start(bf16[4112,128]{1,0:T(8,128)(2,1)S(1)} %collective-permute-done.refs_1_), channel_id=1, source_target_pairs={{0,64},{64,0},{128,192},{192,128},{256,320},{320,256},{384,448},{4... | collective-permute-start | bytes 3158024 | tf_op jit(solution)/shard_map/ppermute | solution.py:139
  68.7 0.0 collective-permute-done.3.refs_5_
  68.7 0.7 slice_bitcast_fusion.3
  69.3 7.8 %collective-permute-done.7.refs_2_ = bf16[2048,128]{1,0:T(8,128)(2,1)} collective-permute-done((bf16[2048,128]{1,0:T(8,128)(2,1)S(1)}, bf16[2048,128]{1,0:T(8,128)(2,1)}, u32[]{:S(2)}, u32[]{:S(2)}) %collective-permute-start.7) | collective-permute-done | bytes 524320 | tf_op jit(solution)/shard_map/ppermute | solution.py:136
  77.1 1.9 %collective-permute-start.8 = (bf16[2048,128]{1,0:T(8,128)(2,1)}, bf16[2048,128]{1,0:T(8,128)(2,1)}, u32[]{:S(2)}, u32[]{:S(2)}) collective-permute-start(bf16[2048,128]{1,0:T(8,128)(2,1)} %collective-permute-done.7.refs_2_), channel_id=1, source_target_pairs={{0,64},{64,0},{128,192},{192,128},{256,320},{320,256},{384,448},{4... | collective-permute-start | bytes 1572872 | tf_op jit(solution)/shard_map/ppermute | solution.py:139
  79.0 2.5 %collective-permute-done.1.refs_3_ = bf16[2064,128]{1,0:T(8,128)(2,1)S(1)} collective-permute-done((bf16[2064,128]{1,0:T(8,128)(2,1)S(1)}, bf16[2064,128]{1,0:T(8,128)(2,1)S(1)}, u32[]{:S(2)}, u32[]{:S(2)}) %collective-permute-start.1) | collective-permute-done | bytes 528416 | tf_op jit(solution)/shard_map/ppermute | solution.py:137
  81.5 1.9 %collective-permute-start.5 = (bf16[2064,128]{1,0:T(8,128)(2,1)S(1)}, bf16[2064,128]{1,0:T(8,128)(2,1)S(1)}, u32[]{:S(2)}, u32[]{:S(2)}) collective-permute-start(bf16[2064,128]{1,0:T(8,128)(2,1)S(1)} %collective-permute-done.1.refs_3_), channel_id=1, source_target_pairs={{0,64},{64,0},{128,192},{192,128},{256,320},{320,256},{384,448},{4... | collective-permute-start | bytes 1585160 | tf_op jit(solution)/shard_map/ppermute | solution.py:139
  83.4 0.0 copy-start.3
  83.4 0.8 copy-done.3
  84.2 0.0 collective-permute-done.6.refs_9_
  84.2 0.7 slice_bitcast_fusion
  84.9 0.0 collective-permute-done.4.refs_6_
  84.9 0.0 copy-start.1
  84.9 1.0 copy-done.1
  85.9 0.0 collective-permute-done.5.refs_8_
  85.9 0.0 copy-start.5
  85.9 0.8 copy-done.5
  86.7 0.1 concatenate.25
  86.8 6.9 %all-gather.2.cloned.1.call-done = bf16[64,272,128]{2,1,0:T(8,128)(2,1)} async-done(((bf16[8,272,128]{2,1,0:T(8,128)(2,1)}), bf16[64,272,128]{2,1,0:T(8,128)(2,1)}) %all-gather.2.cloned.1.call-update) | async-done | bytes 4456464 | tf_op jit(solution)/shard_map/all_gather | solution.py:145
  93.8 1.0 fusion.2
  94.8 0.1 reshape.58.ids
  94.9 0.0 collective-permute-done.8.refs_7_
  94.9 0.0 copy-start
  94.9 2.3 %copy-done = bf16[64,272,128]{2,1,0:T(8,128)(2,1)S(1)} copy-done((bf16[64,272,128]{2,1,0:T(8,128)(2,1)S(1)}, bf16[64,272,128]{2,1,0:T(8,128)(2,1)}, u32[]{:S(2)}) %copy-start) | copy-done | bytes 4456472
  97.2 0.0 copy-start.2
  97.2 1.2 %copy-done.2 = bf16[4112,128]{1,0:T(8,128)(2,1)S(1)} copy-done((bf16[4112,128]{1,0:T(8,128)(2,1)S(1)}, bf16[4112,128]{1,0:T(8,128)(2,1)}, u32[]{:S(2)}) %copy-start.2) | copy-done | bytes 1052696
  98.4 0.0 copy-start.4
  98.4 1.0 copy-done.4
  99.4 0.0 copy-start.6
  99.4 1.0 copy-done.6
  100.5 11.9 %shard_map.55 = bf16[1024,1024]{1,0:T(8,128)(2,1)} custom-call(s32[1]{0:T(128)} %bitcast.place, s32[256]{0:T(256)S(1)} %convert_element_type.26.columns, s32[256]{0:T(256)S(1)} %reshape.58.ids, bf16[17408,128]{1,0:T(8,128)(2,1)S(1)} %bitcast.22, bf16[4112,128]{1,0:T(8,128)(2,1)S(1)} %fusion.1.refs_0_, bf16[4112,128]{1,0:T(8,128)(2,1)S(1)} %collective-permute-done.refs_1_, ...), custom_call_target="tpu_custom_call" | custom-call | flops 4294967296 | bytes 14680064 | tf_op jit(solution)/shard_map/pallas_call | solution.py:109
  (9 shorter events, 0.1 us)
Async XLA Ops:
  6.5 87.2 %all-gather.2.cloned.1.call-start = ((), (), s32[]{:S(2)}) async-start(), calls=%async_computation.1 | async-start | bytes 5013504 | tf_op jit(solution)/shard_map/all_gather | solution.py:145
  8.1 25.4 %copy-start.8 = (s32[8,4]{0,1:T(4,128)S(1)}, s32[8,4]{0,1:T(4,128)}, u32[]{:S(2)}) copy-start(s32[8,4]{0,1:T(4,128)} %param.9) | copy-start | bytes 388
  8.1 25.7 %copy-start.7 = (bf16[8,4,128,128]{3,2,1,0:T(8,128)(2,1)S(1)}, bf16[8,4,128,128]{3,2,1,0:T(8,128)(2,1)}, u32[]{:S(2)}) copy-start(bf16[8,4,128,128]{3,2,1,0:T(8,128)(2,1)} %param.8) | copy-start | bytes 3145732
  33.9 24.9 %collective-permute-start.2 = (bf16[4112,128]{1,0:T(8,128)(2,1)S(1)}, bf16[4112,128]{1,0:T(8,128)(2,1)S(1)}, u32[]{:S(2)}, u32[]{:S(2)}) collective-permute-start(bf16[4112,128]{1,0:T(8,128)(2,1)S(1)} %fusion.1.refs_0_), channel_id=1, source_target_pairs={{0,128},{64,192},{128,256},{192,320},{256,384},{320,448},{384,0},{... | collective-permute-start | bytes 3158024 | tf_op jit(solution)/shard_map/ppermute | solution.py:135
  36.3 27.9 %collective-permute-start = (bf16[4112,128]{1,0:T(8,128)(2,1)S(1)}, bf16[4112,128]{1,0:T(8,128)(2,1)S(1)}, u32[]{:S(2)}, u32[]{:S(2)}) collective-permute-start(bf16[4112,128]{1,0:T(8,128)(2,1)S(1)} %fusion.1.refs_0_), channel_id=1, source_target_pairs={{0,384},{64,448},{128,0},{192,64},{256,128},{320,192},{384,256},{4... | collective-permute-start | bytes 3158024 | tf_op jit(solution)/shard_map/ppermute | solution.py:134
  39.7 28.9 %collective-permute-start.3 = (bf16[4112,128]{1,0:T(8,128)(2,1)S(1)}, bf16[4112,128]{1,0:T(8,128)(2,1)}, u32[]{:S(2)}, u32[]{:S(2)}) collective-permute-start(bf16[4112,128]{1,0:T(8,128)(2,1)S(1)} %fusion.1.refs_0_), channel_id=1, source_target_pairs={{0,64},{64,0},{128,192},{192,128},{256,320},{320,256},{384,448},{4... | collective-permute-start | bytes 3158024 | tf_op jit(solution)/shard_map/ppermute | solution.py:139
  58.7 25.5 %collective-permute-start.6 = (bf16[4112,128]{1,0:T(8,128)(2,1)S(1)}, bf16[4112,128]{1,0:T(8,128)(2,1)}, u32[]{:S(2)}, u32[]{:S(2)}) collective-permute-start(bf16[4112,128]{1,0:T(8,128)(2,1)S(1)} %collective-permute-done.2.refs_4_), channel_id=1, source_target_pairs={{0,64},{64,0},{128,192},{192,128},{256,320},{320,256},{384,448},{4... | collective-permute-start | bytes 3158024 | tf_op jit(solution)/shard_map/ppermute | solution.py:139
  60.8 16.3 %collective-permute-start.7 = (bf16[2048,128]{1,0:T(8,128)(2,1)S(1)}, bf16[2048,128]{1,0:T(8,128)(2,1)}, u32[]{:S(2)}, u32[]{:S(2)}) collective-permute-start(bf16[2048,128]{1,0:T(8,128)(2,1)S(1)} %slice.50), channel_id=1, source_target_pairs={{0,128},{64,192},{128,256},{192,320},{256,384},{320,448},{384,0},{... | collective-permute-start | bytes 1572872 | tf_op jit(solution)/shard_map/ppermute | solution.py:136
  64.3 17.2 %collective-permute-start.1 = (bf16[2064,128]{1,0:T(8,128)(2,1)S(1)}, bf16[2064,128]{1,0:T(8,128)(2,1)S(1)}, u32[]{:S(2)}, u32[]{:S(2)}) collective-permute-start(bf16[2064,128]{1,0:T(8,128)(2,1)S(1)} %slice.42), channel_id=1, source_target_pairs={{0,384},{64,448},{128,0},{192,64},{256,128},{320,192},{384,256},{4... | collective-permute-start | bytes 1585160 | tf_op jit(solution)/shard_map/ppermute | solution.py:137
  66.7 18.2 %collective-permute-start.4 = (bf16[4112,128]{1,0:T(8,128)(2,1)S(1)}, bf16[4112,128]{1,0:T(8,128)(2,1)S(1)}, u32[]{:S(2)}, u32[]{:S(2)}) collective-permute-start(bf16[4112,128]{1,0:T(8,128)(2,1)S(1)} %collective-permute-done.refs_1_), channel_id=1, source_target_pairs={{0,64},{64,0},{128,192},{192,128},{256,320},{320,256},{384,448},{4... | collective-permute-start | bytes 3158024 | tf_op jit(solution)/shard_map/ppermute | solution.py:139
  77.1 17.8 %collective-permute-start.8 = (bf16[2048,128]{1,0:T(8,128)(2,1)}, bf16[2048,128]{1,0:T(8,128)(2,1)}, u32[]{:S(2)}, u32[]{:S(2)}) collective-permute-start(bf16[2048,128]{1,0:T(8,128)(2,1)} %collective-permute-done.7.refs_2_), channel_id=1, source_target_pairs={{0,64},{64,0},{128,192},{192,128},{256,320},{320,256},{384,448},{4... | collective-permute-start | bytes 1572872 | tf_op jit(solution)/shard_map/ppermute | solution.py:139
  81.5 4.4 %collective-permute-start.5 = (bf16[2064,128]{1,0:T(8,128)(2,1)S(1)}, bf16[2064,128]{1,0:T(8,128)(2,1)S(1)}, u32[]{:S(2)}, u32[]{:S(2)}) collective-permute-start(bf16[2064,128]{1,0:T(8,128)(2,1)S(1)} %collective-permute-done.1.refs_3_), channel_id=1, source_target_pairs={{0,64},{64,0},{128,192},{192,128},{256,320},{320,256},{384,448},{4... | collective-permute-start | bytes 1585160 | tf_op jit(solution)/shard_map/ppermute | solution.py:139
  83.4 0.8 copy-start.3
  84.9 1.0 copy-start.1
  85.9 0.9 copy-start.5
  94.9 2.3 %copy-start = (bf16[64,272,128]{2,1,0:T(8,128)(2,1)S(1)}, bf16[64,272,128]{2,1,0:T(8,128)(2,1)}, u32[]{:S(2)}) copy-start(bf16[64,272,128]{2,1,0:T(8,128)(2,1)} %all-gather.2.cloned.1.call-done) | copy-start | bytes 13369348
  97.2 1.2 %copy-start.2 = (bf16[4112,128]{1,0:T(8,128)(2,1)S(1)}, bf16[4112,128]{1,0:T(8,128)(2,1)}, u32[]{:S(2)}) copy-start(bf16[4112,128]{1,0:T(8,128)(2,1)} %copy-done.1) | copy-start | bytes 3158020
  98.4 1.0 copy-start.4
  99.4 1.0 copy-start.6
Sparse Core Ops, SparseCore 0:
  33.7 60.0 all-gather.1

commit v2 on v1

v2 whole, which is shorter than its diff:
```python
import jax
import jax.numpy as jnp
from jax import lax
from jax.experimental import pallas as pl
from jax.experimental.pallas import tpu as pltpu
from jax.sharding import PartitionSpec as P

BS = 128
RG = 8
KS = 64
JB = 8
NBR = 4
PER_ROW = 16
N_X = 4
N_Y = 8
N_Z = 8
PAD = 16
OWN_K = 8
R_ROWS = OWN_K * NBR * BS
L_ROWS = 2 * BS
N_LEFT = 128
N_RIGHT = KS * NBR


def shift_x(step):
    return [(x * 2 + c, ((x + step) % N_X) * 2 + c) for x in range(N_X) for c in range(2)]


SWAP_CORES = [(g, g ^ 1) for g in range(2 * N_X)]
Y_LINES = [[z * N_Y + y for y in range(N_Y)] for z in range(N_Z)]
Z_LINES = [[z * N_Y + y for z in range(N_Z)] for y in range(N_Y)]


def arrange_kernel(place, columns, ids, *refs):
    pieces, (right, order, found, table, filled, sem) = refs[:10], refs[10:]
    copies = []
    slot = 0
    for i, piece in enumerate(pieces):
        blocks = piece.shape[0] // BS
        copies.append(
            pltpu.make_async_copy(
                piece.at[pl.ds(0, blocks * BS)], right.at[pl.ds(slot * BS, blocks * BS)], sem.at[i]
            )
        )
        slot += blocks
    for copy in copies:
        copy.start()
    right[pl.ds(N_RIGHT * BS, BS), :] = jnp.zeros((BS, BS), jnp.bfloat16)
    own_x, own_core = place[0] // 2, place[0] % 2

    def clear(i, carry):
        table[i] = N_RIGHT * BS
        return carry

    lax.fori_loop(0, KS * JB, clear, 0, unroll=16)

    def fill(k, carry):
        g = k // OWN_K
        s = ((g + own_core) % 2) * N_X + (g // 2 + N_X - own_x) % N_X
        first = (s * OWN_K + k % OWN_K) * NBR
        for m in range(NBR):
            table[k * JB + columns[first + m]] = (first + m) * BS
        return carry

    lax.fori_loop(0, KS, fill, 0, unroll=2)
    for r in range(RG):
        filled[r] = 0

    def list_row(i, carry):
        device, b = i // 2, i % 2
        r = ids[device * 4 + b]
        k = ids[device * 4 + 2 + b]
        n = filled[r]
        p = r * PER_ROW + n
        order[p] = i * BS
        for j in range(JB):
            found[p * JB + j] = table[k * JB + j]
        filled[r] = n + 1
        return carry

    lax.fori_loop(0, N_LEFT, list_row, 0, unroll=2)
    for copy in copies:
        copy.wait()


def arrange(place, columns, ids, pieces):
    smem = pl.BlockSpec(memory_space=pltpu.SMEM)
    return pl.pallas_call(
        arrange_kernel,
        out_shape=(
            pltpu.VMEM(((N_RIGHT + 1) * BS, BS), jnp.bfloat16),
            jax.ShapeDtypeStruct((N_LEFT,), jnp.int32),
            jax.ShapeDtypeStruct((N_LEFT * JB,), jnp.int32),
        ),
        in_specs=[smem] * 3 + [pl.BlockSpec(memory_space=pl.ANY)] * len(pieces),
        out_specs=(pl.BlockSpec(memory_space=pltpu.VMEM), smem, smem),
        scratch_shapes=[
            pltpu.SMEM((KS * JB,), jnp.int32),
            pltpu.SMEM((RG,), jnp.int32),
            pltpu.SemaphoreType.DMA((len(pieces),)),
        ],
        compiler_params=pltpu.CompilerParams(vmem_limit_bytes=8 * 2**20),
        cost_estimate=pl.CostEstimate(flops=0, bytes_accessed=16 * 2**20, transcendentals=0),
    )(place, columns, ids, *pieces)


def multiply_kernel(order, found, right, left, out, left_buf, sem):
    row = pl.program_id(0)

    def fetch(r, start):
        for p in range(PER_ROW):
            copy = pltpu.make_async_copy(
                left.at[pl.ds(pl.multiple_of(order[r * PER_ROW + p], BS), BS)],
                left_buf.at[r, :, pl.ds(p * BS, BS)],
                sem.at[r],
            )
            copy.start() if start else copy.wait()

    @pl.when(row == 0)
    def first():
        for r in range(2):
            fetch(r, True)

    @pl.when(row + 2 < RG)
    def later():
        fetch(row + 2, True)

    fetch(row, False)
    lhs = left_buf[row]
    for j in range(0, JB, 2):
        rhs = jnp.concatenate(
            [
                jnp.concatenate(
                    [
                        right[pl.ds(pl.multiple_of(found[(row * PER_ROW + p) * JB + j + h], BS), BS), :]
                        for h in range(2)
                    ],
                    axis=1,
                )
                for p in range(PER_ROW)
            ],
            axis=0,
        )
        out[:, j * BS : (j + 2) * BS] = jnp.dot(lhs, rhs, preferred_element_type=jnp.float32).astype(out.dtype)


def multiply(order, found, right, left):
    smem = pl.BlockSpec(memory_space=pltpu.SMEM)
    return pl.pallas_call(
        multiply_kernel,
        grid=(RG,),
        out_shape=jax.ShapeDtypeStruct((RG * BS, JB * BS), jnp.bfloat16),
        in_specs=[smem, smem, pl.BlockSpec(memory_space=pltpu.VMEM), pl.BlockSpec(memory_space=pl.ANY)],
        out_specs=pl.BlockSpec((BS, JB * BS), lambda r: (r, 0)),
        scratch_shapes=[
            pltpu.VMEM((RG, BS, PER_ROW * BS), jnp.bfloat16),
            pltpu.SemaphoreType.DMA((RG,)),
        ],
        compiler_params=pltpu.CompilerParams(vmem_limit_bytes=16 * 2**20),
        cost_estimate=pl.CostEstimate(flops=4 * 2**30, bytes_accessed=14 * 2**20, transcendentals=0),
    )(order, found, pltpu.with_memory_space_constraint(right, pltpu.VMEM), left)


def tail(values):
    flat = values.astype(jnp.bfloat16).reshape(1, -1)
    return jnp.pad(flat, ((0, PAD - 1), (0, BS - flat.shape[1])))


def gather_right(own):
    after = lax.ppermute(own, "grp", shift_x(-1))
    before = lax.ppermute(own, "grp", shift_x(1))
    far_head = lax.ppermute(before[: R_ROWS // 2], "grp", shift_x(1))
    far_tail = lax.ppermute(after[R_ROWS // 2 :], "grp", shift_x(-1))
    mine = [own, after, far_head, far_tail, before]
    return mine + [lax.ppermute(v, "grp", SWAP_CORES) for v in mine]


def body(panel_blocks, panel_rows, panel_inner, right_blocks, right_columns):
    right = jnp.concatenate([right_blocks.reshape(R_ROWS, BS), tail(right_columns)])
    left = jnp.concatenate(
        [panel_blocks.reshape(L_ROWS, BS), tail(jnp.concatenate([panel_rows, panel_inner]))]
    )
    copies = jnp.broadcast_to(left[None], (N_Y,) + left.shape)
    line = lax.all_to_all(copies, "col", 0, 0, axis_index_groups=Y_LINES)
    lefts = lax.all_gather(line[:, :L_ROWS], "col", axis=0, tiled=True, axis_index_groups=Z_LINES)
    line_ids = tail(line[:, L_ROWS, :4])
    ids = lax.all_to_all(
        jnp.broadcast_to(line_ids[None], (N_Z,) + line_ids.shape), "col", 0, 0, axis_index_groups=Z_LINES
    )
    ids = ids[:, 0, : 4 * N_Y].astype(jnp.int32).reshape(-1)
    pieces = gather_right(right)
    columns = jnp.concatenate(
        [v[-PAD, : OWN_K * NBR] for v in pieces if v.shape[0] % BS == PAD]
    ).astype(jnp.int32)
    place = lax.axis_index("grp").reshape(1)
    rights, order, found = arrange(place, columns, ids, pieces)
    return multiply(order, found, rights, lefts.reshape(-1, BS))


def solution(mesh):
    placed = (
        P(("grp", "col"), None, None),
        P(("grp", "col")),
        P(("grp", "col")),
        P("grp", "col", None, None),
        P("grp", "col"),
    )
    return jax.shard_map(
        body, mesh=mesh, in_specs=placed, out_specs=P("grp", "col"), check_vma=False
    )
```

time: 121 us -> 129 us (1.066)
  the two profiles are of different devices: /device:TPU:6 before, /device:TPU:1 now
where the time goes in v2:
time: 129 us; the launch traced here: 128 us
  starting transfers between devices  43.5 us (34%)
  blocking collectives  22.8 us (18%)
  local copies, waits for them, and re-layouts  20.1 us (16%)
  Pallas kernels  15.4 us (12%)
  between operations  13.6 us (11%)
  waiting for transfers between devices  10.7 us (8%)
  other arithmetic  1.7 us (1%)
    all_to_all x1, blocking collectives, body(): line = lax.all_to_all(copies, 'col', 0, 0, axis_index_groups=Y_LINES)  22.8 us
    ppermute x5, starting transfers between devices, gather_right(): return mine + [lax.ppermute(v, 'grp', SWAP_CORES) for v in mine]  20.7 us
    unnamed x24, local copies, waits for them, and re-layouts  15.8 us
    all_to_all x1, starting transfers between devices, body(): lax.all_to_all(jnp.broadcast_to(line_ids[None], (N_Z,) + line_ids.shape),...  10 us
    ppermute x1, waiting for transfers between devices, gather_right(): far_head = lax.ppermute(before[:R_ROWS // 2], 'grp', shift_x(1))  8.93 us
    pallas_call x1, Pallas kernels, multiply(): pl.pallas_call(multiply_kernel, grid=(RG,), out_shape=jax.ShapeDtypeStruc...  8.84 us
    pallas_call x1, Pallas kernels, arrange(): pl.pallas_call(arrange_kernel, out_shape=(pltpu.VMEM(((N_RIGHT + 1) * BS,...  6.59 us
    ppermute x1, starting transfers between devices, gather_right(): before = lax.ppermute(own, 'grp', shift_x(1))  4.27 us
  transfers between devices with their start and end apart: 11, of which 2 were waited for; matrix products, arithmetic and copies ran while one was open for 3% of the time, Pallas kernels for 5%

profile of v2, /device:TPU:1, one launch (start us, length us, event | category | flops | bytes accessed | tf_op | source)
XLA Modules:
  0.0 127.8 jit_solution(6065803913108654204)
XLA Ops:
  6.5 0.0 all-gather.2.cloned.1.call-start
  6.5 0.7 convert_bitcast_fusion
  7.2 0.1 fusion.7
  7.3 0.8 pad_maximum_fusion
  8.1 0.1 broadcast_in_dim.4
  8.2 22.8 %all_to_all.10 = bf16[8,272,128]{2,1,0:T(8,128)(2,1)S(1)} all-to-all(bf16[8,272,128]{2,1,0:T(8,128)(2,1)S(1)} %broadcast_in_dim.4), channel_id=1, replica_groups={{0,1,2,3,4,5,6,7},{8,9,10,11,12,13,14,15},{16,17,18,19,20,21,22,23},{24..., dimensions={0} | all-to-all | bytes 1114112 | tf_op jit(solution)/shard_map/all_to_all | solution.py:184
  31.0 0.0 copy-start.9
  31.0 0.8 copy-done.9
  31.8 0.0 copy-start.11
  31.8 0.0 copy-start.10
  31.8 0.9 slice.60
  32.7 0.0 all-gather.2.cloned.1.call-update
  32.7 0.0 copy-done.11
  32.7 0.1 copy.14
  32.8 0.1 reshape.56
  32.9 0.3 copy-done.10
  33.2 0.1 fusion.1.refs_0_
  33.3 4.3 %collective-permute-start.2 = (bf16[4112,128]{1,0:T(8,128)(2,1)S(1)}, bf16[4112,128]{1,0:T(8,128)(2,1)S(1)}, u32[]{:S(2)}, u32[]{:S(2)}) collective-permute-start(bf16[4112,128]{1,0:T(8,128)(2,1)S(1)} %fusion.1.refs_0_), channel_id=1, source_target_pairs={{0,128},{64,192},{128,256},{192,320},{256,384},{320,448},{384,0},{... | collective-permute-start | bytes 3158024 | tf_op jit(solution)/shard_map/ppermute | solution.py:171
  37.6 3.2 %collective-permute-start = (bf16[4112,128]{1,0:T(8,128)(2,1)S(1)}, bf16[4112,128]{1,0:T(8,128)(2,1)S(1)}, u32[]{:S(2)}, u32[]{:S(2)}) collective-permute-start(bf16[4112,128]{1,0:T(8,128)(2,1)S(1)} %fusion.1.refs_0_), channel_id=1, source_target_pairs={{0,384},{64,448},{128,0},{192,64},{256,128},{320,192},{384,256},{4... | collective-permute-start | bytes 3158024 | tf_op jit(solution)/shard_map/ppermute | solution.py:170
  40.8 5.3 %collective-permute-start.3 = (bf16[4112,128]{1,0:T(8,128)(2,1)S(1)}, bf16[4112,128]{1,0:T(8,128)(2,1)}, u32[]{:S(2)}, u32[]{:S(2)}) collective-permute-start(bf16[4112,128]{1,0:T(8,128)(2,1)S(1)} %fusion.1.refs_0_), channel_id=1, source_target_pairs={{0,64},{64,0},{128,192},{192,128},{256,320},{320,256},{384,448},{4... | collective-permute-start | bytes 3158024 | tf_op jit(solution)/shard_map/ppermute | solution.py:175
  46.1 0.7 slice_reduce_fusion
  46.8 0.1 reshape_squeeze.3
  46.9 0.6 broadcast_in_dim.5
  47.6 10.0 %all-to-all-start.1 = ((bf16[8,16,128]{2,1,0:T(8,128)(2,1)}), bf16[8,16,128]{2,1,0:T(8,128)(2,1)S(1)}, u32[]{:S(2)}, u32[]{:S(2)}) async-start(bf16[8,16,128]{2,1,0:T(8,128)(2,1)} %broadcast_in_dim.5), calls=%async_computation.1 | async-start | bytes 65536 | tf_op jit(solution)/shard_map/all_to_all | solution.py:187
  57.6 1.7 %collective-permute-done.2.refs_4_ = bf16[4112,128]{1,0:T(8,128)(2,1)S(1)} collective-permute-done((bf16[4112,128]{1,0:T(8,128)(2,1)S(1)}, bf16[4112,128]{1,0:T(8,128)(2,1)S(1)}, u32[]{:S(2)}, u32[]{:S(2)}) %collective-permute-start.2) | collective-permute-done | bytes 1052704 | tf_op jit(solution)/shard_map/ppermute | solution.py:171
  59.3 5.6 %collective-permute-start.6 = (bf16[4112,128]{1,0:T(8,128)(2,1)S(1)}, bf16[4112,128]{1,0:T(8,128)(2,1)}, u32[]{:S(2)}, u32[]{:S(2)}) collective-permute-start(bf16[4112,128]{1,0:T(8,128)(2,1)S(1)} %collective-permute-done.2.refs_4_), channel_id=1, source_target_pairs={{0,64},{64,0},{128,192},{192,128},{256,320},{320,256},{384,448},{4... | collective-permute-start | bytes 3158024 | tf_op jit(solution)/shard_map/ppermute | solution.py:175
  64.9 0.1 squeeze.25
  65.0 0.0 all-to-all-done.1
  65.0 0.1 reshape.59.ids
  65.1 0.0 collective-permute-done.refs_1_
  65.2 3.4 %collective-permute-start.1 = (bf16[2064,128]{1,0:T(8,128)(2,1)S(1)}, bf16[2064,128]{1,0:T(8,128)(2,1)S(1)}, u32[]{:S(2)}, u32[]{:S(2)}) collective-permute-start(bf16[2064,128]{1,0:T(8,128)(2,1)S(1)} %slice.50), channel_id=1, source_target_pairs={{0,384},{64,448},{128,0},{192,64},{256,128},{320,192},{384,256},{4... | collective-permute-start | bytes 1585160 | tf_op jit(solution)/shard_map/ppermute | solution.py:173
  68.6 1.9 %collective-permute-start.7 = (bf16[2048,128]{1,0:T(8,128)(2,1)S(1)}, bf16[2048,128]{1,0:T(8,128)(2,1)}, u32[]{:S(2)}, u32[]{:S(2)}) collective-permute-start(bf16[2048,128]{1,0:T(8,128)(2,1)S(1)} %slice.59), channel_id=1, source_target_pairs={{0,128},{64,192},{128,256},{192,320},{256,384},{320,448},{384,0},{... | collective-permute-start | bytes 1572872 | tf_op jit(solution)/shard_map/ppermute | solution.py:172
  70.5 3.7 %collective-permute-start.4 = (bf16[4112,128]{1,0:T(8,128)(2,1)S(1)}, bf16[4112,128]{1,0:T(8,128)(2,1)S(1)}, u32[]{:S(2)}, u32[]{:S(2)}) collective-permute-start(bf16[4112,128]{1,0:T(8,128)(2,1)S(1)} %collective-permute-done.refs_1_), channel_id=1, source_target_pairs={{0,64},{64,0},{128,192},{192,128},{256,320},{320,256},{384,448},{4... | collective-permute-start | bytes 3158024 | tf_op jit(solution)/shard_map/ppermute | solution.py:175
  74.2 0.0 collective-permute-done.3.refs_5_
  74.2 0.7 slice_bitcast_fusion.3
  74.9 8.9 %collective-permute-done.7.refs_2_ = bf16[2048,128]{1,0:T(8,128)(2,1)} collective-permute-done((bf16[2048,128]{1,0:T(8,128)(2,1)S(1)}, bf16[2048,128]{1,0:T(8,128)(2,1)}, u32[]{:S(2)}, u32[]{:S(2)}) %collective-permute-start.7) | collective-permute-done | bytes 524320 | tf_op jit(solution)/shard_map/ppermute | solution.py:172
  83.9 4.2 %collective-permute-start.8 = (bf16[2048,128]{1,0:T(8,128)(2,1)}, bf16[2048,128]{1,0:T(8,128)(2,1)}, u32[]{:S(2)}, u32[]{:S(2)}) collective-permute-start(bf16[2048,128]{1,0:T(8,128)(2,1)} %collective-permute-done.7.refs_2_), channel_id=1, source_target_pairs={{0,64},{64,0},{128,192},{192,128},{256,320},{320,256},{384,448},{4... | collective-permute-start | bytes 1572872 | tf_op jit(solution)/shard_map/ppermute | solution.py:175
  88.0 0.0 collective-permute-done.1.refs_3_
  88.0 1.9 %collective-permute-start.5 = (bf16[2064,128]{1,0:T(8,128)(2,1)S(1)}, bf16[2064,128]{1,0:T(8,128)(2,1)S(1)}, u32[]{:S(2)}, u32[]{:S(2)}) collective-permute-start(bf16[2064,128]{1,0:T(8,128)(2,1)S(1)} %collective-permute-done.1.refs_3_), channel_id=1, source_target_pairs={{0,64},{64,0},{128,192},{192,128},{256,320},{320,256},{384,448},{4... | collective-permute-start | bytes 1585160 | tf_op jit(solution)/shard_map/ppermute | solution.py:175
  90.0 0.0 copy-start.2
  90.0 0.8 copy-done.2
  90.8 0.0 collective-permute-done.6.refs_9_
  90.8 0.7 slice_bitcast_fusion
  91.5 0.0 collective-permute-done.4.refs_6_
  91.5 0.0 copy-start
  91.5 1.0 copy-done
  92.4 0.0 collective-permute-done.5.refs_8_
  92.4 0.0 copy-start.4
  92.4 0.8 copy-done.4
  93.2 0.1 concatenate.25
  93.3 0.0 collective-permute-done.8.refs_7_
  93.3 0.0 copy-start.1
  93.3 1.2 copy-done.1
  94.6 0.0 copy-start.3
  94.6 1.0 copy-done.3
  95.6 0.0 copy-start.5
  95.6 1.0 copy-done.5
  96.7 6.6 %shard_map.55 = (bf16[32896,128]{1,0:T(8,128)(2,1)S(1)}, s32[128]{0:T(128)S(1)}, s32[1024]{0:T(1024)S(1)}) custom-call(s32[1]{0:T(128)} %bitcast.place, s32[256]{0:T(256)S(1)} %convert_element_type.27.columns, s32[256]{0:T(256)S(1)} %reshape.59.ids, bf16[4112,128]{1,0:T(8,128)(2,1)S(1)} %fusion.1.refs_0_, ...), custom_call_target="tpu_custom_call" | custom-call | bytes 16777216 | tf_op jit(solution)/shard_map/pallas_call | solution.py:88
  103.3 0.0 copy-start.6
  103.3 3.2 %copy-done.6 = bf16[32896,128]{1,0:T(8,128)(2,1)} copy-done((bf16[32896,128]{1,0:T(8,128)(2,1)}, bf16[32896,128]{1,0:T(8,128)(2,1)S(1)}, u32[]{:S(2)}) %copy-start.6) | copy-done | bytes 8421400
  106.5 0.0 all-gather.2.cloned.1.call-done
  106.5 3.4 %copy-done.7 = bf16[32896,128]{1,0:T(8,128)(2,1)S(1)} copy-done((bf16[32896,128]{1,0:T(8,128)(2,1)S(1)}, bf16[32896,128]{1,0:T(8,128)(2,1)}, u32[]{:S(2)}) %copy-start.7) | copy-done | bytes 8421400
  109.9 2.2 %copy-done.8 = bf16[64,256,128]{2,1,0:T(8,128)(2,1)S(1)} copy-done((bf16[64,256,128]{2,1,0:T(8,128)(2,1)S(1)}, bf16[64,256,128]{2,1,0:T(8,128)(2,1)}, u32[]{:S(2)}) %copy-start.8) | copy-done | bytes 4194328
  112.1 8.8 %shard_map.56 = bf16[1024,1024]{1,0:T(8,128)(2,1)} custom-call(s32[128]{0:T(128)S(1)} %get-tuple-element.8.order, s32[1024]{0:T(1024)S(1)} %get-tuple-element.9.found, bf16[32896,128]{1,0:T(8,128)(2,1)S(1)} %copy-done.7, bf16[16384,128]{1,0:T(8,128)(2,1)S(1)} %bitcast.22), custom_call_target="tpu_custom_call" | custom-call | flops 4294967296 | bytes 14680064 | tf_op jit(solution)/shard_map/pallas_call | solution.py:149
  (13 shorter events, 0.1 us)
Async XLA Ops:
  6.5 100.0 %all-gather.2.cloned.1.call-start = ((), (), s32[]{:S(2)}) async-start(), calls=%async_computation.2 | async-start | bytes 4718592 | tf_op jit(solution)/shard_map/all_gather | solution.py:185
  31.0 0.8 copy-start.9
  31.8 0.9 copy-start.11
  31.8 1.4 %copy-start.10 = (bf16[8,4,128,128]{3,2,1,0:T(8,128)(2,1)S(1)}, bf16[8,4,128,128]{3,2,1,0:T(8,128)(2,1)}, u32[]{:S(2)}) copy-start(bf16[8,4,128,128]{3,2,1,0:T(8,128)(2,1)} %param.8) | copy-start | bytes 3145732
  33.3 26.0 %collective-permute-start.2 = (bf16[4112,128]{1,0:T(8,128)(2,1)S(1)}, bf16[4112,128]{1,0:T(8,128)(2,1)S(1)}, u32[]{:S(2)}, u32[]{:S(2)}) collective-permute-start(bf16[4112,128]{1,0:T(8,128)(2,1)S(1)} %fusion.1.refs_0_), channel_id=1, source_target_pairs={{0,128},{64,192},{128,256},{192,320},{256,384},{320,448},{384,0},{... | collective-permute-start | bytes 3158024 | tf_op jit(solution)/shard_map/ppermute | solution.py:171
  37.6 27.6 %collective-permute-start = (bf16[4112,128]{1,0:T(8,128)(2,1)S(1)}, bf16[4112,128]{1,0:T(8,128)(2,1)S(1)}, u32[]{:S(2)}, u32[]{:S(2)}) collective-permute-start(bf16[4112,128]{1,0:T(8,128)(2,1)S(1)} %fusion.1.refs_0_), channel_id=1, source_target_pairs={{0,384},{64,448},{128,0},{192,64},{256,128},{320,192},{384,256},{4... | collective-permute-start | bytes 3158024 | tf_op jit(solution)/shard_map/ppermute | solution.py:170
  40.8 33.5 %collective-permute-start.3 = (bf16[4112,128]{1,0:T(8,128)(2,1)S(1)}, bf16[4112,128]{1,0:T(8,128)(2,1)}, u32[]{:S(2)}, u32[]{:S(2)}) collective-permute-start(bf16[4112,128]{1,0:T(8,128)(2,1)S(1)} %fusion.1.refs_0_), channel_id=1, source_target_pairs={{0,64},{64,0},{128,192},{192,128},{256,320},{320,256},{384,448},{4... | collective-permute-start | bytes 3158024 | tf_op jit(solution)/shard_map/ppermute | solution.py:175
  47.6 17.4 %all-to-all-start.1 = ((bf16[8,16,128]{2,1,0:T(8,128)(2,1)}), bf16[8,16,128]{2,1,0:T(8,128)(2,1)S(1)}, u32[]{:S(2)}, u32[]{:S(2)}) async-start(bf16[8,16,128]{2,1,0:T(8,128)(2,1)} %broadcast_in_dim.5), calls=%async_computation.1 | async-start | bytes 65536 | tf_op jit(solution)/shard_map/all_to_all | solution.py:187
  59.3 31.5 %collective-permute-start.6 = (bf16[4112,128]{1,0:T(8,128)(2,1)S(1)}, bf16[4112,128]{1,0:T(8,128)(2,1)}, u32[]{:S(2)}, u32[]{:S(2)}) collective-permute-start(bf16[4112,128]{1,0:T(8,128)(2,1)S(1)} %collective-permute-done.2.refs_4_), channel_id=1, source_target_pairs={{0,64},{64,0},{128,192},{192,128},{256,320},{320,256},{384,448},{4... | collective-permute-start | bytes 3158024 | tf_op jit(solution)/shard_map/ppermute | solution.py:175
  65.2 22.9 %collective-permute-start.1 = (bf16[2064,128]{1,0:T(8,128)(2,1)S(1)}, bf16[2064,128]{1,0:T(8,128)(2,1)S(1)}, u32[]{:S(2)}, u32[]{:S(2)}) collective-permute-start(bf16[2064,128]{1,0:T(8,128)(2,1)S(1)} %slice.50), channel_id=1, source_target_pairs={{0,384},{64,448},{128,0},{192,64},{256,128},{320,192},{384,256},{4... | collective-permute-start | bytes 1585160 | tf_op jit(solution)/shard_map/ppermute | solution.py:173
  68.6 15.3 %collective-permute-start.7 = (bf16[2048,128]{1,0:T(8,128)(2,1)S(1)}, bf16[2048,128]{1,0:T(8,128)(2,1)}, u32[]{:S(2)}, u32[]{:S(2)}) collective-permute-start(bf16[2048,128]{1,0:T(8,128)(2,1)S(1)} %slice.59), channel_id=1, source_target_pairs={{0,128},{64,192},{128,256},{192,320},{256,384},{320,448},{384,0},{... | collective-permute-start | bytes 1572872 | tf_op jit(solution)/shard_map/ppermute | solution.py:172
  70.5 21.0 %collective-permute-start.4 = (bf16[4112,128]{1,0:T(8,128)(2,1)S(1)}, bf16[4112,128]{1,0:T(8,128)(2,1)S(1)}, u32[]{:S(2)}, u32[]{:S(2)}) collective-permute-start(bf16[4112,128]{1,0:T(8,128)(2,1)S(1)} %collective-permute-done.refs_1_), channel_id=1, source_target_pairs={{0,64},{64,0},{128,192},{192,128},{256,320},{320,256},{384,448},{4... | collective-permute-start | bytes 3158024 | tf_op jit(solution)/shard_map/ppermute | solution.py:175
  83.9 9.5 %collective-permute-start.8 = (bf16[2048,128]{1,0:T(8,128)(2,1)}, bf16[2048,128]{1,0:T(8,128)(2,1)}, u32[]{:S(2)}, u32[]{:S(2)}) collective-permute-start(bf16[2048,128]{1,0:T(8,128)(2,1)} %collective-permute-done.7.refs_2_), channel_id=1, source_target_pairs={{0,64},{64,0},{128,192},{192,128},{256,320},{320,256},{384,448},{4... | collective-permute-start | bytes 1572872 | tf_op jit(solution)/shard_map/ppermute | solution.py:175
  88.0 4.4 %collective-permute-start.5 = (bf16[2064,128]{1,0:T(8,128)(2,1)S(1)}, bf16[2064,128]{1,0:T(8,128)(2,1)S(1)}, u32[]{:S(2)}, u32[]{:S(2)}) collective-permute-start(bf16[2064,128]{1,0:T(8,128)(2,1)S(1)} %collective-permute-done.1.refs_3_), channel_id=1, source_target_pairs={{0,64},{64,0},{128,192},{192,128},{256,320},{320,256},{384,448},{4... | collective-permute-start | bytes 1585160 | tf_op jit(solution)/shard_map/ppermute | solution.py:175
  90.0 0.8 copy-start.2
  91.5 1.0 copy-start
  92.4 0.8 copy-start.4
  93.3 1.2 copy-start.1
  94.6 1.0 copy-start.3
  95.6 1.0 copy-start.5
  103.3 3.3 %copy-start.6 = (bf16[32896,128]{1,0:T(8,128)(2,1)}, bf16[32896,128]{1,0:T(8,128)(2,1)S(1)}, u32[]{:S(2)}) copy-start(bf16[32896,128]{1,0:T(8,128)(2,1)S(1)} %get-tuple-element.10.right) | copy-start | bytes 25264132
  106.5 3.4 %copy-start.7 = (bf16[32896,128]{1,0:T(8,128)(2,1)S(1)}, bf16[32896,128]{1,0:T(8,128)(2,1)}, u32[]{:S(2)}) copy-start(bf16[32896,128]{1,0:T(8,128)(2,1)} %copy-done.6) | copy-start | bytes 25264132
  109.9 2.2 %copy-start.8 = (bf16[64,256,128]{2,1,0:T(8,128)(2,1)S(1)}, bf16[64,256,128]{2,1,0:T(8,128)(2,1)}, u32[]{:S(2)}) copy-start(bf16[64,256,128]{2,1,0:T(8,128)(2,1)} %all-gather.2.cloned.1.call-done) | copy-start | bytes 12582916
Sparse Core Ops, SparseCore 0:
  32.8 61.5 all-gather.1

commit v3 on v0

v3 whole, which is shorter than its diff:
```python
import jax
import jax.numpy as jnp
from jax import lax
from jax.experimental import pallas as pl
from jax.experimental.pallas import tpu as pltpu
from jax.sharding import PartitionSpec as P

BS = 128
RG = 8
KS = 64
JB = 8
NBR = 4
PER_ROW = 16
N_GRP = 8
N_Y = 8
N_Z = 8
PAD = 16
OWN_K = 8
R_BLOCKS = OWN_K * NBR * BS
R_ROWS = R_BLOCKS + PAD + BS
ZERO = R_BLOCKS + PAD
L_BLOCKS = 2 * BS
L_ROWS = L_BLOCKS + PAD
MIB = 2**20
CHUNK = 4

Y_LINES = [[z * N_Y + y for y in range(N_Y)] for z in range(N_Z)]


def shift_z(step):
    return [(z * N_Y + y, ((z + step) % N_Z) * N_Y + y) for z in range(N_Z) for y in range(N_Y)]


def table_kernel(right, table, tiles, values, columns, sem):
    copies = [
        pltpu.make_async_copy(right.at[pl.ds(g * R_ROWS + R_BLOCKS, PAD)], tiles.at[g], sem.at[g])
        for g in range(N_GRP)
    ]
    for copy in copies:
        copy.start()

    def clear(i, carry):
        table[i] = ZERO
        return carry

    lax.fori_loop(0, (KS + 1) * JB, clear, 0, unroll=8)
    for copy in copies:
        copy.wait()
    values[...] = tiles[:, 0, :].astype(jnp.float32).astype(jnp.int32)
    copy = pltpu.make_async_copy(values, columns, sem.at[0])
    copy.start()
    copy.wait()

    def fill(k, carry):
        g, i = k // OWN_K, k % OWN_K
        for m in range(NBR):
            table[k * JB + columns[g, i * NBR + m]] = g * R_ROWS + (i * NBR + m) * BS
        return carry

    lax.fori_loop(0, KS, fill, 0, unroll=2)


def make_table(right):
    return pl.pallas_call(
        table_kernel,
        out_shape=jax.ShapeDtypeStruct(((KS + 1) * JB,), jnp.int32),
        in_specs=[pl.BlockSpec(memory_space=pl.ANY)],
        out_specs=pl.BlockSpec(memory_space=pltpu.SMEM),
        scratch_shapes=[
            pltpu.VMEM((N_GRP, PAD, BS), jnp.bfloat16),
            pltpu.VMEM((N_GRP, BS), jnp.int32),
            pltpu.SMEM((N_GRP, BS), jnp.int32),
            pltpu.SemaphoreType.DMA((N_GRP,)),
        ],
        compiler_params=pltpu.CompilerParams(vmem_limit_bytes=2 * MIB),
        cost_estimate=pl.CostEstimate(flops=0, bytes_accessed=MIB, transcendentals=0),
    )(pltpu.with_memory_space_constraint(right, pltpu.HBM))


def multiply_kernel(counts, later, last, table, right, *refs):
    n = len(counts)
    pieces, refs = refs[:n], refs[n:]
    if later:
        before, refs = refs[0], refs[1:]
    out, lhs, total, values, ids, inner, filled, sem = refs
    row = pl.program_id(0)
    firsts = [sum(counts[:i]) for i in range(n)]

    @pl.when(row == 0)
    def load():
        for i, piece in enumerate(pieces):
            tiles = piece[:, L_BLOCKS : L_BLOCKS + PAD, :]
            values[firsts[i] : firsts[i] + counts[i], :] = tiles[:, 0, :].astype(jnp.float32).astype(jnp.int32)
        copy = pltpu.make_async_copy(values, ids, sem.at[1])
        copy.start()
        for r in range(RG):
            filled[r] = 0
        copy.wait()
        for i, piece in enumerate(pieces):

            def place(d, carry, i=i, piece=piece):
                for b in range(2):
                    r = ids[firsts[i] + d, b]
                    p = filled[r]
                    filled[r] = p + 1
                    inner[r * PER_ROW + p] = ids[firsts[i] + d, 2 + b] * JB
                    pltpu.make_async_copy(
                        piece.at[d, pl.ds(b * BS, BS), :],
                        lhs.at[r, :, pl.ds(pl.multiple_of(p * BS, BS), BS)],
                        sem.at[0],
                    ).start()
                return carry

            lax.fori_loop(0, counts[i], place, 0, unroll=4)
        for r in range(RG):
            p = filled[r]

            def pad(q, carry, r=r):
                inner[r * PER_ROW + q] = KS * JB
                lhs[r, :, pl.ds(pl.multiple_of(q * BS, BS), BS)] = jnp.zeros((BS, BS), jnp.bfloat16)
                return carry

            lax.fori_loop(p, (p + CHUNK - 1) // CHUNK * CHUNK, pad, 0)
        whole = lhs.at[pl.ds(0, sum(counts) * 2 // PER_ROW)]
        pltpu.make_async_copy(whole, whole, sem.at[0]).wait()

    rows = pl.ds(pl.multiple_of(row * BS, BS), BS)
    if last:
        total[...] = before[rows, :]
        sums = total
    else:
        sums = out.at[rows, :]
        if not later:
            sums[...] = jnp.zeros(sums.shape, jnp.float32)

    def step(c, carry):
        a = lhs[row, :, pl.ds(pl.multiple_of(c * CHUNK * BS, CHUNK * BS), CHUNK * BS)]
        ks = [inner[row * PER_ROW + CHUNK * c + h] for h in range(CHUNK)]
        for j in range(0, JB, 2):
            b = jnp.concatenate(
                [
                    jnp.concatenate(
                        [right[pl.ds(pl.multiple_of(table[k + j + h], PAD), BS), :] for h in range(2)],
                        axis=1,
                    )
                    for k in ks
                ],
                axis=0,
            )
            sums[:, j * BS : (j + 2) * BS] += jnp.dot(a, b, preferred_element_type=jnp.float32)
        return carry

    lax.fori_loop(0, (filled[row] + CHUNK - 1) // CHUNK, step, 0)
    if last:
        out[...] = total[...].astype(out.dtype)


def multiply(table, right, pieces, before=None, last=False):
    later = before is not None
    counts = tuple(piece.shape[0] for piece in pieces)
    devices = sum(counts)
    vmem = pl.BlockSpec(memory_space=pltpu.VMEM)
    shape = (RG * BS, JB * BS)
    held = [right, *pieces] + [before] * later
    return pl.pallas_call(
        lambda *refs: multiply_kernel(counts, later, last, *refs),
        grid=(RG,),
        out_shape=jax.ShapeDtypeStruct(shape, jnp.bfloat16) if last else pltpu.VMEM(shape, jnp.float32),
        in_specs=[pl.BlockSpec(memory_space=pltpu.SMEM)] + [vmem] * len(held),
        out_specs=pl.BlockSpec((BS, JB * BS), lambda r: (r, 0)) if last else vmem,
        input_output_aliases={len(held): 0} if later and not last else {},
        scratch_shapes=[
            pltpu.VMEM((RG, BS, PER_ROW * BS), jnp.bfloat16),
            pltpu.VMEM((BS, JB * BS) if last else (8, BS), jnp.float32),
            pltpu.VMEM((devices, BS), jnp.int32),
            pltpu.SMEM((devices, BS), jnp.int32),
            pltpu.SMEM((RG * PER_ROW,), jnp.int32),
            pltpu.SMEM((RG,), jnp.int32),
            pltpu.SemaphoreType.DMA((2,)),
        ],
        compiler_params=pltpu.CompilerParams(vmem_limit_bytes=12 * MIB),
        cost_estimate=pl.CostEstimate(
            flops=devices * 2 * BS * BS * JB * BS * 2, bytes_accessed=4 * MIB, transcendentals=0
        ),
    )(table, *(pltpu.with_memory_space_constraint(v, pltpu.VMEM) for v in held))


def tail(values):
    flat = values.astype(jnp.bfloat16).reshape(1, -1)
    return jnp.pad(flat, ((0, PAD - 1), (0, BS - flat.shape[1])))


def body(panel_blocks, panel_rows, panel_inner, right_blocks, right_columns):
    right = jnp.concatenate(
        [right_blocks.reshape(R_BLOCKS, BS), tail(right_columns), jnp.zeros((BS, BS), jnp.bfloat16)]
    )
    left = jnp.concatenate(
        [panel_blocks.reshape(L_BLOCKS, BS), tail(jnp.concatenate([panel_rows, panel_inner]))]
    )
    right = lax.all_gather(right, "grp", axis=0, tiled=True)
    line = lax.all_to_all(
        jnp.broadcast_to(left[None], (N_Y,) + left.shape), "col", 0, 0, axis_index_groups=Y_LINES
    )
    up_1, down_1 = (lax.ppermute(line, "col", shift_z(s)) for s in (1, -1))
    up_2, down_2 = lax.ppermute(up_1, "col", shift_z(1)), lax.ppermute(down_1, "col", shift_z(-1))
    up_3, down_3 = lax.ppermute(up_2, "col", shift_z(1)), lax.ppermute(down_2, "col", shift_z(-1))
    right = lax.optimization_barrier((right, up_2, down_2))[0]
    table = make_table(right)
    total = multiply(table, right, [line, up_1, down_1])
    up_3, down_3, total = lax.optimization_barrier((up_3, down_3, total))
    ends = [
        lax.ppermute(up_3[: N_Y // 2], "col", shift_z(1)),
        lax.ppermute(down_3[N_Y // 2 :], "col", shift_z(-1)),
    ]
    total = multiply(table, right, [up_2, down_2, up_3, down_3], total)
    return multiply(table, right, ends, total, True)


def solution(mesh):
    placed = (
        P(("grp", "col"), None, None),
        P(("grp", "col")),
        P(("grp", "col")),
        P("grp", "col", None, None),
        P("grp", "col"),
    )
    return jax.shard_map(
        body, mesh=mesh, in_specs=placed, out_specs=P("grp", "col"), check_vma=False
    )
```

time: 305 us -> 123 us (0.40); the launches traced: 300 us -> 122 us
  local copies, waits for them, and re-layouts: 103 us -> 2.28 us
  waiting for transfers between devices: 93.2 us -> 14.2 us
  matrix products: 44.6 us -> 0 us
  starting transfers between devices: 0.04 us -> 35.3 us
  Pallas kernels: 0 us -> 25.8 us
  blocking collectives: 42.8 us -> 25.1 us
    all_gather x2 -> x1, waiting for transfers between devices: 91.8 us -> 0.02 us  [body(): right = lax.all_gather(right, 'grp', axis=0, tiled=True)]
    gather x10 -> x0, local copies, waits for them, and re-layouts: 74.6 us -> none  [the longest x8 68.1 us: one_row(): chosen = strips[pieces[1]]]
    dot_general x9 -> x0, matrix products: 44.6 us -> none  [the longest x8 30.2 us: one_row(): jnp.einsum('pab,pbn->an', pieces[0], chosen, preferred_element_type=jnp.f...]
    ppermute x0 -> x8, starting transfers between devices: none -> 35.3 us  [the longest x2 12.9 us: body(): up_1, down_1 = (lax.ppermute(line, 'col', shift_z(s)) for s in (1, -1))]
    unnamed x1 -> x0, blocking collectives: 31.7 us -> none
    pallas_call x0 -> x4, Pallas kernels: none -> 25.8 us  [the longest x3 22.3 us: multiply(): pl.pallas_call(lambda *refs: multiply_kernel(counts, later, last, *refs),...]
    reshape x2 -> x1, local copies, waits for them, and re-layouts: 25.4 us -> 0.09 us  [tail(): flat = values.astype(jnp.bfloat16).reshape(1, -1)]
    all_to_all x0 -> x1, blocking collectives: none -> 25.1 us  [body(): lax.all_to_all(jnp.broadcast_to(left[None], (N_Y,) + left.shape), 'col',...]
  transfers between devices with their start and end apart: 2 -> 9, of which waited for: 2 -> 2; matrix products, arithmetic and copies ran while one was open for 4% -> 0% of each run, Pallas kernels for 0% -> 16%
where the time goes in v3:
time: 123 us; the launch traced here: 122 us
  starting transfers between devices  35.3 us (29%)
  Pallas kernels  25.8 us (21%)
  blocking collectives  25.1 us (20%)
  waiting for transfers between devices  14.2 us (12%)
  between operations  13.6 us (11%)
  other arithmetic  5.55 us (5%)
  local copies, waits for them, and re-layouts  2.28 us (2%)
    all_to_all x1, blocking collectives, body(): lax.all_to_all(jnp.broadcast_to(left[None], (N_Y,) + left.shape), 'col',...  25.1 us
    pallas_call x3, Pallas kernels, multiply(): pl.pallas_call(lambda *refs: multiply_kernel(counts, later, last, *refs),...  22.3 us
    ppermute x2, starting transfers between devices, body(): up_1, down_1 = (lax.ppermute(line, 'col', shift_z(s)) for s in (1, -1))  12.9 us
    ppermute x2, waiting for transfers between devices, body(): up_1, down_1 = (lax.ppermute(line, 'col', shift_z(s)) for s in (1, -1))  7.93 us
    ppermute x1, waiting for transfers between devices, body(): lax.ppermute(down_1, 'col', shift_z(-1))  6.25 us
    ppermute x1, starting transfers between devices, body(): lax.ppermute(down_1, 'col', shift_z(-1))  5.59 us
    ppermute x1, starting transfers between devices, body(): lax.ppermute(down_2, 'col', shift_z(-1))  5.59 us
    ppermute x1, starting transfers between devices, body(): lax.ppermute(down_3[N_Y // 2:], 'col', shift_z(-1))  5.49 us
  transfers between devices with their start and end apart: 9, of which 2 were waited for; matrix products, arithmetic and copies ran while one was open for 0% of the time, Pallas kernels for 16%

profile of v3, /device:TPU:6, one launch (start us, length us, event | category | flops | bytes accessed | tf_op | source)
XLA Modules:
  0.0 121.9 jit_solution(7236015657543691019)
XLA Ops:
  6.5 0.0 copy-start.4
  6.5 0.0 copy-start.5
  6.5 0.0 copy-start.3
  6.5 0.0 all-gather.2.cloned.1.call-start
  6.5 0.7 convert_element_type.15
  7.3 0.1 copy.8
  7.4 0.1 reshape.43
  7.5 0.1 pad.16.clone
  7.5 4.7 %fusion.3 = bf16[4240,128]{1,0:T(8,128)(2,1)} fusion(bf16[1,32]{1,0:T(2,128)(2,1)S(1)} %reshape.43, bf16[4096,128]{1,0:T(8,128)(2,1)} %bitcast.6, bf16[4240]{0:T(1024)(128)(2,1)S(1)} %pad.16.clone), kind=kLoop, calls=%fused_computation.5 | loop fusion | flops 5427200 | bytes 2142560 | tf_op jit(solution)/shard_map/concatenate | solution.py:194
  12.3 0.0 all-gather.2.cloned.1.call-update
  12.3 0.0 copy-done.4
  12.3 0.0 copy-done.5
  12.3 0.1 fusion.9
  12.4 0.0 copy-done.3
  12.4 0.1 broadcast_in_dim.10
  12.5 25.1 %all_to_all.5.refs_2_ = bf16[8,272,128]{2,1,0:T(8,128)(2,1)S(1)} all-to-all(bf16[8,272,128]{2,1,0:T(8,128)(2,1)S(1)} %broadcast_in_dim.10), channel_id=1, replica_groups={{0,1,2,3,4,5,6,7},{8,9,10,11,12,13,14,15},{16,17,18,19,20,21,22,23},{24..., dimensions={0} | all-to-all | bytes 1114112 | tf_op jit(solution)/shard_map/all_to_all | solution.py:201
  37.6 10.9 %collective-permute-start.2 = (bf16[8,272,128]{2,1,0:T(8,128)(2,1)S(1)}, bf16[8,272,128]{2,1,0:T(8,128)(2,1)S(1)}, u32[]{:S(2)}, u32[]{:S(2)}) collective-permute-start(bf16[8,272,128]{2,1,0:T(8,128)(2,1)S(1)} %all_to_all.5.refs_2_), channel_id=1, source_target_pairs={{0,56},{1,57},{2,58},{3,59},{4,60},{5,61},{6,62},{7,63},{8,0},{9,1... | collective-permute-start | bytes 1671176 | tf_op jit(solution)/shard_map/ppermute | solution.py:204
  48.5 1.9 %collective-permute-start = (bf16[8,272,128]{2,1,0:T(8,128)(2,1)S(1)}, bf16[8,272,128]{2,1,0:T(8,128)(2,1)S(1)}, u32[]{:S(2)}, u32[]{:S(2)}) collective-permute-start(bf16[8,272,128]{2,1,0:T(8,128)(2,1)S(1)} %all_to_all.5.refs_2_), channel_id=1, source_target_pairs={{0,8},{1,9},{2,10},{3,11},{4,12},{5,13},{6,14},{7,15},{8,16},{9,17... | collective-permute-start | bytes 1671176 | tf_op jit(solution)/shard_map/ppermute | solution.py:204
  50.5 7.9 %collective-permute-done.2.refs_4_ = bf16[8,272,128]{2,1,0:T(8,128)(2,1)S(1)} collective-permute-done((bf16[8,272,128]{2,1,0:T(8,128)(2,1)S(1)}, bf16[8,272,128]{2,1,0:T(8,128)(2,1)S(1)}, u32[]{:S(2)}, u32[]{:S(2)}) %collective-permute-start.2) | collective-permute-done | bytes 557088 | tf_op jit(solution)/shard_map/ppermute | solution.py:204
  58.4 5.6 %collective-permute-start.3 = (bf16[8,272,128]{2,1,0:T(8,128)(2,1)S(1)}, bf16[8,272,128]{2,1,0:T(8,128)(2,1)S(1)}, u32[]{:S(2)}, u32[]{:S(2)}) collective-permute-start(bf16[8,272,128]{2,1,0:T(8,128)(2,1)S(1)} %collective-permute-done.2.refs_4_), channel_id=1, source_target_pairs={{0,56},{1,57},{2,58},{3,59},{4,60},{5,61},{6,62},{7,63},{8,0},{9,1... | collective-permute-start | bytes 1671176 | tf_op jit(solution)/shard_map/ppermute | solution.py:205
  64.0 0.0 collective-permute-done.refs_3_
  64.0 1.9 %collective-permute-start.1 = (bf16[8,272,128]{2,1,0:T(8,128)(2,1)S(1)}, bf16[8,272,128]{2,1,0:T(8,128)(2,1)S(1)}, u32[]{:S(2)}, u32[]{:S(2)}) collective-permute-start(bf16[8,272,128]{2,1,0:T(8,128)(2,1)S(1)} %collective-permute-done.refs_3_), channel_id=1, source_target_pairs={{0,8},{1,9},{2,10},{3,11},{4,12},{5,13},{6,14},{7,15},{8,16},{9,17... | collective-permute-start | bytes 1671176 | tf_op jit(solution)/shard_map/ppermute | solution.py:205
  65.9 0.0 copy-start.1
  65.9 0.8 copy-done.1
  66.8 6.2 %collective-permute-done.3.refs_3_ = bf16[8,272,128]{2,1,0:T(8,128)(2,1)S(1)} collective-permute-done((bf16[8,272,128]{2,1,0:T(8,128)(2,1)S(1)}, bf16[8,272,128]{2,1,0:T(8,128)(2,1)S(1)}, u32[]{:S(2)}, u32[]{:S(2)}) %collective-permute-start.3) | collective-permute-done | bytes 557088 | tf_op jit(solution)/shard_map/ppermute | solution.py:205
  73.0 5.6 %collective-permute-start.5 = (bf16[8,272,128]{2,1,0:T(8,128)(2,1)S(1)}, bf16[8,272,128]{2,1,0:T(8,128)(2,1)S(1)}, u32[]{:S(2)}, u32[]{:S(2)}) collective-permute-start(bf16[8,272,128]{2,1,0:T(8,128)(2,1)S(1)} %collective-permute-done.3.refs_3_), channel_id=1, source_target_pairs={{0,56},{1,57},{2,58},{3,59},{4,60},{5,61},{6,62},{7,63},{8,0},{9,1... | collective-permute-start | bytes 1671176 | tf_op jit(solution)/shard_map/ppermute | solution.py:206
  78.6 0.0 collective-permute-done.1.refs_2_
  78.6 1.9 %collective-permute-start.4 = (bf16[8,272,128]{2,1,0:T(8,128)(2,1)S(1)}, bf16[8,272,128]{2,1,0:T(8,128)(2,1)S(1)}, u32[]{:S(2)}, u32[]{:S(2)}) collective-permute-start(bf16[8,272,128]{2,1,0:T(8,128)(2,1)S(1)} %collective-permute-done.1.refs_2_), channel_id=1, source_target_pairs={{0,8},{1,9},{2,10},{3,11},{4,12},{5,13},{6,14},{7,15},{8,16},{9,17... | collective-permute-start | bytes 1671176 | tf_op jit(solution)/shard_map/ppermute | solution.py:206
  80.6 0.0 all-gather.2.cloned.1.call-done.right.refs_1_
  80.6 0.0 copy-start
  80.6 3.5 %shard_map.55.refs_0_ = s32[520]{0:T(1024)S(1)} custom-call(bf16[33920,128]{1,0:T(8,128)(2,1)} %all-gather.2.cloned.1.call-done.right.refs_1_), custom_call_target="tpu_custom_call" | custom-call | bytes 1048576 | tf_op jit(solution)/shard_map/pallas_call | solution.py:64
  84.1 0.0 copy-done
  84.1 0.0 copy-start.2
  84.1 1.0 copy-done.2
  85.2 7.2 %shard_map.56.refs_6_ = f32[1024,1024]{1,0:T(8,128)S(1)} custom-call(s32[520]{0:T(1024)S(1)} %shard_map.55.refs_0_, bf16[33920,128]{1,0:T(8,128)(2,1)S(1)} %copy-done, bf16[8,272,128]{2,1,0:T(8,128)(2,1)S(1)} %all_to_all.5.refs_2_, bf16[8,272,128]{2,1,0:T(8,128)(2,1)S(1)} %copy-done.2, bf16[8,272,128]{2,1,0:T(8,128)(2,1)S(1)} %collective-permute-done.2.refs_4_), custom_call_target="tpu_custom_call" | custom-call | flops 1610612736 | bytes 4194304 | tf_op jit(solution)/shard_map/pallas_call | solution.py:165
  92.4 0.0 collective-permute-done.5.refs_5_
  92.4 0.0 collective-permute-done.4.refs_4_
  92.5 1.9 %collective-permute-start.6 = (bf16[4,272,128]{2,1,0:T(8,128)(2,1)S(1)}, bf16[4,272,128]{2,1,0:T(8,128)(2,1)S(1)}, u32[]{:S(2)}, u32[]{:S(2)}) collective-permute-start(bf16[4,272,128]{2,1,0:T(8,128)(2,1)S(1)} %slice.6), channel_id=1, source_target_pairs={{0,8},{1,9},{2,10},{3,11},{4,12},{5,13},{6,14},{7,15},{8,16},{9,17... | collective-permute-start | bytes 835592 | tf_op jit(solution)/shard_map/ppermute | solution.py:212
  94.4 5.5 %collective-permute-start.7 = (bf16[4,272,128]{2,1,0:T(8,128)(2,1)S(1)}, bf16[4,272,128]{2,1,0:T(8,128)(2,1)S(1)}, u32[]{:S(2)}, u32[]{:S(2)}) collective-permute-start(bf16[4,272,128]{2,1,0:T(8,128)(2,1)S(1)} %slice.7), channel_id=1, source_target_pairs={{0,56},{1,57},{2,58},{3,59},{4,60},{5,61},{6,62},{7,63},{8,0},{9,1... | collective-permute-start | bytes 835592 | tf_op jit(solution)/shard_map/ppermute | solution.py:213
  99.9 9.0 %shard_map.57.refs_4_ = f32[1024,1024]{1,0:T(8,128)S(1)} custom-call(s32[520]{0:T(1024)S(1)} %shard_map.55.refs_0_, bf16[33920,128]{1,0:T(8,128)(2,1)S(1)} %copy-done, bf16[8,272,128]{2,1,0:T(8,128)(2,1)S(1)} %collective-permute-done.1.refs_2_, bf16[8,272,128]{2,1,0:T(8,128)(2,1)S(1)} %collective-permute-done.3.refs_3_, ...), custom_call_target="tpu_custom_call", output_to_operand_aliasing={{}: (6, {})} | custom-call | flops 2147483648 | bytes 4194304 | tf_op jit(solution)/shard_map/pallas_call | solution.py:165
  108.9 0.0 collective-permute-done.6.refs_2_
  108.9 0.0 collective-permute-done.7.refs_3_
  108.9 6.2 %shard_map.58 = bf16[1024,1024]{1,0:T(8,128)(2,1)} custom-call(s32[520]{0:T(1024)S(1)} %shard_map.55.refs_0_, bf16[33920,128]{1,0:T(8,128)(2,1)S(1)} %copy-done, bf16[4,272,128]{2,1,0:T(8,128)(2,1)S(1)} %collective-permute-done.6.refs_2_, bf16[4,272,128]{2,1,0:T(8,128)(2,1)S(1)} %collective-permute-done.7.refs_3_, f32[1024,1024]{1,0:T(8,128)S(1)} %shard_map.57.refs_4_), custom_call_target="tpu_custom_call" | custom-call | flops 536870912 | bytes 4194304 | tf_op jit(solution)/shard_map/pallas_call | solution.py:165
  (5 shorter events, 0.1 us)
Async XLA Ops:
  6.5 5.8 %copy-start.4 = (s32[2]{0:T(128)S(1)}, s32[2]{0:T(128)}, u32[]{:S(2)}) copy-start(s32[2]{0:T(128)} %param.7) | copy-start | bytes 28
  6.5 5.8 %copy-start.5 = (s32[2]{0:T(128)S(1)}, s32[2]{0:T(128)}, u32[]{:S(2)}) copy-start(s32[2]{0:T(128)} %param.6) | copy-start | bytes 28
  6.5 5.9 %copy-start.3 = (bf16[2,128,128]{2,1,0:T(8,128)(2,1)S(1)}, bf16[2,128,128]{2,1,0:T(8,128)(2,1)}, u32[]{:S(2)}) copy-start(bf16[2,128,128]{2,1,0:T(8,128)(2,1)} %param.5) | copy-start | bytes 196612
  6.5 74.0 %all-gather.2.cloned.1.call-start = ((), (), s32[]{:S(2)}) async-start(), calls=%async_computation.1 | async-start | bytes 9768960 | tf_op jit(solution)/shard_map/all_gather | solution.py:200
  37.6 20.8 %collective-permute-start.2 = (bf16[8,272,128]{2,1,0:T(8,128)(2,1)S(1)}, bf16[8,272,128]{2,1,0:T(8,128)(2,1)S(1)}, u32[]{:S(2)}, u32[]{:S(2)}) collective-permute-start(bf16[8,272,128]{2,1,0:T(8,128)(2,1)S(1)} %all_to_all.5.refs_2_), channel_id=1, source_target_pairs={{0,56},{1,57},{2,58},{3,59},{4,60},{5,61},{6,62},{7,63},{8,0},{9,1... | collective-permute-start | bytes 1671176 | tf_op jit(solution)/shard_map/ppermute | solution.py:204
  48.5 15.5 %collective-permute-start = (bf16[8,272,128]{2,1,0:T(8,128)(2,1)S(1)}, bf16[8,272,128]{2,1,0:T(8,128)(2,1)S(1)}, u32[]{:S(2)}, u32[]{:S(2)}) collective-permute-start(bf16[8,272,128]{2,1,0:T(8,128)(2,1)S(1)} %all_to_all.5.refs_2_), channel_id=1, source_target_pairs={{0,8},{1,9},{2,10},{3,11},{4,12},{5,13},{6,14},{7,15},{8,16},{9,17... | collective-permute-start | bytes 1671176 | tf_op jit(solution)/shard_map/ppermute | solution.py:204
  58.4 14.6 %collective-permute-start.3 = (bf16[8,272,128]{2,1,0:T(8,128)(2,1)S(1)}, bf16[8,272,128]{2,1,0:T(8,128)(2,1)S(1)}, u32[]{:S(2)}, u32[]{:S(2)}) collective-permute-start(bf16[8,272,128]{2,1,0:T(8,128)(2,1)S(1)} %collective-permute-done.2.refs_4_), channel_id=1, source_target_pairs={{0,56},{1,57},{2,58},{3,59},{4,60},{5,61},{6,62},{7,63},{8,0},{9,1... | collective-permute-start | bytes 1671176 | tf_op jit(solution)/shard_map/ppermute | solution.py:205
  64.0 14.6 %collective-permute-start.1 = (bf16[8,272,128]{2,1,0:T(8,128)(2,1)S(1)}, bf16[8,272,128]{2,1,0:T(8,128)(2,1)S(1)}, u32[]{:S(2)}, u32[]{:S(2)}) collective-permute-start(bf16[8,272,128]{2,1,0:T(8,128)(2,1)S(1)} %collective-permute-done.refs_3_), channel_id=1, source_target_pairs={{0,8},{1,9},{2,10},{3,11},{4,12},{5,13},{6,14},{7,15},{8,16},{9,17... | collective-permute-start | bytes 1671176 | tf_op jit(solution)/shard_map/ppermute | solution.py:205
  65.9 0.8 copy-start.1
  73.0 19.4 %collective-permute-start.5 = (bf16[8,272,128]{2,1,0:T(8,128)(2,1)S(1)}, bf16[8,272,128]{2,1,0:T(8,128)(2,1)S(1)}, u32[]{:S(2)}, u32[]{:S(2)}) collective-permute-start(bf16[8,272,128]{2,1,0:T(8,128)(2,1)S(1)} %collective-permute-done.3.refs_3_), channel_id=1, source_target_pairs={{0,56},{1,57},{2,58},{3,59},{4,60},{5,61},{6,62},{7,63},{8,0},{9,1... | collective-permute-start | bytes 1671176 | tf_op jit(solution)/shard_map/ppermute | solution.py:206
  78.6 13.8 %collective-permute-start.4 = (bf16[8,272,128]{2,1,0:T(8,128)(2,1)S(1)}, bf16[8,272,128]{2,1,0:T(8,128)(2,1)S(1)}, u32[]{:S(2)}, u32[]{:S(2)}) collective-permute-start(bf16[8,272,128]{2,1,0:T(8,128)(2,1)S(1)} %collective-permute-done.1.refs_2_), channel_id=1, source_target_pairs={{0,8},{1,9},{2,10},{3,11},{4,12},{5,13},{6,14},{7,15},{8,16},{9,17... | collective-permute-start | bytes 1671176 | tf_op jit(solution)/shard_map/ppermute | solution.py:206
  80.6 3.5 %copy-start = (bf16[33920,128]{1,0:T(8,128)(2,1)S(1)}, bf16[33920,128]{1,0:T(8,128)(2,1)}, u32[]{:S(2)}) copy-start(bf16[33920,128]{1,0:T(8,128)(2,1)} %all-gather.2.cloned.1.call-done.right.refs_1_) | copy-start | bytes 26050564
  84.1 1.1 copy-start.2
  92.5 16.4 %collective-permute-start.6 = (bf16[4,272,128]{2,1,0:T(8,128)(2,1)S(1)}, bf16[4,272,128]{2,1,0:T(8,128)(2,1)S(1)}, u32[]{:S(2)}, u32[]{:S(2)}) collective-permute-start(bf16[4,272,128]{2,1,0:T(8,128)(2,1)S(1)} %slice.6), channel_id=1, source_target_pairs={{0,8},{1,9},{2,10},{3,11},{4,12},{5,13},{6,14},{7,15},{8,16},{9,17... | collective-permute-start | bytes 835592 | tf_op jit(solution)/shard_map/ppermute | solution.py:212
  94.4 14.5 %collective-permute-start.7 = (bf16[4,272,128]{2,1,0:T(8,128)(2,1)S(1)}, bf16[4,272,128]{2,1,0:T(8,128)(2,1)S(1)}, u32[]{:S(2)}, u32[]{:S(2)}) collective-permute-start(bf16[4,272,128]{2,1,0:T(8,128)(2,1)S(1)} %slice.7), channel_id=1, source_target_pairs={{0,56},{1,57},{2,58},{3,59},{4,60},{5,61},{6,62},{7,63},{8,0},{9,1... | collective-permute-start | bytes 835592 | tf_op jit(solution)/shard_map/ppermute | solution.py:213
Sparse Core Ops, SparseCore 0:
  12.4 59.0 all-gather.1

commit v4 on v1

--- a/solution.py
+++ b/solution.py
@@ -31,48 +31,58 @@
 Z_LINES = [[z * N_Y + y for z in range(N_Z)] for y in range(N_Y)]
 
 
-def multiply_kernel(place, columns, ids, left, *refs):
-    pieces, (out, left_buf, right_buf, table, order, filled, sem) = refs[:10], refs[10:]
+def multiply_kernel(place, columns, left, *refs):
+    pieces, (out, right, lhs, tiles, values, ids, table, inner, filled, sem) = refs[:10], refs[10:]
     row = pl.program_id(0)
 
     @pl.when(row == 0)
     def load():
-        copies = [pltpu.make_async_copy(left, left_buf, sem.at[0])]
+        heads = pltpu.make_async_copy(left.at[:, pl.ds(L_ROWS, PAD), :], tiles, sem.at[RG])
+        heads.start()
+        copies = []
         slot = 0
         for i, piece in enumerate(pieces):
-            rows = piece.shape[0]
-            blocks = rows // BS
+            blocks = piece.shape[0] // BS
             copies.append(
                 pltpu.make_async_copy(
                     piece.at[pl.ds(0, blocks * BS)],
-                    right_buf.at[pl.ds(slot * BS, blocks * BS)],
-                    sem.at[i + 1],
+                    right.at[pl.ds(slot * BS, blocks * BS)],
+                    sem.at[RG + 1 + i],
                 )
             )
             slot += blocks
         for copy in copies:
             copy.start()
-        right_buf[pl.ds(N_RIGHT * BS, BS), :] = jnp.zeros((BS, BS), jnp.bfloat16)
-        own_x, own_core = place[0] // 2, place[0] % 2
+        right[pl.ds(N_RIGHT * BS, BS), :] = jnp.zeros((BS, BS), jnp.bfloat16)
         for r in range(RG):
             filled[r] = 0
-
-        def list_row(i, carry):
-            device, b = i // 2, i % 2
-            r = ids[device * 4 + b]
-            n = filled[r]
-            order[(r * PER_ROW + n) * 2] = device * (L_ROWS + PAD) + b * BS
-            order[(r * PER_ROW + n) * 2 + 1] = ids[device * 4 + 2 + b]
-            filled[r] = n + 1
-            return carry
-
-        lax.fori_loop(0, N_LEFT, list_row, 0, unroll=4)
+        heads.wait()
+        values[...] = tiles[:, 0, :].astype(jnp.float32).astype(jnp.int32)
+        heads = pltpu.make_async_copy(values, ids, sem.at[RG])
+        heads.start()
+        own_x, own_core = place[0] // 2, place[0] % 2
 
         def clear(i, carry):
             table[i] = N_RIGHT * BS
             return carry
 
         lax.fori_loop(0, KS * JB, clear, 0, unroll=16)
+        heads.wait()
+
+        def list_row(d, carry):
+            for b in range(2):
+                r = ids[d, b]
+                p = filled[r]
+                filled[r] = p + 1
+                inner[r * PER_ROW + p] = ids[d, 2 + b] * JB
+                pltpu.make_async_copy(
+                    left.at[d, pl.ds(b * BS, BS), :],
+                    lhs.at[r, :, pl.ds(pl.multiple_of(p * BS, BS), BS)],
+                    sem.at[r],
+                ).start()
+            return carry
+
+        lax.fori_loop(0, N_LEFT // 2, list_row, 0, unroll=2)
 
         def fill(k, carry):
             g = k // OWN_K
@@ -86,43 +96,49 @@
         for copy in copies:
             copy.wait()
 
-    starts = [pl.multiple_of(order[(row * PER_ROW + p) * 2], BS // 8) for p in range(PER_ROW)]
-    inner = [order[(row * PER_ROW + p) * 2 + 1] * JB for p in range(PER_ROW)]
-    lhs = jnp.concatenate([left_buf[pl.ds(s, BS), :] for s in starts], axis=1)
+    strip = lhs.at[row]
+    pltpu.make_async_copy(strip, strip, sem.at[row]).wait()
+    ks = [inner[row * PER_ROW + p] for p in range(PER_ROW)]
     for j in range(0, JB, 2):
         rhs = jnp.concatenate(
             [
                 jnp.concatenate(
-                    [right_buf[pl.ds(pl.multiple_of(table[k + j + h], BS), BS), :] for h in range(2)],
+                    [right[pl.ds(pl.multiple_of(table[k + j + h], BS), BS), :] for h in range(2)],
                     axis=1,
                 )
-                for k in inner
+                for k in ks
             ],
             axis=0,
         )
-        out[:, j * BS : (j + 2) * BS] = jnp.dot(lhs, rhs, preferred_element_type=jnp.float32).astype(out.dtype)
+        out[:, j * BS : (j + 2) * BS] = jnp.dot(
+            strip[...], rhs, preferred_element_type=jnp.float32
+        ).astype(out.dtype)
 
 
-def multiply(place, columns, ids, left, pieces):
+def multiply(place, columns, left, pieces):
     smem = pl.BlockSpec(memory_space=pltpu.SMEM)
     hbm = pl.BlockSpec(memory_space=pl.ANY)
+    devices = left.shape[0]
     return pl.pallas_call(
         multiply_kernel,
         grid=(RG,),
         out_shape=jax.ShapeDtypeStruct((RG * BS, JB * BS), jnp.bfloat16),
-        in_specs=[smem] * 3 + [hbm] * (1 + len(pieces)),
+        in_specs=[smem] * 2 + [hbm] * (1 + len(pieces)),
         out_specs=pl.BlockSpec((BS, JB * BS), lambda r: (r, 0)),
         scratch_shapes=[
-            pltpu.VMEM(left.shape, jnp.bfloat16),
             pltpu.VMEM(((N_RIGHT + 1) * BS, BS), jnp.bfloat16),
+            pltpu.VMEM((RG, BS, PER_ROW * BS), jnp.bfloat16),
+            pltpu.VMEM((devices, PAD, BS), jnp.bfloat16),
+            pltpu.VMEM((devices, BS), jnp.int32),
+            pltpu.SMEM((devices, BS), jnp.int32),
             pltpu.SMEM((KS * JB,), jnp.int32),
-            pltpu.SMEM((N_LEFT * 2,), jnp.int32),
+            pltpu.SMEM((N_LEFT,), jnp.int32),
             pltpu.SMEM((RG,), jnp.int32),
-            pltpu.SemaphoreType.DMA((1 + len(pieces),)),
+            pltpu.SemaphoreType.DMA((RG + 1 + len(pieces),)),
         ],
-        compiler_params=pltpu.CompilerParams(vmem_limit_bytes=32 * 2**20),
+        compiler_params=pltpu.CompilerParams(vmem_limit_bytes=24 * 2**20),
         cost_estimate=pl.CostEstimate(flops=4 * 2**30, bytes_accessed=14 * 2**20, transcendentals=0),
-    )(place, columns, ids, left, *pieces)
+    )(place, columns, *(pltpu.with_memory_space_constraint(v, pltpu.HBM) for v in [left, *pieces]))
 
 
 def tail(values):
@@ -155,9 +171,8 @@
     columns = jnp.concatenate(
         [v[-PAD, : OWN_K * NBR] for v in pieces if v.shape[0] % BS == PAD]
     ).astype(jnp.int32)
-    ids = lefts[:, L_ROWS, :4].astype(jnp.int32).reshape(-1)
     place = lax.axis_index("grp").reshape(1)
-    return multiply(place, columns, ids, lefts.reshape(-1, BS), pieces)
+    return multiply(place, columns, lefts, pieces)
 
 
 def solution(mesh):

time: 121 us -> 114 us (0.942)
  local copies, waits for them, and re-layouts: 10.1 us -> 1.91 us
  waiting for transfers between devices: 34.3 us -> 36.8 us
    unnamed x18 -> x16, local copies, waits for them, and re-layouts: 8.18 us -> 0.03 us
    all_gather x1, waiting for transfers between devices: 6.95 us -> 8.31 us  [gather_left(): lax.all_gather(line, 'col', axis=0, tiled=True, axis_index_groups=Z_LINES)]
  transfers between devices with their start and end apart: 10 -> 10, of which waited for: 4 -> 5; matrix products, arithmetic and copies ran while one was open for 2% -> 2% of each run, Pallas kernels for 0% -> 0%
where the time goes in v4:
time: 114 us; the launch traced here: 113 us
  waiting for transfers between devices  36.8 us (32%)
  blocking collectives  25.3 us (22%)
  starting transfers between devices  21.3 us (19%)
  between operations  13.6 us (12%)
  Pallas kernels  12.3 us (11%)
  local copies, waits for them, and re-layouts  1.91 us (2%)
  other arithmetic  1.68 us (1%)
    all_to_all x1, blocking collectives, gather_left(): line = lax.all_to_all(copies, 'col', 0, 0, axis_index_groups=Y_LINES)  25.3 us
    ppermute x1, waiting for transfers between devices, gather_right(): before = lax.ppermute(own, 'grp', shift_x(1))  17.1 us
    pallas_call x1, Pallas kernels, multiply(): pl.pallas_call(multiply_kernel, grid=(RG,), out_shape=jax.ShapeDtypeStruc...  12.3 us
    ppermute x5, starting transfers between devices, gather_right(): return mine + [lax.ppermute(v, 'grp', SWAP_CORES) for v in mine]  9.57 us
    all_gather x1, waiting for transfers between devices, gather_left(): lax.all_gather(line, 'col', axis=0, tiled=True, axis_index_groups=Z_LINES)  8.31 us
    ppermute x1, waiting for transfers between devices, gather_right(): far_head = lax.ppermute(before[:R_ROWS // 2], 'grp', shift_x(1))  7.76 us
    ppermute x1, starting transfers between devices, gather_right(): after = lax.ppermute(own, 'grp', shift_x(-1))  3.46 us
    ppermute x1, starting transfers between devices, gather_right(): far_head = lax.ppermute(before[:R_ROWS // 2], 'grp', shift_x(1))  3.41 us
  transfers between devices with their start and end apart: 10, of which 5 were waited for; matrix products, arithmetic and copies ran while one was open for 2% of the time, Pallas kernels for 0%

profile of v4, /device:TPU:6, one launch (start us, length us, event | category | flops | bytes accessed | tf_op | source)
XLA Modules:
  0.0 112.9 jit_solution(11361417936542894269)
XLA Ops:
  6.5 0.0 all-gather.2.cloned.1.call-start
  6.5 0.7 convert_bitcast_fusion
  7.2 0.1 fusion.7
  7.3 0.8 pad_maximum_fusion
  8.1 0.0 copy-start.4
  8.1 0.0 copy-start.1
  8.1 0.1 broadcast_in_dim.2
  8.2 25.3 %all_to_all.5 = bf16[8,272,128]{2,1,0:T(8,128)(2,1)} all-to-all(bf16[8,272,128]{2,1,0:T(8,128)(2,1)S(1)} %broadcast_in_dim.2), channel_id=1, replica_groups={{0,1,2,3,4,5,6,7},{8,9,10,11,12,13,14,15},{16,17,18,19,20,21,22,23},{24..., dimensions={0} | all-to-all | bytes 1114112 | tf_op jit(solution)/shard_map/all_to_all | solution.py:160
  33.6 0.0 all-gather.2.cloned.1.call-update
  33.6 0.0 copy-done.4
  33.6 0.1 copy.10
  33.7 0.1 reshape.48
  33.8 0.0 copy-done.1
  33.8 0.1 fusion.1.refs_0_
  33.9 0.0 copy-start
  33.9 2.4 %collective-permute-start.2 = (bf16[4112,128]{1,0:T(8,128)(2,1)S(1)}, bf16[4112,128]{1,0:T(8,128)(2,1)S(1)}, u32[]{:S(2)}, u32[]{:S(2)}) collective-permute-start(bf16[4112,128]{1,0:T(8,128)(2,1)S(1)} %fusion.1.refs_0_), channel_id=1, source_target_pairs={{0,128},{64,192},{128,256},{192,320},{256,384},{320,448},{384,0},{... | collective-permute-start | bytes 3158024 | tf_op jit(solution)/shard_map/ppermute | solution.py:151
  36.3 3.5 %collective-permute-start = (bf16[4112,128]{1,0:T(8,128)(2,1)S(1)}, bf16[4112,128]{1,0:T(8,128)(2,1)S(1)}, u32[]{:S(2)}, u32[]{:S(2)}) collective-permute-start(bf16[4112,128]{1,0:T(8,128)(2,1)S(1)} %fusion.1.refs_0_), channel_id=1, source_target_pairs={{0,384},{64,448},{128,0},{192,64},{256,128},{320,192},{384,256},{4... | collective-permute-start | bytes 3158024 | tf_op jit(solution)/shard_map/ppermute | solution.py:150
  39.7 1.9 %collective-permute-start.3 = (bf16[4112,128]{1,0:T(8,128)(2,1)S(1)}, bf16[4112,128]{1,0:T(8,128)(2,1)}, u32[]{:S(2)}, u32[]{:S(2)}) collective-permute-start(bf16[4112,128]{1,0:T(8,128)(2,1)S(1)} %fusion.1.refs_0_), channel_id=1, source_target_pairs={{0,64},{64,0},{128,192},{192,128},{256,320},{320,256},{384,448},{4... | collective-permute-start | bytes 3158024 | tf_op jit(solution)/shard_map/ppermute | solution.py:155
  41.7 17.1 %collective-permute-done.2.refs_4_ = bf16[4112,128]{1,0:T(8,128)(2,1)S(1)} collective-permute-done((bf16[4112,128]{1,0:T(8,128)(2,1)S(1)}, bf16[4112,128]{1,0:T(8,128)(2,1)S(1)}, u32[]{:S(2)}, u32[]{:S(2)}) %collective-permute-start.2) | collective-permute-done | bytes 1052704 | tf_op jit(solution)/shard_map/ppermute | solution.py:151
  58.8 0.0 copy-start.3
  58.8 1.9 %collective-permute-start.6 = (bf16[4112,128]{1,0:T(8,128)(2,1)S(1)}, bf16[4112,128]{1,0:T(8,128)(2,1)}, u32[]{:S(2)}, u32[]{:S(2)}) collective-permute-start(bf16[4112,128]{1,0:T(8,128)(2,1)S(1)} %collective-permute-done.2.refs_4_), channel_id=1, source_target_pairs={{0,64},{64,0},{128,192},{192,128},{256,320},{320,256},{384,448},{4... | collective-permute-start | bytes 3158024 | tf_op jit(solution)/shard_map/ppermute | solution.py:155
  60.7 0.1 squeeze.24
  60.8 3.4 %collective-permute-start.7 = (bf16[2048,128]{1,0:T(8,128)(2,1)S(1)}, bf16[2048,128]{1,0:T(8,128)(2,1)}, u32[]{:S(2)}, u32[]{:S(2)}) collective-permute-start(bf16[2048,128]{1,0:T(8,128)(2,1)S(1)} %slice.45), channel_id=1, source_target_pairs={{0,128},{64,192},{128,256},{192,320},{256,384},{320,448},{384,0},{... | collective-permute-start | bytes 1572872 | tf_op jit(solution)/shard_map/ppermute | solution.py:152
  64.2 0.0 collective-permute-done.refs_1_
  64.2 0.0 copy-start.2
  64.3 0.0 copy-done
  64.3 2.4 %collective-permute-start.1 = (bf16[2064,128]{1,0:T(8,128)(2,1)S(1)}, bf16[2064,128]{1,0:T(8,128)(2,1)S(1)}, u32[]{:S(2)}, u32[]{:S(2)}) collective-permute-start(bf16[2064,128]{1,0:T(8,128)(2,1)S(1)} %slice.38), channel_id=1, source_target_pairs={{0,384},{64,448},{128,0},{192,64},{256,128},{320,192},{384,256},{4... | collective-permute-start | bytes 1585160 | tf_op jit(solution)/shard_map/ppermute | solution.py:153
  66.7 1.9 %collective-permute-start.4 = (bf16[4112,128]{1,0:T(8,128)(2,1)S(1)}, bf16[4112,128]{1,0:T(8,128)(2,1)S(1)}, u32[]{:S(2)}, u32[]{:S(2)}) collective-permute-start(bf16[4112,128]{1,0:T(8,128)(2,1)S(1)} %collective-permute-done.refs_1_), channel_id=1, source_target_pairs={{0,64},{64,0},{128,192},{192,128},{256,320},{320,256},{384,448},{4... | collective-permute-start | bytes 3158024 | tf_op jit(solution)/shard_map/ppermute | solution.py:155
  68.7 0.0 collective-permute-done.3.refs_5_
  68.7 0.7 slice_bitcast_fusion.3
  69.4 7.8 %collective-permute-done.7.refs_2_ = bf16[2048,128]{1,0:T(8,128)(2,1)} collective-permute-done((bf16[2048,128]{1,0:T(8,128)(2,1)S(1)}, bf16[2048,128]{1,0:T(8,128)(2,1)}, u32[]{:S(2)}, u32[]{:S(2)}) %collective-permute-start.7) | collective-permute-done | bytes 524320 | tf_op jit(solution)/shard_map/ppermute | solution.py:152
  77.1 1.9 %collective-permute-start.8 = (bf16[2048,128]{1,0:T(8,128)(2,1)}, bf16[2048,128]{1,0:T(8,128)(2,1)}, u32[]{:S(2)}, u32[]{:S(2)}) collective-permute-start(bf16[2048,128]{1,0:T(8,128)(2,1)} %collective-permute-done.7.refs_2_), channel_id=1, source_target_pairs={{0,64},{64,0},{128,192},{192,128},{256,320},{320,256},{384,448},{4... | collective-permute-start | bytes 1572872 | tf_op jit(solution)/shard_map/ppermute | solution.py:155
  79.0 2.5 %collective-permute-done.1.refs_3_ = bf16[2064,128]{1,0:T(8,128)(2,1)S(1)} collective-permute-done((bf16[2064,128]{1,0:T(8,128)(2,1)S(1)}, bf16[2064,128]{1,0:T(8,128)(2,1)S(1)}, u32[]{:S(2)}, u32[]{:S(2)}) %collective-permute-start.1) | collective-permute-done | bytes 528416 | tf_op jit(solution)/shard_map/ppermute | solution.py:153
  81.5 0.0 copy-start.6
  81.5 1.9 %collective-permute-start.5 = (bf16[2064,128]{1,0:T(8,128)(2,1)S(1)}, bf16[2064,128]{1,0:T(8,128)(2,1)S(1)}, u32[]{:S(2)}, u32[]{:S(2)}) collective-permute-start(bf16[2064,128]{1,0:T(8,128)(2,1)S(1)} %collective-permute-done.1.refs_3_), channel_id=1, source_target_pairs={{0,64},{64,0},{128,192},{192,128},{256,320},{320,256},{384,448},{4... | collective-permute-start | bytes 1585160 | tf_op jit(solution)/shard_map/ppermute | solution.py:155
  83.5 0.0 collective-permute-done.6.refs_9_
  83.5 0.7 slice_bitcast_fusion
  84.2 0.0 collective-permute-done.4.refs_6_
  84.2 0.0 copy-start.5
  84.2 1.2 %collective-permute-done.5.refs_8_ = bf16[2064,128]{1,0:T(8,128)(2,1)S(1)} collective-permute-done((bf16[2064,128]{1,0:T(8,128)(2,1)S(1)}, bf16[2064,128]{1,0:T(8,128)(2,1)S(1)}, u32[]{:S(2)}, u32[]{:S(2)}) %collective-permute-start.5) | collective-permute-done | bytes 528416 | tf_op jit(solution)/shard_map/ppermute | solution.py:155
  85.3 0.0 copy-done.6
  85.3 0.0 copy-done.5
  85.3 0.0 copy-start.7
  85.4 0.1 concatenate.25
  85.5 0.0 collective-permute-done.8.refs_7_
  85.5 8.3 %all-gather.2.cloned.1.call-done.left = bf16[64,272,128]{2,1,0:T(8,128)(2,1)} async-done(((bf16[8,272,128]{2,1,0:T(8,128)(2,1)}), bf16[64,272,128]{2,1,0:T(8,128)(2,1)}) %all-gather.2.cloned.1.call-update) | async-done | bytes 4456464 | tf_op jit(solution)/shard_map/all_gather | solution.py:161
  93.8 0.0 copy-done.3
  93.8 0.0 copy-done.2
  93.8 0.0 copy-done.7
  93.8 12.3 %shard_map.55 = bf16[1024,1024]{1,0:T(8,128)(2,1)} custom-call(s32[1]{0:T(128)} %bitcast.place, s32[256]{0:T(256)S(1)} %convert_element_type.19.columns, bf16[64,272,128]{2,1,0:T(8,128)(2,1)} %all-gather.2.cloned.1.call-done.left, bf16[4112,128]{1,0:T(8,128)(2,1)} %copy-done, bf16[4112,128]{1,0:T(8,128)(2,1)} %copy-done.2, ...), custom_call_target="tpu_custom_call" | custom-call | flops 4294967296 | bytes 14680064 | tf_op jit(solution)/shard_map/pallas_call | solution.py:122
  (9 shorter events, 0.1 us)
Async XLA Ops:
  6.5 87.2 %all-gather.2.cloned.1.call-start = ((), (), s32[]{:S(2)}) async-start(), calls=%async_computation.1 | async-start | bytes 5013504 | tf_op jit(solution)/shard_map/all_gather | solution.py:161
  8.1 25.4 %copy-start.4 = (s32[8,4]{0,1:T(4,128)S(1)}, s32[8,4]{0,1:T(4,128)}, u32[]{:S(2)}) copy-start(s32[8,4]{0,1:T(4,128)} %param.9) | copy-start | bytes 388
  8.1 25.7 %copy-start.1 = (bf16[8,4,128,128]{3,2,1,0:T(8,128)(2,1)S(1)}, bf16[8,4,128,128]{3,2,1,0:T(8,128)(2,1)}, u32[]{:S(2)}) copy-start(bf16[8,4,128,128]{3,2,1,0:T(8,128)(2,1)} %param.8) | copy-start | bytes 3145732
  33.9 30.4 %copy-start = (bf16[4112,128]{1,0:T(8,128)(2,1)}, bf16[4112,128]{1,0:T(8,128)(2,1)S(1)}, u32[]{:S(2)}) copy-start(bf16[4112,128]{1,0:T(8,128)(2,1)S(1)} %fusion.1.refs_0_) | copy-start | bytes 3158020
  33.9 24.9 %collective-permute-start.2 = (bf16[4112,128]{1,0:T(8,128)(2,1)S(1)}, bf16[4112,128]{1,0:T(8,128)(2,1)S(1)}, u32[]{:S(2)}, u32[]{:S(2)}) collective-permute-start(bf16[4112,128]{1,0:T(8,128)(2,1)S(1)} %fusion.1.refs_0_), channel_id=1, source_target_pairs={{0,128},{64,192},{128,256},{192,320},{256,384},{320,448},{384,0},{... | collective-permute-start | bytes 3158024 | tf_op jit(solution)/shard_map/ppermute | solution.py:151
  36.3 28.0 %collective-permute-start = (bf16[4112,128]{1,0:T(8,128)(2,1)S(1)}, bf16[4112,128]{1,0:T(8,128)(2,1)S(1)}, u32[]{:S(2)}, u32[]{:S(2)}) collective-permute-start(bf16[4112,128]{1,0:T(8,128)(2,1)S(1)} %fusion.1.refs_0_), channel_id=1, source_target_pairs={{0,384},{64,448},{128,0},{192,64},{256,128},{320,192},{384,256},{4... | collective-permute-start | bytes 3158024 | tf_op jit(solution)/shard_map/ppermute | solution.py:150
  39.7 29.0 %collective-permute-start.3 = (bf16[4112,128]{1,0:T(8,128)(2,1)S(1)}, bf16[4112,128]{1,0:T(8,128)(2,1)}, u32[]{:S(2)}, u32[]{:S(2)}) collective-permute-start(bf16[4112,128]{1,0:T(8,128)(2,1)S(1)} %fusion.1.refs_0_), channel_id=1, source_target_pairs={{0,64},{64,0},{128,192},{192,128},{256,320},{320,256},{384,448},{4... | collective-permute-start | bytes 3158024 | tf_op jit(solution)/shard_map/ppermute | solution.py:155
  58.8 35.0 %copy-start.3 = (bf16[4112,128]{1,0:T(8,128)(2,1)}, bf16[4112,128]{1,0:T(8,128)(2,1)S(1)}, u32[]{:S(2)}) copy-start(bf16[4112,128]{1,0:T(8,128)(2,1)S(1)} %collective-permute-done.2.refs_4_) | copy-start | bytes 3158020
  58.8 24.7 %collective-permute-start.6 = (bf16[4112,128]{1,0:T(8,128)(2,1)S(1)}, bf16[4112,128]{1,0:T(8,128)(2,1)}, u32[]{:S(2)}, u32[]{:S(2)}) collective-permute-start(bf16[4112,128]{1,0:T(8,128)(2,1)S(1)} %collective-permute-done.2.refs_4_), channel_id=1, source_target_pairs={{0,64},{64,0},{128,192},{192,128},{256,320},{320,256},{384,448},{4... | collective-permute-start | bytes 3158024 | tf_op jit(solution)/shard_map/ppermute | solution.py:155
  60.8 16.3 %collective-permute-start.7 = (bf16[2048,128]{1,0:T(8,128)(2,1)S(1)}, bf16[2048,128]{1,0:T(8,128)(2,1)}, u32[]{:S(2)}, u32[]{:S(2)}) collective-permute-start(bf16[2048,128]{1,0:T(8,128)(2,1)S(1)} %slice.45), channel_id=1, source_target_pairs={{0,128},{64,192},{128,256},{192,320},{256,384},{320,448},{384,0},{... | collective-permute-start | bytes 1572872 | tf_op jit(solution)/shard_map/ppermute | solution.py:152
  64.2 29.5 %copy-start.2 = (bf16[4112,128]{1,0:T(8,128)(2,1)}, bf16[4112,128]{1,0:T(8,128)(2,1)S(1)}, u32[]{:S(2)}) copy-start(bf16[4112,128]{1,0:T(8,128)(2,1)S(1)} %collective-permute-done.refs_1_) | copy-start | bytes 3158020
  64.3 17.2 %collective-permute-start.1 = (bf16[2064,128]{1,0:T(8,128)(2,1)S(1)}, bf16[2064,128]{1,0:T(8,128)(2,1)S(1)}, u32[]{:S(2)}, u32[]{:S(2)}) collective-permute-start(bf16[2064,128]{1,0:T(8,128)(2,1)S(1)} %slice.38), channel_id=1, source_target_pairs={{0,384},{64,448},{128,0},{192,64},{256,128},{320,192},{384,256},{4... | collective-permute-start | bytes 1585160 | tf_op jit(solution)/shard_map/ppermute | solution.py:153
  66.7 17.4 %collective-permute-start.4 = (bf16[4112,128]{1,0:T(8,128)(2,1)S(1)}, bf16[4112,128]{1,0:T(8,128)(2,1)S(1)}, u32[]{:S(2)}, u32[]{:S(2)}) collective-permute-start(bf16[4112,128]{1,0:T(8,128)(2,1)S(1)} %collective-permute-done.refs_1_), channel_id=1, source_target_pairs={{0,64},{64,0},{128,192},{192,128},{256,320},{320,256},{384,448},{4... | collective-permute-start | bytes 3158024 | tf_op jit(solution)/shard_map/ppermute | solution.py:155
  77.1 8.3 %collective-permute-start.8 = (bf16[2048,128]{1,0:T(8,128)(2,1)}, bf16[2048,128]{1,0:T(8,128)(2,1)}, u32[]{:S(2)}, u32[]{:S(2)}) collective-permute-start(bf16[2048,128]{1,0:T(8,128)(2,1)} %collective-permute-done.7.refs_2_), channel_id=1, source_target_pairs={{0,64},{64,0},{128,192},{192,128},{256,320},{320,256},{384,448},{4... | collective-permute-start | bytes 1572872 | tf_op jit(solution)/shard_map/ppermute | solution.py:155
  81.5 3.8 %copy-start.6 = (bf16[2064,128]{1,0:T(8,128)(2,1)}, bf16[2064,128]{1,0:T(8,128)(2,1)S(1)}, u32[]{:S(2)}) copy-start(bf16[2064,128]{1,0:T(8,128)(2,1)S(1)} %collective-permute-done.1.refs_3_) | copy-start | bytes 1585156
  81.5 3.8 %collective-permute-start.5 = (bf16[2064,128]{1,0:T(8,128)(2,1)S(1)}, bf16[2064,128]{1,0:T(8,128)(2,1)S(1)}, u32[]{:S(2)}, u32[]{:S(2)}) collective-permute-start(bf16[2064,128]{1,0:T(8,128)(2,1)S(1)} %collective-permute-done.1.refs_3_), channel_id=1, source_target_pairs={{0,64},{64,0},{128,192},{192,128},{256,320},{320,256},{384,448},{4... | collective-permute-start | bytes 1585160 | tf_op jit(solution)/shard_map/ppermute | solution.py:155
  84.2 1.2 %copy-start.5 = (bf16[4112,128]{1,0:T(8,128)(2,1)}, bf16[4112,128]{1,0:T(8,128)(2,1)S(1)}, u32[]{:S(2)}) copy-start(bf16[4112,128]{1,0:T(8,128)(2,1)S(1)} %collective-permute-done.4.refs_6_) | copy-start | bytes 3158020
  85.3 8.4 %copy-start.7 = (bf16[2064,128]{1,0:T(8,128)(2,1)}, bf16[2064,128]{1,0:T(8,128)(2,1)S(1)}, u32[]{:S(2)}) copy-start(bf16[2064,128]{1,0:T(8,128)(2,1)S(1)} %collective-permute-done.5.refs_8_) | copy-start | bytes 1585156
Sparse Core Ops, SparseCore 0:
  33.7 60.0 all-gather.1

commit v5 on v1

v5 whole, which is shorter than its diff:
```python
import jax
import jax.numpy as jnp
from jax import lax
from jax.experimental import pallas as pl
from jax.experimental.pallas import tpu as pltpu
from jax.sharding import PartitionSpec as P

BS = 128
RG = 8
KS = 64
JB = 8
NBR = 4
PER_ROW = 16
N_GRP = 8
N_X = 4
N_Y = 8
N_Z = 8
PAD = 16
OWN_K = 8
R_ROWS = OWN_K * NBR * BS
L_ROWS = 2 * BS
N_LEFT = 128
N_RIGHT = KS * NBR


def shift_x(step):
    return [(x * 2 + c, ((x + step) % N_X) * 2 + c) for x in range(N_X) for c in range(2)]


SWAP_CORES = [(g, g ^ 1) for g in range(2 * N_X)]
Y_LINES = [[z * N_Y + y for y in range(N_Y)] for z in range(N_Z)]


def shift_z(step):
    return [(z * N_Y + y, ((z + step) % N_Z) * N_Y + y) for z in range(N_Z) for y in range(N_Y)]


def assemble_kernel(counts, *refs):
    n = len(counts)
    pieces, (strips, inner, tiles, values, ids, filled, sem) = refs[:n], refs[n:]
    firsts = [sum(counts[:i]) for i in range(n)]
    copies = [
        pltpu.make_async_copy(
            piece.at[:, pl.ds(L_ROWS, PAD), :], tiles.at[pl.ds(firsts[i], counts[i])], sem.at[i + 1]
        )
        for i, piece in enumerate(pieces)
    ]
    for copy in copies:
        copy.start()
    for r in range(RG):
        filled[r] = 0
    for copy in copies:
        copy.wait()
    values[...] = tiles[:, 0, :].astype(jnp.float32).astype(jnp.int32)
    copy = pltpu.make_async_copy(values, ids, sem.at[1])
    copy.start()
    copy.wait()
    for i, piece in enumerate(pieces):

        def place(d, carry, i=i, piece=piece):
            for b in range(2):
                r = ids[firsts[i] + d, b]
                p = filled[r]
                filled[r] = p + 1
                inner[r * PER_ROW + p] = ids[firsts[i] + d, 2 + b] * JB
                pltpu.make_async_copy(
                    piece.at[d, pl.ds(b * BS, BS), :],
                    strips.at[r, :, pl.ds(pl.multiple_of(p * BS, BS), BS)],
                    sem.at[0],
                ).start()
            return carry

        lax.fori_loop(0, counts[i], place, 0, unroll=2)
    pltpu.make_async_copy(strips, strips, sem.at[0]).wait()


def assemble(pieces):
    counts = tuple(piece.shape[0] for piece in pieces)
    devices = sum(counts)
    return pl.pallas_call(
        lambda *refs: assemble_kernel(counts, *refs),
        out_shape=(
            pltpu.VMEM((RG, BS, PER_ROW * BS), jnp.bfloat16),
            jax.ShapeDtypeStruct((N_LEFT,), jnp.int32),
        ),
        in_specs=[pl.BlockSpec(memory_space=pl.ANY)] * len(pieces),
        out_specs=(pl.BlockSpec(memory_space=pltpu.VMEM), pl.BlockSpec(memory_space=pltpu.SMEM)),
        scratch_shapes=[
            pltpu.VMEM((devices, PAD, BS), jnp.bfloat16),
            pltpu.VMEM((devices, BS), jnp.int32),
            pltpu.SMEM((devices, BS), jnp.int32),
            pltpu.SMEM((RG,), jnp.int32),
            pltpu.SemaphoreType.DMA((1 + len(pieces),)),
        ],
        compiler_params=pltpu.CompilerParams(vmem_limit_bytes=4 * 2**20),
        cost_estimate=pl.CostEstimate(flops=0, bytes_accessed=8 * 2**20, transcendentals=0),
    )(*pieces)


def multiply_kernel(place, inner, strips, *refs):
    pieces, (out, right, tiles, values, columns, table, sem) = refs[:10], refs[10:]
    row = pl.program_id(0)

    @pl.when(row == 0)
    def load():
        heads, copies = [], []
        slot = 0
        for i, piece in enumerate(pieces):
            rows = piece.shape[0]
            blocks = rows // BS
            if rows % BS:
                n = len(heads)
                heads.append(
                    pltpu.make_async_copy(piece.at[pl.ds(rows - PAD, PAD)], tiles.at[n], sem.at[10 + n])
                )
            copies.append(
                pltpu.make_async_copy(
                    piece.at[pl.ds(0, blocks * BS)], right.at[pl.ds(slot * BS, blocks * BS)], sem.at[i]
                )
            )
            slot += blocks
        for copy in heads + copies:
            copy.start()
        right[pl.ds(N_RIGHT * BS, BS), :] = jnp.zeros((BS, BS), jnp.bfloat16)
        for copy in heads:
            copy.wait()
        values[...] = tiles[:, 0, :].astype(jnp.float32).astype(jnp.int32)
        copy = pltpu.make_async_copy(values, columns, sem.at[10])
        copy.start()
        own_x, own_core = place[0] // 2, place[0] % 2

        def clear(i, carry):
            table[i] = N_RIGHT * BS
            return carry

        lax.fori_loop(0, KS * JB, clear, 0, unroll=16)
        copy.wait()

        def fill(k, carry):
            g, i = k // OWN_K, k % OWN_K
            s = ((g + own_core) % 2) * N_X + (g // 2 + N_X - own_x) % N_X
            for m in range(NBR):
                table[k * JB + columns[s, i * NBR + m]] = ((s * OWN_K + i) * NBR + m) * BS
            return carry

        lax.fori_loop(0, KS, fill, 0, unroll=2)
        for copy in copies:
            copy.wait()

    ks = [inner[row * PER_ROW + p] for p in range(PER_ROW)]
    for j in range(0, JB, 2):
        rhs = jnp.concatenate(
            [
                jnp.concatenate(
                    [right[pl.ds(pl.multiple_of(table[k + j + h], BS), BS), :] for h in range(2)],
                    axis=1,
                )
                for k in ks
            ],
            axis=0,
        )
        out[:, j * BS : (j + 2) * BS] = jnp.dot(
            strips[row], rhs, preferred_element_type=jnp.float32
        ).astype(out.dtype)


def multiply(place, inner, strips, pieces):
    smem = pl.BlockSpec(memory_space=pltpu.SMEM)
    return pl.pallas_call(
        multiply_kernel,
        grid=(RG,),
        out_shape=jax.ShapeDtypeStruct((RG * BS, JB * BS), jnp.bfloat16),
        in_specs=[smem] * 2
        + [pl.BlockSpec(memory_space=pltpu.VMEM)]
        + [pl.BlockSpec(memory_space=pl.ANY)] * len(pieces),
        out_specs=pl.BlockSpec((BS, JB * BS), lambda r: (r, 0)),
        scratch_shapes=[
            pltpu.VMEM(((N_RIGHT + 1) * BS, BS), jnp.bfloat16),
            pltpu.VMEM((N_GRP, PAD, BS), jnp.bfloat16),
            pltpu.VMEM((N_GRP, BS), jnp.int32),
            pltpu.SMEM((N_GRP, BS), jnp.int32),
            pltpu.SMEM((KS * JB,), jnp.int32),
            pltpu.SemaphoreType.DMA((10 + N_GRP,)),
        ],
        compiler_params=pltpu.CompilerParams(vmem_limit_bytes=16 * 2**20),
        cost_estimate=pl.CostEstimate(flops=4 * 2**30, bytes_accessed=14 * 2**20, transcendentals=0),
    )(place, inner, pltpu.with_memory_space_constraint(strips, pltpu.VMEM), *pieces)


def tail(values):
    flat = values.astype(jnp.bfloat16).reshape(1, -1)
    return jnp.pad(flat, ((0, PAD - 1), (0, BS - flat.shape[1])))


def gather(left, right):
    copies = jnp.broadcast_to(left[None], (N_Y,) + left.shape)
    line = lax.all_to_all(copies, "col", 0, 0, axis_index_groups=Y_LINES)
    up_1, down_1 = (lax.ppermute(line, "col", shift_z(s)) for s in (1, -1))
    after = lax.ppermute(right, "grp", shift_x(-1))
    before = lax.ppermute(right, "grp", shift_x(1))
    far_head = lax.ppermute(before[: R_ROWS // 2], "grp", shift_x(1))
    far_tail = lax.ppermute(after[R_ROWS // 2 :], "grp", shift_x(-1))
    mine = [right, after, far_head, far_tail, before]
    others = [lax.ppermute(v, "grp", SWAP_CORES) for v in mine]
    up_1, down_1 = lax.optimization_barrier((up_1, down_1, after, before))[:2]
    up_2, down_2 = lax.ppermute(up_1, "col", shift_z(1)), lax.ppermute(down_1, "col", shift_z(-1))
    up_3, down_3 = lax.ppermute(up_2, "col", shift_z(1)), lax.ppermute(down_2, "col", shift_z(-1))
    up_3, down_3 = lax.optimization_barrier((up_3, down_3, others[0], others[1], others[4]))[:2]
    ends = [
        lax.ppermute(up_3[: N_Y // 2], "col", shift_z(1)),
        lax.ppermute(down_3[N_Y // 2 :], "col", shift_z(-1)),
    ]
    return [line, up_1, down_1, up_2, down_2, up_3, down_3] + ends, mine + others


def body(panel_blocks, panel_rows, panel_inner, right_blocks, right_columns):
    right = jnp.concatenate([right_blocks.reshape(R_ROWS, BS), tail(right_columns)])
    left = jnp.concatenate(
        [panel_blocks.reshape(L_ROWS, BS), tail(jnp.concatenate([panel_rows, panel_inner]))]
    )
    lefts, pieces = gather(left, right)
    strips, inner = assemble(lefts)
    place = lax.axis_index("grp").reshape(1)
    return multiply(place, inner, strips, pieces)


def solution(mesh):
    placed = (
        P(("grp", "col"), None, None),
        P(("grp", "col")),
        P(("grp", "col")),
        P("grp", "col", None, None),
        P("grp", "col"),
    )
    return jax.shard_map(
        body, mesh=mesh, in_specs=placed, out_specs=P("grp", "col"), check_vma=False
    )
```

time: 121 us -> 123 us (1.017)
  starting transfers between devices: 21.3 us -> 63.3 us
  blocking collectives: 25.3 us -> 0 us
  between operations: 13.6 us -> 0.31 us
  waiting for transfers between devices: 34.3 us -> 28.3 us
  Pallas kernels: 11.9 us -> 16.5 us
  local copies, waits for them, and re-layouts: 10.1 us -> 11.4 us
    ppermute x9 -> x17, starting transfers between devices: 21.3 us -> 56.2 us  [the longest x2 12.9 us: gather(): up_1, down_1 = (lax.ppermute(line, 'col', shift_z(s)) for s in (1, -1))]
    all_to_all x1 -> x0, blocking collectives: 25.3 us -> none  [gather_left(): line = lax.all_to_all(copies, 'col', 0, 0, axis_index_groups=Y_LINES)]
    all_to_all x0 -> x1, waiting for transfers between devices: none -> 9.84 us  [gather(): line = lax.all_to_all(copies, 'col', 0, 0, axis_index_groups=Y_LINES)]
    ppermute x9 -> x17, waiting for transfers between devices: 27.3 us -> 18.5 us  [the longest x2 6.62 us: gather(): up_1, down_1 = (lax.ppermute(line, 'col', shift_z(s)) for s in (1, -1))]
    all_to_all x0 -> x1, starting transfers between devices: none -> 7.1 us  [gather(): line = lax.all_to_all(copies, 'col', 0, 0, axis_index_groups=Y_LINES)]
    all_gather x1 -> x0, waiting for transfers between devices: 6.95 us -> none  [gather_left(): lax.all_gather(line, 'col', axis=0, tiled=True, axis_index_groups=Z_LINES)]
    pallas_call x0 -> x1, Pallas kernels: none -> 5.55 us  [assemble(): pl.pallas_call(lambda *refs: assemble_kernel(counts, *refs), out_shape=(p...]
    slice x2 -> x4, local copies, waits for them, and re-layouts: 0.07 us -> 3.64 us  [the longest x1 1.08 us: gather(): far_tail = lax.ppermute(after[R_ROWS // 2:], 'grp', shift_x(-1))]
  transfers between devices with their start and end apart: 10 -> 18, of which waited for: 4 -> 8; matrix products, arithmetic and copies ran while one was open for 2% -> 3% of each run, Pallas kernels for 0% -> 5%
where the time goes in v5:
time: 123 us; the launch traced here: 122 us
  starting transfers between devices  63.3 us (51%)
  waiting for transfers between devices  28.3 us (23%)
  Pallas kernels  16.5 us (13%)
  local copies, waits for them, and re-layouts  11.4 us (9%)
  other arithmetic  1.76 us (1%)
    ppermute x2, starting transfers between devices, gather(): up_1, down_1 = (lax.ppermute(line, 'col', shift_z(s)) for s in (1, -1))  12.9 us
    pallas_call x1, Pallas kernels, multiply(): pl.pallas_call(multiply_kernel, grid=(RG,), out_shape=jax.ShapeDtypeStruc...  11 us
    ppermute x5, starting transfers between devices, gather(): others = [lax.ppermute(v, 'grp', SWAP_CORES) for v in mine]  10.1 us
    all_to_all x1, waiting for transfers between devices, gather(): line = lax.all_to_all(copies, 'col', 0, 0, axis_index_groups=Y_LINES)  9.84 us
    all_to_all x1, starting transfers between devices, gather(): line = lax.all_to_all(copies, 'col', 0, 0, axis_index_groups=Y_LINES)  7.1 us
    unnamed x24, local copies, waits for them, and re-layouts  6.74 us
    ppermute x2, waiting for transfers between devices, gather(): up_1, down_1 = (lax.ppermute(line, 'col', shift_z(s)) for s in (1, -1))  6.62 us
    ppermute x1, starting transfers between devices, gather(): lax.ppermute(down_1, 'col', shift_z(-1))  5.6 us
  transfers between devices with their start and end apart: 18, of which 8 were waited for; matrix products, arithmetic and copies ran while one was open for 3% of the time, Pallas kernels for 5%

profile of v5, /device:TPU:6, one launch (start us, length us, event | category | flops | bytes accessed | tf_op | source)
XLA Modules:
  0.0 121.6 jit_solution(12122709332484304558)
XLA Ops:
  0.0 0.8 convert_bitcast_fusion
  0.8 0.1 fusion.7
  0.8 0.8 pad_maximum_fusion
  1.7 0.9 broadcast_in_dim.2
  2.6 7.1 %all-to-all-start = ((bf16[8,272,128]{2,1,0:T(8,128)(2,1)}), bf16[8,272,128]{2,1,0:T(8,128)(2,1)S(1)}, u32[]{:S(2)}, u32[]{:S(2)}) async-start(bf16[8,272,128]{2,1,0:T(8,128)(2,1)} %broadcast_in_dim.2), calls=%async_computation | async-start | bytes 1114112 | tf_op jit(solution)/shard_map/all_to_all | solution.py:197
  9.7 0.0 copy-done.11
  9.7 0.1 copy.7
  9.8 0.1 reshape.48
  9.9 0.0 copy-done.10
  9.9 0.1 fusion.1.refs_0_
  10.0 4.2 %collective-permute-start.3 = (bf16[4112,128]{1,0:T(8,128)(2,1)S(1)}, bf16[4112,128]{1,0:T(8,128)(2,1)}, u32[]{:S(2)}, u32[]{:S(2)}) collective-permute-start(bf16[4112,128]{1,0:T(8,128)(2,1)S(1)} %fusion.1.refs_0_), channel_id=1, source_target_pairs={{0,128},{64,192},{128,256},{192,320},{256,384},{320,448},{384,0},{... | collective-permute-start | bytes 3158024 | tf_op jit(solution)/shard_map/ppermute | solution.py:200
  14.2 1.9 %collective-permute-start.2 = (bf16[4112,128]{1,0:T(8,128)(2,1)S(1)}, bf16[4112,128]{1,0:T(8,128)(2,1)}, u32[]{:S(2)}, u32[]{:S(2)}) collective-permute-start(bf16[4112,128]{1,0:T(8,128)(2,1)S(1)} %fusion.1.refs_0_), channel_id=1, source_target_pairs={{0,384},{64,448},{128,0},{192,64},{256,128},{320,192},{384,256},{4... | collective-permute-start | bytes 3158024 | tf_op jit(solution)/shard_map/ppermute | solution.py:199
  16.1 1.9 %collective-permute-start.8 = (bf16[4112,128]{1,0:T(8,128)(2,1)S(1)}, bf16[4112,128]{1,0:T(8,128)(2,1)}, u32[]{:S(2)}, u32[]{:S(2)}) collective-permute-start(bf16[4112,128]{1,0:T(8,128)(2,1)S(1)} %fusion.1.refs_0_), channel_id=1, source_target_pairs={{0,64},{64,0},{128,192},{192,128},{256,320},{320,256},{384,448},{4... | collective-permute-start | bytes 3158024 | tf_op jit(solution)/shard_map/ppermute | solution.py:204
  18.0 9.8 %all-to-all-done.refs_0_ = bf16[8,272,128]{2,1,0:T(8,128)(2,1)S(1)} async-done(((bf16[8,272,128]{2,1,0:T(8,128)(2,1)}), bf16[8,272,128]{2,1,0:T(8,128)(2,1)S(1)}, u32[]{:S(2)}, u32[]{:S(2)}) %all-to-all-start) | async-done | bytes 557088 | tf_op jit(solution)/shard_map/all_to_all | solution.py:197
  27.9 4.3 %collective-permute-start = (bf16[8,272,128]{2,1,0:T(8,128)(2,1)S(1)}, bf16[8,272,128]{2,1,0:T(8,128)(2,1)S(1)}, u32[]{:S(2)}, u32[]{:S(2)}) collective-permute-start(bf16[8,272,128]{2,1,0:T(8,128)(2,1)S(1)} %all-to-all-done.refs_0_), channel_id=1, source_target_pairs={{0,8},{1,9},{2,10},{3,11},{4,12},{5,13},{6,14},{7,15},{8,16},{9,17... | collective-permute-start | bytes 1671176 | tf_op jit(solution)/shard_map/ppermute | solution.py:198
  32.1 8.6 %collective-permute-start.1 = (bf16[8,272,128]{2,1,0:T(8,128)(2,1)S(1)}, bf16[8,272,128]{2,1,0:T(8,128)(2,1)S(1)}, u32[]{:S(2)}, u32[]{:S(2)}) collective-permute-start(bf16[8,272,128]{2,1,0:T(8,128)(2,1)S(1)} %all-to-all-done.refs_0_), channel_id=1, source_target_pairs={{0,56},{1,57},{2,58},{3,59},{4,60},{5,61},{6,62},{7,63},{8,0},{9,1... | collective-permute-start | bytes 1671176 | tf_op jit(solution)/shard_map/ppermute | solution.py:198
  40.7 0.0 collective-permute-done.3.refs_4_
  40.8 1.1 slice.16
  41.8 2.4 %collective-permute-start.13 = (bf16[2048,128]{1,0:T(8,128)(2,1)S(1)}, bf16[2048,128]{1,0:T(8,128)(2,1)}, u32[]{:S(2)}, u32[]{:S(2)}) collective-permute-start(bf16[2048,128]{1,0:T(8,128)(2,1)S(1)} %slice.16), channel_id=1, source_target_pairs={{0,128},{64,192},{128,256},{192,320},{256,384},{320,448},{384,0},{... | collective-permute-start | bytes 1572872 | tf_op jit(solution)/shard_map/ppermute | solution.py:201
  44.2 0.0 collective-permute-done.2.refs_1_
  44.2 1.9 %collective-permute-start.10 = (bf16[4112,128]{1,0:T(8,128)(2,1)}, bf16[4112,128]{1,0:T(8,128)(2,1)S(1)}, u32[]{:S(2)}, u32[]{:S(2)}) collective-permute-start(bf16[4112,128]{1,0:T(8,128)(2,1)} %collective-permute-done.3.refs_4_), channel_id=1, source_target_pairs={{0,64},{64,0},{128,192},{192,128},{256,320},{320,256},{384,448},{4... | collective-permute-start | bytes 3158024 | tf_op jit(solution)/shard_map/ppermute | solution.py:204
  46.2 5.4 %collective-permute-done.refs_1_ = bf16[8,272,128]{2,1,0:T(8,128)(2,1)S(1)} collective-permute-done((bf16[8,272,128]{2,1,0:T(8,128)(2,1)S(1)}, bf16[8,272,128]{2,1,0:T(8,128)(2,1)S(1)}, u32[]{:S(2)}, u32[]{:S(2)}) %collective-permute-start) | collective-permute-done | bytes 557088 | tf_op jit(solution)/shard_map/ppermute | solution.py:198
  51.6 1.2 collective-permute-done.1.refs_2_
  52.8 1.9 %collective-permute-start.4 = (bf16[8,272,128]{2,1,0:T(8,128)(2,1)S(1)}, bf16[8,272,128]{2,1,0:T(8,128)(2,1)S(1)}, u32[]{:S(2)}, u32[]{:S(2)}) collective-permute-start(bf16[8,272,128]{2,1,0:T(8,128)(2,1)S(1)} %collective-permute-done.refs_1_), channel_id=1, source_target_pairs={{0,8},{1,9},{2,10},{3,11},{4,12},{5,13},{6,14},{7,15},{8,16},{9,17... | collective-permute-start | bytes 1671176 | tf_op jit(solution)/shard_map/ppermute | solution.py:206
  54.7 5.6 %collective-permute-start.5 = (bf16[8,272,128]{2,1,0:T(8,128)(2,1)S(1)}, bf16[8,272,128]{2,1,0:T(8,128)(2,1)S(1)}, u32[]{:S(2)}, u32[]{:S(2)}) collective-permute-start(bf16[8,272,128]{2,1,0:T(8,128)(2,1)S(1)} %collective-permute-done.1.refs_2_), channel_id=1, source_target_pairs={{0,56},{1,57},{2,58},{3,59},{4,60},{5,61},{6,62},{7,63},{8,0},{9,1... | collective-permute-start | bytes 1671176 | tf_op jit(solution)/shard_map/ppermute | solution.py:206
  60.3 0.0 collective-permute-done.8.refs_5_
  60.3 1.9 %collective-permute-start.9 = (bf16[4112,128]{1,0:T(8,128)(2,1)}, bf16[4112,128]{1,0:T(8,128)(2,1)S(1)}, u32[]{:S(2)}, u32[]{:S(2)}) collective-permute-start(bf16[4112,128]{1,0:T(8,128)(2,1)} %collective-permute-done.2.refs_1_), channel_id=1, source_target_pairs={{0,64},{64,0},{128,192},{192,128},{256,320},{320,256},{384,448},{4... | collective-permute-start | bytes 3158024 | tf_op jit(solution)/shard_map/ppermute | solution.py:204
  62.3 1.1 slice.17
  63.3 0.0 collective-permute-done.13.refs_2_
  63.3 2.7 %collective-permute-start.14 = (bf16[2064,128]{1,0:T(8,128)(2,1)S(1)}, bf16[2064,128]{1,0:T(8,128)(2,1)}, u32[]{:S(2)}, u32[]{:S(2)}) collective-permute-start(bf16[2064,128]{1,0:T(8,128)(2,1)S(1)} %slice.17), channel_id=1, source_target_pairs={{0,384},{64,448},{128,0},{192,64},{256,128},{320,192},{384,256},{4... | collective-permute-start | bytes 1585160 | tf_op jit(solution)/shard_map/ppermute | solution.py:202
  66.1 4.2 %collective-permute-done.4.refs_3_ = bf16[8,272,128]{2,1,0:T(8,128)(2,1)S(1)} collective-permute-done((bf16[8,272,128]{2,1,0:T(8,128)(2,1)S(1)}, bf16[8,272,128]{2,1,0:T(8,128)(2,1)S(1)}, u32[]{:S(2)}, u32[]{:S(2)}) %collective-permute-start.4) | collective-permute-done | bytes 557088 | tf_op jit(solution)/shard_map/ppermute | solution.py:206
  70.3 1.9 %collective-permute-start.6 = (bf16[8,272,128]{2,1,0:T(8,128)(2,1)S(1)}, bf16[8,272,128]{2,1,0:T(8,128)(2,1)S(1)}, u32[]{:S(2)}, u32[]{:S(2)}) collective-permute-start(bf16[8,272,128]{2,1,0:T(8,128)(2,1)S(1)} %collective-permute-done.4.refs_3_), channel_id=1, source_target_pairs={{0,8},{1,9},{2,10},{3,11},{4,12},{5,13},{6,14},{7,15},{8,16},{9,17... | collective-permute-start | bytes 1671176 | tf_op jit(solution)/shard_map/ppermute | solution.py:207
  72.2 0.0 copy-done
  72.3 0.0 copy-start.2
  72.3 0.8 copy-done.2
  73.1 0.0 collective-permute-done.5.refs_4_
  73.1 5.1 %collective-permute-start.7 = (bf16[8,272,128]{2,1,0:T(8,128)(2,1)S(1)}, bf16[8,272,128]{2,1,0:T(8,128)(2,1)S(1)}, u32[]{:S(2)}, u32[]{:S(2)}) collective-permute-start(bf16[8,272,128]{2,1,0:T(8,128)(2,1)S(1)} %collective-permute-done.5.refs_4_), channel_id=1, source_target_pairs={{0,56},{1,57},{2,58},{3,59},{4,60},{5,61},{6,62},{7,63},{8,0},{9,1... | collective-permute-start | bytes 1671176 | tf_op jit(solution)/shard_map/ppermute | solution.py:207
  78.2 0.0 copy-start.4
  78.2 0.8 copy-done.4
  79.0 1.9 %collective-permute-done.14.refs_3_ = bf16[2064,128]{1,0:T(8,128)(2,1)} collective-permute-done((bf16[2064,128]{1,0:T(8,128)(2,1)S(1)}, bf16[2064,128]{1,0:T(8,128)(2,1)}, u32[]{:S(2)}, u32[]{:S(2)}) %collective-permute-start.14) | collective-permute-done | bytes 528416 | tf_op jit(solution)/shard_map/ppermute | solution.py:202
  81.0 1.9 %collective-permute-start.16 = (bf16[2064,128]{1,0:T(8,128)(2,1)}, bf16[2064,128]{1,0:T(8,128)(2,1)}, u32[]{:S(2)}, u32[]{:S(2)}) collective-permute-start(bf16[2064,128]{1,0:T(8,128)(2,1)} %collective-permute-done.14.refs_3_), channel_id=1, source_target_pairs={{0,64},{64,0},{128,192},{192,128},{256,320},{320,256},{384,448},{4... | collective-permute-start | bytes 1585160 | tf_op jit(solution)/shard_map/ppermute | solution.py:204
  82.9 0.0 collective-permute-done.10.refs_9_
  82.9 0.0 copy-start.6
  82.9 1.0 copy-done.6
  83.9 2.4 %collective-permute-start.15 = (bf16[2048,128]{1,0:T(8,128)(2,1)}, bf16[2048,128]{1,0:T(8,128)(2,1)}, u32[]{:S(2)}, u32[]{:S(2)}) collective-permute-start(bf16[2048,128]{1,0:T(8,128)(2,1)} %collective-permute-done.13.refs_2_), channel_id=1, source_target_pairs={{0,64},{64,0},{128,192},{192,128},{256,320},{320,256},{384,448},{4... | collective-permute-start | bytes 1572872 | tf_op jit(solution)/shard_map/ppermute | solution.py:204
  86.3 0.0 collective-permute-done.9.refs_6_
  86.3 0.0 copy-start.8
  86.3 1.0 copy-done.8
  87.3 0.0 collective-permute-done.6.refs_5_
  87.3 1.2 %collective-permute-done.7.refs_6_ = bf16[8,272,128]{2,1,0:T(8,128)(2,1)S(1)} collective-permute-done((bf16[8,272,128]{2,1,0:T(8,128)(2,1)S(1)}, bf16[8,272,128]{2,1,0:T(8,128)(2,1)S(1)}, u32[]{:S(2)}, u32[]{:S(2)}) %collective-permute-start.7) | collective-permute-done | bytes 557088 | tf_op jit(solution)/shard_map/ppermute | solution.py:207
  88.5 0.8 slice.12
  89.3 1.9 %collective-permute-start.11 = (bf16[4,272,128]{2,1,0:T(8,128)(2,1)}, bf16[4,272,128]{2,1,0:T(8,128)(2,1)}, u32[]{:S(2)}, u32[]{:S(2)}) collective-permute-start(bf16[4,272,128]{2,1,0:T(8,128)(2,1)} %slice.12), channel_id=1, source_target_pairs={{0,8},{1,9},{2,10},{3,11},{4,12},{5,13},{6,14},{7,15},{8,16},{9,17... | collective-permute-start | bytes 835592 | tf_op jit(solution)/shard_map/ppermute | solution.py:210
  91.2 0.7 slice.13
  91.9 5.6 %collective-permute-start.12 = (bf16[4,272,128]{2,1,0:T(8,128)(2,1)}, bf16[4,272,128]{2,1,0:T(8,128)(2,1)}, u32[]{:S(2)}, u32[]{:S(2)}) collective-permute-start(bf16[4,272,128]{2,1,0:T(8,128)(2,1)} %slice.13), channel_id=1, source_target_pairs={{0,56},{1,57},{2,58},{3,59},{4,60},{5,61},{6,62},{7,63},{8,0},{9,1... | collective-permute-start | bytes 835592 | tf_op jit(solution)/shard_map/ppermute | solution.py:211
  97.5 2.5 %collective-permute-done.11.refs_7_ = bf16[4,272,128]{2,1,0:T(8,128)(2,1)} collective-permute-done((bf16[4,272,128]{2,1,0:T(8,128)(2,1)}, bf16[4,272,128]{2,1,0:T(8,128)(2,1)}, u32[]{:S(2)}, u32[]{:S(2)}) %collective-permute-start.11) | collective-permute-done | bytes 278560 | tf_op jit(solution)/shard_map/ppermute | solution.py:210
  100.0 1.9 %collective-permute-done.12.refs_8_ = bf16[4,272,128]{2,1,0:T(8,128)(2,1)} collective-permute-done((bf16[4,272,128]{2,1,0:T(8,128)(2,1)}, bf16[4,272,128]{2,1,0:T(8,128)(2,1)}, u32[]{:S(2)}, u32[]{:S(2)}) %collective-permute-start.12) | collective-permute-done | bytes 278560 | tf_op jit(solution)/shard_map/ppermute | solution.py:211
  101.9 1.1 copy-done.1
  103.0 1.1 copy-done.3
  104.0 1.1 copy-done.5
  105.1 5.5 %shard_map.55 = (bf16[8,128,2048]{2,1,0:T(8,128)(2,1)S(1)}, s32[128]{0:T(128)S(1)}) custom-call(bf16[8,272,128]{2,1,0:T(8,128)(2,1)S(1)} %all-to-all-done.refs_0_, bf16[8,272,128]{2,1,0:T(8,128)(2,1)S(1)} %collective-permute-done.refs_1_, bf16[8,272,128]{2,1,0:T(8,128)(2,1)S(1)} %copy-done.1, bf16[8,272,128]{2,1,0:T(8,128)(2,1)S(1)} %copy-done.3, ...), custom_call_target="tpu_custom_call" | custom-call | bytes 8388608 | tf_op jit(solution)/shard_map/pallas_call | solution.py:80
  110.6 0.0 collective-permute-done.15.refs_7_
  110.6 0.0 collective-permute-done.16.refs_8_
  110.7 0.0 copy-done.7
  110.7 11.0 %shard_map.56 = bf16[1024,1024]{1,0:T(8,128)(2,1)} custom-call(s32[1]{0:T(128)} %bitcast.place, s32[128]{0:T(128)S(1)} %get-tuple-element.15.inner, bf16[8,128,2048]{2,1,0:T(8,128)(2,1)S(1)} %get-tuple-element.16.strips, bf16[4112,128]{1,0:T(8,128)(2,1)S(1)} %fusion.1.refs_0_, bf16[4112,128]{1,0:T(8,128)(2,1)} %collective-permute-done.2.refs_1_, ...), custom_call_target="tpu_custom_call" | custom-call | flops 4294967296 | bytes 14680064 | tf_op jit(solution)/shard_map/pallas_call | solution.py:169
  (10 shorter events, 0.0 us)
Async XLA Ops:
  0.0 9.7 %copy-start.11 = (s32[8,4]{0,1:T(4,128)S(1)}, s32[8,4]{0,1:T(4,128)}, u32[]{:S(2)}) copy-start(s32[8,4]{0,1:T(4,128)} %param.9) | copy-start | bytes 388
  0.0 9.9 %copy-start.10 = (bf16[8,4,128,128]{3,2,1,0:T(8,128)(2,1)S(1)}, bf16[8,4,128,128]{3,2,1,0:T(8,128)(2,1)}, u32[]{:S(2)}) copy-start(bf16[8,4,128,128]{3,2,1,0:T(8,128)(2,1)} %param.8) | copy-start | bytes 3145732
  2.6 25.3 %all-to-all-start = ((bf16[8,272,128]{2,1,0:T(8,128)(2,1)}), bf16[8,272,128]{2,1,0:T(8,128)(2,1)S(1)}, u32[]{:S(2)}, u32[]{:S(2)}) async-start(bf16[8,272,128]{2,1,0:T(8,128)(2,1)} %broadcast_in_dim.2), calls=%async_computation | async-start | bytes 1114112 | tf_op jit(solution)/shard_map/all_to_all | solution.py:197
  10.0 30.8 %collective-permute-start.3 = (bf16[4112,128]{1,0:T(8,128)(2,1)S(1)}, bf16[4112,128]{1,0:T(8,128)(2,1)}, u32[]{:S(2)}, u32[]{:S(2)}) collective-permute-start(bf16[4112,128]{1,0:T(8,128)(2,1)S(1)} %fusion.1.refs_0_), channel_id=1, source_target_pairs={{0,128},{64,192},{128,256},{192,320},{256,384},{320,448},{384,0},{... | collective-permute-start | bytes 3158024 | tf_op jit(solution)/shard_map/ppermute | solution.py:200
  14.2 30.1 %collective-permute-start.2 = (bf16[4112,128]{1,0:T(8,128)(2,1)S(1)}, bf16[4112,128]{1,0:T(8,128)(2,1)}, u32[]{:S(2)}, u32[]{:S(2)}) collective-permute-start(bf16[4112,128]{1,0:T(8,128)(2,1)S(1)} %fusion.1.refs_0_), channel_id=1, source_target_pairs={{0,384},{64,448},{128,0},{192,64},{256,128},{320,192},{384,256},{4... | collective-permute-start | bytes 3158024 | tf_op jit(solution)/shard_map/ppermute | solution.py:199
  16.1 44.2 %collective-permute-start.8 = (bf16[4112,128]{1,0:T(8,128)(2,1)S(1)}, bf16[4112,128]{1,0:T(8,128)(2,1)}, u32[]{:S(2)}, u32[]{:S(2)}) collective-permute-start(bf16[4112,128]{1,0:T(8,128)(2,1)S(1)} %fusion.1.refs_0_), channel_id=1, source_target_pairs={{0,64},{64,0},{128,192},{192,128},{256,320},{320,256},{384,448},{4... | collective-permute-start | bytes 3158024 | tf_op jit(solution)/shard_map/ppermute | solution.py:204
  27.9 23.7 %collective-permute-start = (bf16[8,272,128]{2,1,0:T(8,128)(2,1)S(1)}, bf16[8,272,128]{2,1,0:T(8,128)(2,1)S(1)}, u32[]{:S(2)}, u32[]{:S(2)}) collective-permute-start(bf16[8,272,128]{2,1,0:T(8,128)(2,1)S(1)} %all-to-all-done.refs_0_), channel_id=1, source_target_pairs={{0,8},{1,9},{2,10},{3,11},{4,12},{5,13},{6,14},{7,15},{8,16},{9,17... | collective-permute-start | bytes 1671176 | tf_op jit(solution)/shard_map/ppermute | solution.py:198
  32.1 20.6 %collective-permute-start.1 = (bf16[8,272,128]{2,1,0:T(8,128)(2,1)S(1)}, bf16[8,272,128]{2,1,0:T(8,128)(2,1)S(1)}, u32[]{:S(2)}, u32[]{:S(2)}) collective-permute-start(bf16[8,272,128]{2,1,0:T(8,128)(2,1)S(1)} %all-to-all-done.refs_0_), channel_id=1, source_target_pairs={{0,56},{1,57},{2,58},{3,59},{4,60},{5,61},{6,62},{7,63},{8,0},{9,1... | collective-permute-start | bytes 1671176 | tf_op jit(solution)/shard_map/ppermute | solution.py:198
  41.8 21.5 %collective-permute-start.13 = (bf16[2048,128]{1,0:T(8,128)(2,1)S(1)}, bf16[2048,128]{1,0:T(8,128)(2,1)}, u32[]{:S(2)}, u32[]{:S(2)}) collective-permute-start(bf16[2048,128]{1,0:T(8,128)(2,1)S(1)} %slice.16), channel_id=1, source_target_pairs={{0,128},{64,192},{128,256},{192,320},{256,384},{320,448},{384,0},{... | collective-permute-start | bytes 1572872 | tf_op jit(solution)/shard_map/ppermute | solution.py:201
  44.2 38.7 %collective-permute-start.10 = (bf16[4112,128]{1,0:T(8,128)(2,1)}, bf16[4112,128]{1,0:T(8,128)(2,1)S(1)}, u32[]{:S(2)}, u32[]{:S(2)}) collective-permute-start(bf16[4112,128]{1,0:T(8,128)(2,1)} %collective-permute-done.3.refs_4_), channel_id=1, source_target_pairs={{0,64},{64,0},{128,192},{192,128},{256,320},{320,256},{384,448},{4... | collective-permute-start | bytes 3158024 | tf_op jit(solution)/shard_map/ppermute | solution.py:204
  52.8 19.5 %copy-start = (bf16[8,272,128]{2,1,0:T(8,128)(2,1)}, bf16[8,272,128]{2,1,0:T(8,128)(2,1)S(1)}, u32[]{:S(2)}) copy-start(bf16[8,272,128]{2,1,0:T(8,128)(2,1)S(1)} %collective-permute-done.1.refs_2_) | copy-start | bytes 1671172
  52.8 17.5 %collective-permute-start.4 = (bf16[8,272,128]{2,1,0:T(8,128)(2,1)S(1)}, bf16[8,272,128]{2,1,0:T(8,128)(2,1)S(1)}, u32[]{:S(2)}, u32[]{:S(2)}) collective-permute-start(bf16[8,272,128]{2,1,0:T(8,128)(2,1)S(1)} %collective-permute-done.refs_1_), channel_id=1, source_target_pairs={{0,8},{1,9},{2,10},{3,11},{4,12},{5,13},{6,14},{7,15},{8,16},{9,17... | collective-permute-start | bytes 1671176 | tf_op jit(solution)/shard_map/ppermute | solution.py:206
  54.7 18.4 %collective-permute-start.5 = (bf16[8,272,128]{2,1,0:T(8,128)(2,1)S(1)}, bf16[8,272,128]{2,1,0:T(8,128)(2,1)S(1)}, u32[]{:S(2)}, u32[]{:S(2)}) collective-permute-start(bf16[8,272,128]{2,1,0:T(8,128)(2,1)S(1)} %collective-permute-done.1.refs_2_), channel_id=1, source_target_pairs={{0,56},{1,57},{2,58},{3,59},{4,60},{5,61},{6,62},{7,63},{8,0},{9,1... | collective-permute-start | bytes 1671176 | tf_op jit(solution)/shard_map/ppermute | solution.py:206
  60.3 26.0 %collective-permute-start.9 = (bf16[4112,128]{1,0:T(8,128)(2,1)}, bf16[4112,128]{1,0:T(8,128)(2,1)S(1)}, u32[]{:S(2)}, u32[]{:S(2)}) collective-permute-start(bf16[4112,128]{1,0:T(8,128)(2,1)} %collective-permute-done.2.refs_1_), channel_id=1, source_target_pairs={{0,64},{64,0},{128,192},{192,128},{256,320},{320,256},{384,448},{4... | collective-permute-start | bytes 3158024 | tf_op jit(solution)/shard_map/ppermute | solution.py:204
  63.3 17.6 %collective-permute-start.14 = (bf16[2064,128]{1,0:T(8,128)(2,1)S(1)}, bf16[2064,128]{1,0:T(8,128)(2,1)}, u32[]{:S(2)}, u32[]{:S(2)}) collective-permute-start(bf16[2064,128]{1,0:T(8,128)(2,1)S(1)} %slice.17), channel_id=1, source_target_pairs={{0,384},{64,448},{128,0},{192,64},{256,128},{320,192},{384,256},{4... | collective-permute-start | bytes 1585160 | tf_op jit(solution)/shard_map/ppermute | solution.py:202
  70.3 16.9 %collective-permute-start.6 = (bf16[8,272,128]{2,1,0:T(8,128)(2,1)S(1)}, bf16[8,272,128]{2,1,0:T(8,128)(2,1)S(1)}, u32[]{:S(2)}, u32[]{:S(2)}) collective-permute-start(bf16[8,272,128]{2,1,0:T(8,128)(2,1)S(1)} %collective-permute-done.4.refs_3_), channel_id=1, source_target_pairs={{0,8},{1,9},{2,10},{3,11},{4,12},{5,13},{6,14},{7,15},{8,16},{9,17... | collective-permute-start | bytes 1671176 | tf_op jit(solution)/shard_map/ppermute | solution.py:207
  72.3 0.8 copy-start.2
  73.1 15.4 %collective-permute-start.7 = (bf16[8,272,128]{2,1,0:T(8,128)(2,1)S(1)}, bf16[8,272,128]{2,1,0:T(8,128)(2,1)S(1)}, u32[]{:S(2)}, u32[]{:S(2)}) collective-permute-start(bf16[8,272,128]{2,1,0:T(8,128)(2,1)S(1)} %collective-permute-done.5.refs_4_), channel_id=1, source_target_pairs={{0,56},{1,57},{2,58},{3,59},{4,60},{5,61},{6,62},{7,63},{8,0},{9,1... | collective-permute-start | bytes 1671176 | tf_op jit(solution)/shard_map/ppermute | solution.py:207
  78.2 0.8 copy-start.4
  81.0 29.7 %collective-permute-start.16 = (bf16[2064,128]{1,0:T(8,128)(2,1)}, bf16[2064,128]{1,0:T(8,128)(2,1)}, u32[]{:S(2)}, u32[]{:S(2)}) collective-permute-start(bf16[2064,128]{1,0:T(8,128)(2,1)} %collective-permute-done.14.refs_3_), channel_id=1, source_target_pairs={{0,64},{64,0},{128,192},{192,128},{256,320},{320,256},{384,448},{4... | collective-permute-start | bytes 1585160 | tf_op jit(solution)/shard_map/ppermute | solution.py:204
  82.9 1.0 copy-start.6
  83.9 26.8 %collective-permute-start.15 = (bf16[2048,128]{1,0:T(8,128)(2,1)}, bf16[2048,128]{1,0:T(8,128)(2,1)}, u32[]{:S(2)}, u32[]{:S(2)}) collective-permute-start(bf16[2048,128]{1,0:T(8,128)(2,1)} %collective-permute-done.13.refs_2_), channel_id=1, source_target_pairs={{0,64},{64,0},{128,192},{192,128},{256,320},{320,256},{384,448},{4... | collective-permute-start | bytes 1572872 | tf_op jit(solution)/shard_map/ppermute | solution.py:204
  86.3 1.0 copy-start.8
  89.3 10.8 %collective-permute-start.11 = (bf16[4,272,128]{2,1,0:T(8,128)(2,1)}, bf16[4,272,128]{2,1,0:T(8,128)(2,1)}, u32[]{:S(2)}, u32[]{:S(2)}) collective-permute-start(bf16[4,272,128]{2,1,0:T(8,128)(2,1)} %slice.12), channel_id=1, source_target_pairs={{0,8},{1,9},{2,10},{3,11},{4,12},{5,13},{6,14},{7,15},{8,16},{9,17... | collective-permute-start | bytes 835592 | tf_op jit(solution)/shard_map/ppermute | solution.py:210
  91.9 10.0 %collective-permute-start.12 = (bf16[4,272,128]{2,1,0:T(8,128)(2,1)}, bf16[4,272,128]{2,1,0:T(8,128)(2,1)}, u32[]{:S(2)}, u32[]{:S(2)}) collective-permute-start(bf16[4,272,128]{2,1,0:T(8,128)(2,1)} %slice.13), channel_id=1, source_target_pairs={{0,56},{1,57},{2,58},{3,59},{4,60},{5,61},{6,62},{7,63},{8,0},{9,1... | collective-permute-start | bytes 835592 | tf_op jit(solution)/shard_map/ppermute | solution.py:211
  101.9 1.1 copy-start.1
  103.0 1.1 copy-start.3
  104.0 1.1 copy-start.5
  105.1 5.6 %copy-start.7 = (bf16[4112,128]{1,0:T(8,128)(2,1)S(1)}, bf16[4112,128]{1,0:T(8,128)(2,1)}, u32[]{:S(2)}) copy-start(bf16[4112,128]{1,0:T(8,128)(2,1)} %copy-done.6) | copy-start | bytes 3158020
  105.1 5.6 %copy-start.9 = (bf16[4112,128]{1,0:T(8,128)(2,1)S(1)}, bf16[4112,128]{1,0:T(8,128)(2,1)}, u32[]{:S(2)}) copy-start(bf16[4112,128]{1,0:T(8,128)(2,1)} %copy-done.8) | copy-start | bytes 3158020

commit v6 on v4

v6 whole, which is shorter than its diff:
```python
import jax
import jax.numpy as jnp
from jax import lax
from jax.experimental import pallas as pl
from jax.experimental.pallas import tpu as pltpu
from jax.sharding import PartitionSpec as P

BS = 128
RG = 8
KS = 64
JB = 8
NBR = 4
PER_ROW = 16
N_GRP = 8
N_X = 4
N_Y = 8
N_Z = 8
PAD = 16
OWN_K = 8
R_ROWS = OWN_K * NBR * BS
L_ROWS = 2 * BS
REST = 32
N_LEFT = 128
N_RIGHT = KS * NBR


def shift_x(step):
    return [(x * 2 + c, ((x + step) % N_X) * 2 + c) for x in range(N_X) for c in range(2)]


SWAP_CORES = [(g, g ^ 1) for g in range(2 * N_X)]
Y_LINES = [[z * N_Y + y for y in range(N_Y)] for z in range(N_Z)]
Z_LINES = [[z * N_Y + y for z in range(N_Z)] for y in range(N_Y)]


def arrange_kernel(place, *refs):
    pieces, (right, table, zeros, tiles, values, columns, sem) = refs[:10], refs[10:]
    zeros[...] = jnp.zeros((BS, BS), jnp.bfloat16)
    heads, copies = [], [pltpu.make_async_copy(zeros, right.at[pl.ds(N_RIGHT * BS, BS)], sem.at[10])]
    slot = 0
    for i, piece in enumerate(pieces):
        rows = piece.shape[0]
        blocks = rows // BS
        if rows % BS:
            n = len(heads)
            heads.append(pltpu.make_async_copy(piece.at[pl.ds(rows - PAD, PAD)], tiles.at[n], sem.at[11 + n]))
        copies.append(
            pltpu.make_async_copy(
                piece.at[pl.ds(0, blocks * BS)], right.at[pl.ds(slot * BS, blocks * BS)], sem.at[i]
            )
        )
        slot += blocks
    for copy in heads + copies:
        copy.start()
    for copy in heads:
        copy.wait()
    values[...] = tiles[:, 0, :].astype(jnp.float32).astype(jnp.int32)
    copy = pltpu.make_async_copy(values, columns, sem.at[11])
    copy.start()
    own_x, own_core = place[0] // 2, place[0] % 2

    def clear(i, carry):
        table[i] = N_RIGHT * BS
        return carry

    lax.fori_loop(0, KS * JB, clear, 0, unroll=16)
    copy.wait()

    def fill(k, carry):
        g, i = k // OWN_K, k % OWN_K
        s = ((g + own_core) % 2) * N_X + (g // 2 + N_X - own_x) % N_X
        for m in range(NBR):
            table[k * JB + columns[s, i * NBR + m]] = ((s * OWN_K + i) * NBR + m) * BS
        return carry

    lax.fori_loop(0, KS, fill, 0, unroll=2)
    for copy in copies:
        copy.wait()


def arrange(place, pieces):
    smem = pl.BlockSpec(memory_space=pltpu.SMEM)
    hbm = pl.BlockSpec(memory_space=pl.ANY)
    return pl.pallas_call(
        arrange_kernel,
        out_shape=(
            pltpu.HBM(((N_RIGHT + 1) * BS, BS), jnp.bfloat16),
            jax.ShapeDtypeStruct((KS * JB,), jnp.int32),
        ),
        in_specs=[smem] + [hbm] * len(pieces),
        out_specs=(hbm, smem),
        scratch_shapes=[
            pltpu.VMEM((BS, BS), jnp.bfloat16),
            pltpu.VMEM((N_GRP, PAD, BS), jnp.bfloat16),
            pltpu.VMEM((N_GRP, BS), jnp.int32),
            pltpu.SMEM((N_GRP, BS), jnp.int32),
            pltpu.SemaphoreType.DMA((11 + N_GRP,)),
        ],
        compiler_params=pltpu.CompilerParams(vmem_limit_bytes=4 * 2**20),
        cost_estimate=pl.CostEstimate(flops=2**0, bytes_accessed=16 * 2**20, transcendentals=0),
    )(place, *pieces)


def multiply_kernel(table, right, left, rest, out, held, strips, tiles, values, ids, inner, filled, sem):
    row = pl.program_id(0)

    @pl.when(row == 0)
    def load():
        heads = pltpu.make_async_copy(rest.at[:, :, pl.ds(REST, PAD), :], tiles, sem.at[RG])
        heads.start()
        part = N_RIGHT * BS // 8
        copies = [
            pltpu.make_async_copy(
                right.at[pl.ds(i * part, part)], held.at[pl.ds(i * part, part)], sem.at[RG + 1 + i]
            )
            for i in range(8)
        ]
        for copy in copies:
            copy.start()
        held[pl.ds(N_RIGHT * BS, BS), :] = jnp.zeros((BS, BS), jnp.bfloat16)
        for r in range(RG):
            filled[r] = 0
        heads.wait()
        for y in range(N_Y):
            values[y * N_Z : (y + 1) * N_Z, :] = tiles[y, :, 0, :].astype(jnp.float32).astype(jnp.int32)
        heads = pltpu.make_async_copy(values, ids, sem.at[RG])
        heads.start()
        heads.wait()

        def list_row(n, carry):
            y, z = n // N_Z, n % N_Z
            d = z * N_Y + y
            for b in range(2):
                r = ids[n, b]
                p = filled[r]
                filled[r] = p + 1
                inner[r * PER_ROW + p] = ids[n, 2 + b] * JB
                column = pl.ds(pl.multiple_of(p * BS, BS), BS)
                rows = BS - REST * b
                pltpu.make_async_copy(
                    left.at[d, pl.ds(b * BS, rows), :], strips.at[r, pl.ds(0, rows), column], sem.at[r]
                ).start()
                if b:
                    pltpu.make_async_copy(
                        rest.at[y, z, pl.ds(0, REST), :], strips.at[r, pl.ds(rows, REST), column], sem.at[r]
                    ).start()
            return carry

        lax.fori_loop(0, N_LEFT // 2, list_row, 0, unroll=2)
        for copy in copies:
            copy.wait()

    strip = strips.at[row]
    pltpu.make_async_copy(strip, strip, sem.at[row]).wait()
    ks = [inner[row * PER_ROW + p] for p in range(PER_ROW)]
    for j in range(0, JB, 2):
        rhs = jnp.concatenate(
            [
                jnp.concatenate(
                    [held[pl.ds(pl.multiple_of(table[k + j + h], BS), BS), :] for h in range(2)],
                    axis=1,
                )
                for k in ks
            ],
            axis=0,
        )
        out[:, j * BS : (j + 2) * BS] = jnp.dot(
            strip[...], rhs, preferred_element_type=jnp.float32
        ).astype(out.dtype)


def multiply(table, right, left, rest):
    hbm = pl.BlockSpec(memory_space=pl.ANY)
    devices = left.shape[0]
    return pl.pallas_call(
        multiply_kernel,
        grid=(RG,),
        out_shape=jax.ShapeDtypeStruct((RG * BS, JB * BS), jnp.bfloat16),
        in_specs=[pl.BlockSpec(memory_space=pltpu.SMEM)] + [hbm] * 3,
        out_specs=pl.BlockSpec((BS, JB * BS), lambda r: (r, 0)),
        scratch_shapes=[
            pltpu.VMEM(((N_RIGHT + 1) * BS, BS), jnp.bfloat16),
            pltpu.VMEM((RG, BS, PER_ROW * BS), jnp.bfloat16),
            pltpu.VMEM((N_Y, N_Z, PAD, BS), jnp.bfloat16),
            pltpu.VMEM((devices, BS), jnp.int32),
            pltpu.SMEM((devices, BS), jnp.int32),
            pltpu.SMEM((N_LEFT,), jnp.int32),
            pltpu.SMEM((RG,), jnp.int32),
            pltpu.SemaphoreType.DMA((RG + 9,)),
        ],
        compiler_params=pltpu.CompilerParams(vmem_limit_bytes=24 * 2**20),
        cost_estimate=pl.CostEstimate(flops=4 * 2**30, bytes_accessed=14 * 2**20, transcendentals=0),
    )(table, *(pltpu.with_memory_space_constraint(v, pltpu.HBM) for v in [right, left, rest]))


def tail(values):
    flat = values.astype(jnp.bfloat16).reshape(1, -1)
    return jnp.pad(flat, ((0, PAD - 1), (0, BS - flat.shape[1])))


def gather_right(own):
    after = lax.ppermute(own, "grp", shift_x(-1))
    before = lax.ppermute(own, "grp", shift_x(1))
    far_head = lax.ppermute(before[: R_ROWS // 2], "grp", shift_x(1))
    far_tail = lax.ppermute(after[R_ROWS // 2 :], "grp", shift_x(-1))
    mine = [own, after, far_head, far_tail, before]
    return mine + [lax.ppermute(v, "grp", SWAP_CORES) for v in mine]


def spread(own, lines):
    copies = jnp.broadcast_to(own[None], (len(lines[0]),) + own.shape)
    return lax.all_to_all(copies, "col", 0, 0, axis_index_groups=lines)


def body(panel_blocks, panel_rows, panel_inner, right_blocks, right_columns):
    right = jnp.concatenate([right_blocks.reshape(R_ROWS, BS), tail(right_columns)])
    left = panel_blocks.reshape(L_ROWS, BS)
    line = spread(left[: L_ROWS - REST], Y_LINES)
    lefts = lax.all_gather(line, "col", axis=0, tiled=True, axis_index_groups=Z_LINES)
    rest = jnp.concatenate([left[L_ROWS - REST :], tail(jnp.concatenate([panel_rows, panel_inner]))])
    rest = lax.optimization_barrier((rest, line))[0]
    rest = spread(spread(rest, Z_LINES), Y_LINES)
    place = lax.axis_index("grp").reshape(1)
    rights, table = arrange(place, gather_right(right))
    return multiply(table, rights, lefts, rest)


def solution(mesh):
    placed = (
        P(("grp", "col"), None, None),
        P(("grp", "col")),
        P(("grp", "col")),
        P("grp", "col", None, None),
        P("grp", "col"),
    )
    return jax.shard_map(
        body, mesh=mesh, in_specs=placed, out_specs=P("grp", "col"), check_vma=False
    )
```

time: 114 us -> 278 us (2.44); the launches traced: 113 us -> 273 us
  Pallas kernels: 12.3 us -> 173 us
  waiting for transfers between devices: 36.8 us -> 11.9 us
  blocking collectives: 25.3 us -> 43 us
  starting transfers between devices: 21.3 us -> 28.6 us
    pallas_call x0 -> x1, Pallas kernels: none -> 161 us  [arrange(): pl.pallas_call(arrange_kernel, out_shape=(pltpu.HBM(((N_RIGHT + 1) * BS,...]
    all_to_all x1 -> x2, blocking collectives: 25.3 us -> 43 us  [spread(): return lax.all_to_all(copies, 'col', 0, 0, axis_index_groups=lines)]
    ppermute x1, waiting for transfers between devices: 17.1 us -> 0.01 us  [gather_right(): before = lax.ppermute(own, 'grp', shift_x(1))]
    all_gather x1, waiting for transfers between devices: 8.31 us -> 0.02 us  [body(): lax.all_gather(line, 'col', axis=0, tiled=True, axis_index_groups=Z_LINES)]
    all_to_all x0 -> x1, starting transfers between devices: none -> 4.22 us  [spread(): return lax.all_to_all(copies, 'col', 0, 0, axis_index_groups=lines)]
  transfers between devices with their start and end apart: 10 -> 11, of which waited for: 5 -> 2; matrix products, arithmetic and copies ran while one was open for 2% -> 1% of each run, Pallas kernels for 0% -> 59%
where the time goes in v6:
time: 278 us; the launch traced here: 273 us
  Pallas kernels  173 us (62%)
  blocking collectives  43 us (15%)
  starting transfers between devices  28.6 us (10%)
  between operations  13.6 us (5%)
  waiting for transfers between devices  11.9 us (4%)
  local copies, waits for them, and re-layouts  2.95 us (1%)
    pallas_call x1, Pallas kernels, arrange(): pl.pallas_call(arrange_kernel, out_shape=(pltpu.HBM(((N_RIGHT + 1) * BS,...  161 us
    all_to_all x2, blocking collectives, spread(): return lax.all_to_all(copies, 'col', 0, 0, axis_index_groups=lines)  43 us
    pallas_call x1, Pallas kernels, multiply(): pl.pallas_call(multiply_kernel, grid=(RG,), out_shape=jax.ShapeDtypeStruc...  12.2 us
    ppermute x5, starting transfers between devices, gather_right(): return mine + [lax.ppermute(v, 'grp', SWAP_CORES) for v in mine]  10.3 us
    ppermute x1, waiting for transfers between devices, gather_right(): far_head = lax.ppermute(before[:R_ROWS // 2], 'grp', shift_x(1))  9.68 us
  transfers between devices with their start and end apart: 11, of which 2 were waited for; matrix products, arithmetic and copies ran while one was open for 1% of the time, Pallas kernels for 59%

profile of v6, /device:TPU:6, one launch (start us, length us, event | category | flops | bytes accessed | tf_op | source)
XLA Modules:
  0.0 273.2 jit_solution(4406678614504302344)
XLA Ops:
  6.5 0.0 copy-start.1
  6.5 0.0 copy-start
  6.5 0.0 all-gather.2.cloned.1.call-start
  6.5 0.9 slice.18
  7.5 0.1 broadcast_in_dim.6
  7.5 23.1 %all_to_all.15 = bf16[8,224,128]{2,1,0:T(8,128)(2,1)} all-to-all(bf16[8,224,128]{2,1,0:T(8,128)(2,1)S(1)} %broadcast_in_dim.6), channel_id=1, replica_groups={{0,1,2,3,4,5,6,7},{8,9,10,11,12,13,14,15},{16,17,18,19,20,21,22,23},{24..., dimensions={0} | all-to-all | bytes 917504 | tf_op jit(solution)/shard_map/all_to_all | solution.py:212
  30.6 0.0 all-gather.2.cloned.1.call-update
  30.6 0.0 copy-done.1
  30.7 0.1 copy.8
  30.8 0.1 reshape.49
  30.8 0.0 copy-done
  30.8 0.0 copy-start.2
  30.9 0.0 copy-start.3
  30.9 0.1 fusion.1.refs_0_
  30.9 2.7 %collective-permute-start = (bf16[4112,128]{1,0:T(8,128)(2,1)S(1)}, bf16[4112,128]{1,0:T(8,128)(2,1)S(1)}, u32[]{:S(2)}, u32[]{:S(2)}) collective-permute-start(bf16[4112,128]{1,0:T(8,128)(2,1)S(1)} %fusion.1.refs_0_), channel_id=1, source_target_pairs={{0,384},{64,448},{128,0},{192,64},{256,128},{320,192},{384,256},{4... | collective-permute-start | bytes 3158024 | tf_op jit(solution)/shard_map/ppermute | solution.py:202
  33.7 4.3 %collective-permute-start.1 = (bf16[4112,128]{1,0:T(8,128)(2,1)S(1)}, bf16[4112,128]{1,0:T(8,128)(2,1)S(1)}, u32[]{:S(2)}, u32[]{:S(2)}) collective-permute-start(bf16[4112,128]{1,0:T(8,128)(2,1)S(1)} %fusion.1.refs_0_), channel_id=1, source_target_pairs={{0,128},{64,192},{128,256},{192,320},{256,384},{320,448},{384,0},{... | collective-permute-start | bytes 3158024 | tf_op jit(solution)/shard_map/ppermute | solution.py:203
  38.0 0.7 slice.19
  38.7 0.0 copy-done.2
  38.7 0.0 copy-done.3
  38.7 0.1 fusion.7
  38.8 19.9 %all_to_all.16 = bf16[8,48,128]{2,1,0:T(8,128)(2,1)S(1)} all-to-all(bf16[8,48,128]{2,1,0:T(8,128)(2,1)S(1)} %broadcast_in_dim.7), channel_id=1, replica_groups={{0,8,16,24,32,40,48,56},{1,9,17,25,33,41,49,57},{2,10,18,26,34,42,50,58..., dimensions={0} | all-to-all | bytes 196608 | tf_op jit(solution)/shard_map/all_to_all | solution.py:212
  58.7 1.0 broadcast_in_dim.8
  59.7 4.2 %all-to-all-start.2 = ((bf16[8,8,48,128]{3,2,1,0:T(8,128)(2,1)}), bf16[8,8,48,128]{3,2,1,0:T(8,128)(2,1)}, u32[]{:S(2)}, u32[]{:S(2)}) async-start(bf16[8,8,48,128]{3,2,1,0:T(8,128)(2,1)} %broadcast_in_dim.8), calls=%async_computation.2 | async-start | bytes 1572864 | tf_op jit(solution)/shard_map/all_to_all | solution.py:212
  63.9 0.0 collective-permute-done.refs_1_
  64.0 1.9 collective-permute-start.3
  65.9 1.9 collective-permute-start.4
  67.8 2.4 collective-permute-start.5
  70.2 0.0 collective-permute-done.1.refs_4_
  70.3 1.9 collective-permute-start.8
  72.2 5.1 %collective-permute-start.2 = (bf16[2048,128]{1,0:T(8,128)(2,1)S(1)}, bf16[2048,128]{1,0:T(8,128)(2,1)}, u32[]{:S(2)}, u32[]{:S(2)}) collective-permute-start(bf16[2048,128]{1,0:T(8,128)(2,1)S(1)} %slice.16), channel_id=1, source_target_pairs={{0,128},{64,192},{128,256},{192,320},{256,384},{320,448},{384,0},{... | collective-permute-start | bytes 1572872 | tf_op jit(solution)/shard_map/ppermute | solution.py:204
  77.4 0.0 collective-permute-done.3.refs_3_
  77.4 2.1 collective-permute-start.7
  79.5 9.7 %collective-permute-done.2.refs_2_ = bf16[2048,128]{1,0:T(8,128)(2,1)} collective-permute-done((bf16[2048,128]{1,0:T(8,128)(2,1)S(1)}, bf16[2048,128]{1,0:T(8,128)(2,1)}, u32[]{:S(2)}, u32[]{:S(2)}) %collective-permute-start.2) | collective-permute-done | bytes 524320 | tf_op jit(solution)/shard_map/ppermute | solution.py:204
  89.2 1.9 collective-permute-start.6
  91.1 0.0 collective-permute-done.4.refs_5_
  91.1 2.2 collective-permute-done.6.refs_7_
  93.3 0.0 collective-permute-done.5.refs_6_
  93.3 0.0 collective-permute-done.8.refs_9_
  93.3 0.0 collective-permute-done.7.refs_8_
  93.3 160.7 %shard_map.55 = (bf16[32896,128]{1,0:T(8,128)(2,1)}, s32[512]{0:T(512)S(1)}) custom-call(s32[1]{0:T(128)} %bitcast.place, bf16[4112,128]{1,0:T(8,128)(2,1)S(1)} %fusion.1.refs_0_, bf16[4112,128]{1,0:T(8,128)(2,1)S(1)} %collective-permute-done.refs_1_, bf16[2048,128]{1,0:T(8,128)(2,1)} %collective-permute-done.2.refs_2_, ...), custom_call_target="tpu_custom_call" | custom-call | flops 1 | bytes 16777216 | tf_op jit(solution)/shard_map/pallas_call | solution.py:84
  254.1 0.0 all-to-all-done.2.rest
  254.1 0.0 all-gather.2.cloned.1.call-done.left
  254.1 12.2 %shard_map.56 = bf16[1024,1024]{1,0:T(8,128)(2,1)} custom-call(s32[512]{0:T(512)S(1)} %get-tuple-element.8.table, bf16[32896,128]{1,0:T(8,128)(2,1)} %get-tuple-element.9.right, bf16[64,224,128]{2,1,0:T(8,128)(2,1)} %all-gather.2.cloned.1.call-done.left, bf16[8,8,48,128]{3,2,1,0:T(8,128)(2,1)} %all-to-all-done.2.rest), custom_call_target="tpu_custom_call" | custom-call | flops 4294967296 | bytes 14680064 | tf_op jit(solution)/shard_map/pallas_call | solution.py:175
  (6 shorter events, 0.1 us)
Async XLA Ops:
  6.5 24.1 %copy-start.1 = (s32[8,4]{0,1:T(4,128)S(1)}, s32[8,4]{0,1:T(4,128)}, u32[]{:S(2)}) copy-start(s32[8,4]{0,1:T(4,128)} %param.9) | copy-start | bytes 388
  6.5 24.3 %copy-start = (bf16[8,4,128,128]{3,2,1,0:T(8,128)(2,1)S(1)}, bf16[8,4,128,128]{3,2,1,0:T(8,128)(2,1)}, u32[]{:S(2)}) copy-start(bf16[8,4,128,128]{3,2,1,0:T(8,128)(2,1)} %param.8) | copy-start | bytes 3145732
  6.5 247.6 %all-gather.2.cloned.1.call-start = ((), (), s32[]{:S(2)}) async-start(), calls=%async_computation.3 | async-start | bytes 4128768 | tf_op jit(solution)/shard_map/all_gather | solution.py:219
  30.8 7.9 %copy-start.2 = (s32[2]{0:T(128)S(1)}, s32[2]{0:T(128)}, u32[]{:S(2)}) copy-start(s32[2]{0:T(128)} %param.7) | copy-start | bytes 28
  30.9 7.9 %copy-start.3 = (s32[2]{0:T(128)S(1)}, s32[2]{0:T(128)}, u32[]{:S(2)}) copy-start(s32[2]{0:T(128)} %param.6) | copy-start | bytes 28
  30.9 33.0 %collective-permute-start = (bf16[4112,128]{1,0:T(8,128)(2,1)S(1)}, bf16[4112,128]{1,0:T(8,128)(2,1)S(1)}, u32[]{:S(2)}, u32[]{:S(2)}) collective-permute-start(bf16[4112,128]{1,0:T(8,128)(2,1)S(1)} %fusion.1.refs_0_), channel_id=1, source_target_pairs={{0,384},{64,448},{128,0},{192,64},{256,128},{320,192},{384,256},{4... | collective-permute-start | bytes 3158024 | tf_op jit(solution)/shard_map/ppermute | solution.py:202
  33.7 36.6 %collective-permute-start.1 = (bf16[4112,128]{1,0:T(8,128)(2,1)S(1)}, bf16[4112,128]{1,0:T(8,128)(2,1)S(1)}, u32[]{:S(2)}, u32[]{:S(2)}) collective-permute-start(bf16[4112,128]{1,0:T(8,128)(2,1)S(1)} %fusion.1.refs_0_), channel_id=1, source_target_pairs={{0,128},{64,192},{128,256},{192,320},{256,384},{320,448},{384,0},{... | collective-permute-start | bytes 3158024 | tf_op jit(solution)/shard_map/ppermute | solution.py:203
  59.7 194.4 %all-to-all-start.2 = ((bf16[8,8,48,128]{3,2,1,0:T(8,128)(2,1)}), bf16[8,8,48,128]{3,2,1,0:T(8,128)(2,1)}, u32[]{:S(2)}, u32[]{:S(2)}) async-start(bf16[8,8,48,128]{3,2,1,0:T(8,128)(2,1)} %broadcast_in_dim.8), calls=%async_computation.2 | async-start | bytes 1572864 | tf_op jit(solution)/shard_map/all_to_all | solution.py:212
  64.0 13.4 %collective-permute-start.3 = (bf16[2064,128]{1,0:T(8,128)(2,1)S(1)}, bf16[2064,128]{1,0:T(8,128)(2,1)}, u32[]{:S(2)}, u32[]{:S(2)}) collective-permute-start(bf16[2064,128]{1,0:T(8,128)(2,1)S(1)} %slice.17), channel_id=1, source_target_pairs={{0,384},{64,448},{128,0},{192,64},{256,128},{320,192},{384,256},{4... | collective-permute-start | bytes 1585160 | tf_op jit(solution)/shard_map/ppermute | solution.py:205
  65.9 25.2 %collective-permute-start.4 = (bf16[4112,128]{1,0:T(8,128)(2,1)S(1)}, bf16[4112,128]{1,0:T(8,128)(2,1)}, u32[]{:S(2)}, u32[]{:S(2)}) collective-permute-start(bf16[4112,128]{1,0:T(8,128)(2,1)S(1)} %fusion.1.refs_0_), channel_id=1, source_target_pairs={{0,64},{64,0},{128,192},{192,128},{256,320},{320,256},{384,448},{4... | collective-permute-start | bytes 3158024 | tf_op jit(solution)/shard_map/ppermute | solution.py:207
  67.8 25.5 %collective-permute-start.5 = (bf16[4112,128]{1,0:T(8,128)(2,1)S(1)}, bf16[4112,128]{1,0:T(8,128)(2,1)}, u32[]{:S(2)}, u32[]{:S(2)}) collective-permute-start(bf16[4112,128]{1,0:T(8,128)(2,1)S(1)} %collective-permute-done.refs_1_), channel_id=1, source_target_pairs={{0,64},{64,0},{128,192},{192,128},{256,320},{320,256},{384,448},{4... | collective-permute-start | bytes 3158024 | tf_op jit(solution)/shard_map/ppermute | solution.py:207
  70.3 23.1 %collective-permute-start.8 = (bf16[4112,128]{1,0:T(8,128)(2,1)S(1)}, bf16[4112,128]{1,0:T(8,128)(2,1)}, u32[]{:S(2)}, u32[]{:S(2)}) collective-permute-start(bf16[4112,128]{1,0:T(8,128)(2,1)S(1)} %collective-permute-done.1.refs_4_), channel_id=1, source_target_pairs={{0,64},{64,0},{128,192},{192,128},{256,320},{320,256},{384,448},{4... | collective-permute-start | bytes 3158024 | tf_op jit(solution)/shard_map/ppermute | solution.py:207
  72.2 17.0 %collective-permute-start.2 = (bf16[2048,128]{1,0:T(8,128)(2,1)S(1)}, bf16[2048,128]{1,0:T(8,128)(2,1)}, u32[]{:S(2)}, u32[]{:S(2)}) collective-permute-start(bf16[2048,128]{1,0:T(8,128)(2,1)S(1)} %slice.16), channel_id=1, source_target_pairs={{0,128},{64,192},{128,256},{192,320},{256,384},{320,448},{384,0},{... | collective-permute-start | bytes 1572872 | tf_op jit(solution)/shard_map/ppermute | solution.py:204
  77.4 16.0 %collective-permute-start.7 = (bf16[2064,128]{1,0:T(8,128)(2,1)}, bf16[2064,128]{1,0:T(8,128)(2,1)}, u32[]{:S(2)}, u32[]{:S(2)}) collective-permute-start(bf16[2064,128]{1,0:T(8,128)(2,1)} %collective-permute-done.3.refs_3_), channel_id=1, source_target_pairs={{0,64},{64,0},{128,192},{192,128},{256,320},{320,256},{384,448},{4... | collective-permute-start | bytes 1585160 | tf_op jit(solution)/shard_map/ppermute | solution.py:207
  89.2 4.1 %collective-permute-start.6 = (bf16[2048,128]{1,0:T(8,128)(2,1)}, bf16[2048,128]{1,0:T(8,128)(2,1)}, u32[]{:S(2)}, u32[]{:S(2)}) collective-permute-start(bf16[2048,128]{1,0:T(8,128)(2,1)} %collective-permute-done.2.refs_2_), channel_id=1, source_target_pairs={{0,64},{64,0},{128,192},{192,128},{256,320},{320,256},{384,448},{4... | collective-permute-start | bytes 1572872 | tf_op jit(solution)/shard_map/ppermute | solution.py:207
Sparse Core Ops, SparseCore 0:
  30.8 54.7 all-gather.1

commit v7 on v6

v7 whole, which is shorter than its diff:
```python
import jax
import jax.numpy as jnp
from jax import lax
from jax.experimental import pallas as pl
from jax.experimental.pallas import tpu as pltpu
from jax.sharding import PartitionSpec as P

BS = 128
RG = 8
KS = 64
JB = 8
NBR = 4
PER_ROW = 16
N_GRP = 8
N_X = 4
N_Y = 8
N_Z = 8
PAD = 16
OWN_K = 8
R_ROWS = OWN_K * NBR * BS
L_ROWS = 2 * BS
REST = 32
N_LEFT = 128
N_RIGHT = KS * NBR


def shift_x(step):
    return [(x * 2 + c, ((x + step) % N_X) * 2 + c) for x in range(N_X) for c in range(2)]


SWAP_CORES = [(g, g ^ 1) for g in range(2 * N_X)]
Y_LINES = [[z * N_Y + y for y in range(N_Y)] for z in range(N_Z)]
Z_LINES = [[z * N_Y + y for z in range(N_Z)] for y in range(N_Y)]


def table_kernel(place, *refs):
    pieces, (table, tiles, values, columns, sem) = refs[:10], refs[10:]
    pieces = [piece for piece in pieces if piece.shape[0] % BS]
    heads = [
        pltpu.make_async_copy(piece.at[pl.ds(piece.shape[0] - PAD, PAD)], tiles.at[n], sem.at[n])
        for n, piece in enumerate(pieces)
    ]
    for copy in heads:
        copy.start()
    for copy in heads:
        copy.wait()
    values[...] = tiles[:, 0, :].astype(jnp.float32).astype(jnp.int32)
    copy = pltpu.make_async_copy(values, columns, sem.at[0])
    copy.start()
    own_x, own_core = place[0] // 2, place[0] % 2

    def clear(i, carry):
        table[i] = N_RIGHT * BS
        return carry

    lax.fori_loop(0, KS * JB, clear, 0, unroll=16)
    copy.wait()

    def fill(k, carry):
        g, i = k // OWN_K, k % OWN_K
        s = ((g + own_core) % 2) * N_X + (g // 2 + N_X - own_x) % N_X
        for m in range(NBR):
            table[k * JB + columns[s, i * NBR + m]] = ((s * OWN_K + i) * NBR + m) * BS
        return carry

    lax.fori_loop(0, KS, fill, 0, unroll=2)


def make_table(place, pieces):
    smem = pl.BlockSpec(memory_space=pltpu.SMEM)
    hbm = pl.BlockSpec(memory_space=pl.ANY)
    return pl.pallas_call(
        table_kernel,
        out_shape=jax.ShapeDtypeStruct((KS * JB,), jnp.int32),
        in_specs=[smem] + [hbm] * len(pieces),
        out_specs=smem,
        scratch_shapes=[
            pltpu.VMEM((N_GRP, PAD, BS), jnp.bfloat16),
            pltpu.VMEM((N_GRP, BS), jnp.int32),
            pltpu.SMEM((N_GRP, BS), jnp.int32),
            pltpu.SemaphoreType.DMA((N_GRP,)),
        ],
        compiler_params=pltpu.CompilerParams(vmem_limit_bytes=2 * 2**20),
        cost_estimate=pl.CostEstimate(flops=48 * 2**30, bytes_accessed=2**20, transcendentals=0),
    )(place, *pieces)


def list_kernel(rest, spots, inner, tiles, values, ids, filled, sem):
    copy = pltpu.make_async_copy(rest.at[:, :, pl.ds(REST, PAD), :], tiles, sem.at[0])
    copy.start()
    for r in range(RG):
        filled[r] = 0
    copy.wait()
    for y in range(N_Y):
        values[y * N_Z : (y + 1) * N_Z, :] = tiles[y, :, 0, :].astype(jnp.float32).astype(jnp.int32)
    copy = pltpu.make_async_copy(values, ids, sem.at[0])
    copy.start()
    copy.wait()

    def list_row(n, carry):
        for b in range(2):
            r = ids[n, b]
            p = filled[r]
            filled[r] = p + 1
            spots[2 * n + b] = r * PER_ROW + p
            inner[r * PER_ROW + p] = ids[n, 2 + b] * JB
        return carry

    lax.fori_loop(0, N_LEFT // 2, list_row, 0, unroll=2)


def make_lists(rest):
    smem = pl.BlockSpec(memory_space=pltpu.SMEM)
    devices = N_Y * N_Z
    return pl.pallas_call(
        list_kernel,
        out_shape=[jax.ShapeDtypeStruct((N_LEFT,), jnp.int32)] * 2,
        in_specs=[pl.BlockSpec(memory_space=pl.ANY)],
        out_specs=[smem] * 2,
        scratch_shapes=[
            pltpu.VMEM((N_Y, N_Z, PAD, BS), jnp.bfloat16),
            pltpu.VMEM((devices, BS), jnp.int32),
            pltpu.SMEM((devices, BS), jnp.int32),
            pltpu.SMEM((RG,), jnp.int32),
            pltpu.SemaphoreType.DMA((1,)),
        ],
        compiler_params=pltpu.CompilerParams(vmem_limit_bytes=2 * 2**20),
        cost_estimate=pl.CostEstimate(flops=0 * 2**30, bytes_accessed=2**20, transcendentals=0),
    )(rest)


def multiply_kernel(table, spots, inner, left, rest, *refs):
    pieces, (out, held, strips, sem) = refs[:10], refs[10:]
    row = pl.program_id(0)

    @pl.when(row == 0)
    def load():
        copies = []
        slot = 0
        for i, piece in enumerate(pieces):
            blocks = piece.shape[0] // BS
            copies.append(
                pltpu.make_async_copy(
                    piece.at[pl.ds(0, blocks * BS)],
                    held.at[pl.ds(slot * BS, blocks * BS)],
                    sem.at[RG + i],
                )
            )
            slot += blocks
        for copy in copies:
            copy.start()
        held[pl.ds(N_RIGHT * BS, BS), :] = jnp.zeros((BS, BS), jnp.bfloat16)

        def list_row(n, carry):
            y, z = n // N_Z, n % N_Z
            d = z * N_Y + y
            for b in range(2):
                r, p = spots[2 * n + b] // PER_ROW, spots[2 * n + b] % PER_ROW
                column = pl.ds(pl.multiple_of(p * BS, BS), BS)
                rows = BS - REST * b
                pltpu.make_async_copy(
                    left.at[d, pl.ds(b * BS, rows), :], strips.at[r, pl.ds(0, rows), column], sem.at[r]
                ).start()
                if b:
                    pltpu.make_async_copy(
                        rest.at[y, z, pl.ds(0, REST), :], strips.at[r, pl.ds(rows, REST), column], sem.at[r]
                    ).start()
            return carry

        lax.fori_loop(0, N_LEFT // 2, list_row, 0, unroll=2)
        for copy in copies:
            copy.wait()

    strip = strips.at[row]
    pltpu.make_async_copy(strip, strip, sem.at[row]).wait()
    ks = [inner[row * PER_ROW + p] for p in range(PER_ROW)]
    for j in range(0, JB, 2):
        rhs = jnp.concatenate(
            [
                jnp.concatenate(
                    [held[pl.ds(pl.multiple_of(table[k + j + h], BS), BS), :] for h in range(2)],
                    axis=1,
                )
                for k in ks
            ],
            axis=0,
        )
        out[:, j * BS : (j + 2) * BS] = jnp.dot(
            strip[...], rhs, preferred_element_type=jnp.float32
        ).astype(out.dtype)


def multiply(table, lists, left, rest, pieces):
    hbm = pl.BlockSpec(memory_space=pl.ANY)
    return pl.pallas_call(
        multiply_kernel,
        grid=(RG,),
        out_shape=jax.ShapeDtypeStruct((RG * BS, JB * BS), jnp.bfloat16),
        in_specs=[pl.BlockSpec(memory_space=pltpu.SMEM)] * 3 + [hbm] * (2 + len(pieces)),
        out_specs=pl.BlockSpec((BS, JB * BS), lambda r: (r, 0)),
        scratch_shapes=[
            pltpu.VMEM(((N_RIGHT + 1) * BS, BS), jnp.bfloat16),
            pltpu.VMEM((RG, BS, PER_ROW * BS), jnp.bfloat16),
            pltpu.SemaphoreType.DMA((RG + len(pieces),)),
        ],
        compiler_params=pltpu.CompilerParams(vmem_limit_bytes=24 * 2**20),
        cost_estimate=pl.CostEstimate(flops=4 * 2**30, bytes_accessed=14 * 2**20, transcendentals=0),
    )(table, *lists, *(pltpu.with_memory_space_constraint(v, pltpu.HBM) for v in [left, rest, *pieces]))


def tail(values):
    flat = values.astype(jnp.bfloat16).reshape(1, -1)
    return jnp.pad(flat, ((0, PAD - 1), (0, BS - flat.shape[1])))


def gather_right(own, first, second):
    after = lax.ppermute(own, "grp", shift_x(-1))
    before = lax.ppermute(own, "grp", shift_x(1))
    onward, back = lax.optimization_barrier((before, after, first))[:2]
    far_head = lax.ppermute(onward[: R_ROWS // 2], "grp", shift_x(1))
    far_tail = lax.ppermute(back[R_ROWS // 2 :], "grp", shift_x(-1))
    mine = [own, after, far_head, far_tail, before]
    far_head, far_tail = lax.optimization_barrier((far_head, far_tail, second))[:2]
    others = [own, after, far_head, far_tail, before]
    return mine + [lax.ppermute(v, "grp", SWAP_CORES) for v in others]


def spread(own, lines):
    copies = jnp.broadcast_to(own[None], (len(lines[0]),) + own.shape)
    return lax.all_to_all(copies, "col", 0, 0, axis_index_groups=lines)


def body(panel_blocks, panel_rows, panel_inner, right_blocks, right_columns):
    right = jnp.concatenate([right_blocks.reshape(R_ROWS, BS), tail(right_columns)])
    left = panel_blocks.reshape(L_ROWS, BS)
    line = spread(left[: L_ROWS - REST], Y_LINES)
    lefts = lax.all_gather(line, "col", axis=0, tiled=True, axis_index_groups=Z_LINES)
    rest = jnp.concatenate([left[L_ROWS - REST :], tail(jnp.concatenate([panel_rows, panel_inner]))])
    rest = lax.optimization_barrier((rest, line))[0]
    strip = spread(rest, Z_LINES)
    rest = spread(strip, Y_LINES)
    pieces = gather_right(right, strip, rest)
    place = lax.axis_index("grp").reshape(1)
    table = make_table(place, pieces)
    return multiply(table, make_lists(rest), lefts, rest, pieces)


def solution(mesh):
    placed = (
        P(("grp", "col"), None, None),
        P(("grp", "col")),
        P(("grp", "col")),
        P("grp", "col", None, None),
        P("grp", "col"),
    )
    return jax.shard_map(
        body, mesh=mesh, in_specs=placed, out_specs=P("grp", "col"), check_vma=False
    )
```

time: 278 us -> 128 us (0.46); the launches traced: 273 us -> 126 us
  Pallas kernels: 173 us -> 18.9 us
  blocking collectives: 43 us -> 18.8 us
  waiting for transfers between devices: 11.9 us -> 33.8 us
  starting transfers between devices: 28.6 us -> 34.4 us
  local copies, waits for them, and re-layouts: 2.95 us -> 6.62 us
    pallas_call x1 -> x2, Pallas kernels: 161 us -> 6.61 us  [the longest x1 4.1 us: make_table(): pl.pallas_call(table_kernel, out_shape=jax.ShapeDtypeStruct((KS * JB,), j...]
    all_to_all x2 -> x1, blocking collectives: 43 us -> 18.8 us  [spread(): return lax.all_to_all(copies, 'col', 0, 0, axis_index_groups=lines)]
    all_gather x1, waiting for transfers between devices: 0.02 us -> 18.4 us  [body(): lax.all_gather(line, 'col', axis=0, tiled=True, axis_index_groups=Z_LINES)]
    all_to_all x1 -> x2, waiting for transfers between devices: 0.01 us -> 11.5 us  [spread(): return lax.all_to_all(copies, 'col', 0, 0, axis_index_groups=lines)]
    ppermute x7, waiting for transfers between devices: 11.9 us -> 3.26 us  [the longest x1 3.25 us: gather_right(): far_head = lax.ppermute(onward[:R_ROWS // 2], 'grp', shift_x(1))]
    all_to_all x1 -> x2, starting transfers between devices: 4.22 us -> 10.6 us  [spread(): return lax.all_to_all(copies, 'col', 0, 0, axis_index_groups=lines)]
  transfers between devices with their start and end apart: 11 -> 12, of which waited for: 2 -> 4; matrix products, arithmetic and copies ran while one was open for 1% -> 2% of each run, Pallas kernels for 59% -> 5%
where the time goes in v7:
time: 128 us; the launch traced here: 126 us
  starting transfers between devices  34.4 us (27%)
  waiting for transfers between devices  33.8 us (26%)
  Pallas kernels  18.9 us (15%)
  blocking collectives  18.8 us (15%)
  between operations  13.7 us (11%)
  local copies, waits for them, and re-layouts  6.62 us (5%)
    all_to_all x1, blocking collectives, spread(): return lax.all_to_all(copies, 'col', 0, 0, axis_index_groups=lines)  18.8 us
    all_gather x1, waiting for transfers between devices, body(): lax.all_gather(line, 'col', axis=0, tiled=True, axis_index_groups=Z_LINES)  18.4 us
    pallas_call x1, Pallas kernels, multiply(): pl.pallas_call(multiply_kernel, grid=(RG,), out_shape=jax.ShapeDtypeStruc...  12.3 us
    all_to_all x2, waiting for transfers between devices, spread(): return lax.all_to_all(copies, 'col', 0, 0, axis_index_groups=lines)  11.5 us
    all_to_all x2, starting transfers between devices, spread(): return lax.all_to_all(copies, 'col', 0, 0, axis_index_groups=lines)  10.6 us
    ppermute x5, starting transfers between devices, gather_right(): return mine + [lax.ppermute(v, 'grp', SWAP_CORES) for v in others]  10.6 us
    ppermute x1, starting transfers between devices, gather_right(): far_head = lax.ppermute(onward[:R_ROWS // 2], 'grp', shift_x(1))  4.32 us
    ppermute x1, starting transfers between devices, gather_right(): before = lax.ppermute(own, 'grp', shift_x(1))  4.15 us
  transfers between devices with their start and end apart: 12, of which 4 were waited for; matrix products, arithmetic and copies ran while one was open for 2% of the time, Pallas kernels for 5%

profile of v7, /device:TPU:6, one launch (start us, length us, event | category | flops | bytes accessed | tf_op | source)
XLA Modules:
  0.0 126.4 jit_solution(1657189097039445271)
XLA Ops:
  6.5 0.0 copy-start.8
  6.5 0.0 copy-start.7
  6.5 0.9 slice.17
  7.5 0.8 broadcast_in_dim.6
  8.3 7.1 %all-to-all-start = ((bf16[8,224,128]{2,1,0:T(8,128)(2,1)}), bf16[8,224,128]{2,1,0:T(8,128)(2,1)S(1)}, u32[]{:S(2)}, u32[]{:S(2)}) async-start(bf16[8,224,128]{2,1,0:T(8,128)(2,1)} %broadcast_in_dim.6), calls=%async_computation | async-start | bytes 917504 | tf_op jit(solution)/shard_map/all_to_all | solution.py:230
  15.4 0.0 copy-done.8
  15.4 0.1 copy.8
  15.5 0.1 reshape.49
  15.6 0.0 copy-done.7
  15.6 0.0 copy-start.9
  15.6 0.0 copy-start.10
  15.6 0.1 fusion.1.refs_0_
  15.7 0.0 copy-start.1
  15.7 4.1 %collective-permute-start.1 = (bf16[4112,128]{1,0:T(8,128)(2,1)S(1)}, bf16[4112,128]{1,0:T(8,128)(2,1)}, u32[]{:S(2)}, u32[]{:S(2)}) collective-permute-start(bf16[4112,128]{1,0:T(8,128)(2,1)S(1)} %fusion.1.refs_0_), channel_id=1, source_target_pairs={{0,128},{64,192},{128,256},{192,320},{256,384},{320,448},{384,0},{... | collective-permute-start | bytes 3158024 | tf_op jit(solution)/shard_map/ppermute | solution.py:218
  19.9 1.9 %collective-permute-start = (bf16[4112,128]{1,0:T(8,128)(2,1)S(1)}, bf16[4112,128]{1,0:T(8,128)(2,1)S(1)}, u32[]{:S(2)}, u32[]{:S(2)}) collective-permute-start(bf16[4112,128]{1,0:T(8,128)(2,1)S(1)} %fusion.1.refs_0_), channel_id=1, source_target_pairs={{0,384},{64,448},{128,0},{192,64},{256,128},{320,192},{384,256},{4... | collective-permute-start | bytes 3158024 | tf_op jit(solution)/shard_map/ppermute | solution.py:217
  21.8 0.7 slice.16
  22.5 0.0 copy-done.9
  22.5 0.0 copy-done.10
  22.5 0.1 fusion.7
  22.6 8.9 %all-to-all-done = bf16[8,224,128]{2,1,0:T(8,128)(2,1)S(1)} async-done(((bf16[8,224,128]{2,1,0:T(8,128)(2,1)}), bf16[8,224,128]{2,1,0:T(8,128)(2,1)S(1)}, u32[]{:S(2)}, u32[]{:S(2)}) %all-to-all-start) | async-done | bytes 458784 | tf_op jit(solution)/shard_map/all_to_all | solution.py:230
  31.5 0.0 copy-start.6
  31.5 18.8 %all_to_all.15 = bf16[8,48,128]{2,1,0:T(8,128)(2,1)S(1)} all-to-all(bf16[8,48,128]{2,1,0:T(8,128)(2,1)S(1)} %broadcast_in_dim.7), channel_id=1, replica_groups={{0,8,16,24,32,40,48,56},{1,9,17,25,33,41,49,57},{2,10,18,26,34,42,50,58..., dimensions={0} | all-to-all | bytes 196608 | tf_op jit(solution)/shard_map/all_to_all | solution.py:230
  50.3 1.0 broadcast_in_dim.8
  51.3 0.0 copy-done.6
  51.3 3.5 %all-to-all-start.2 = ((bf16[8,8,48,128]{3,2,1,0:T(8,128)(2,1)}), bf16[8,8,48,128]{3,2,1,0:T(8,128)(2,1)S(1)}, u32[]{:S(2)}, u32[]{:S(2)}) async-start(bf16[8,8,48,128]{3,2,1,0:T(8,128)(2,1)} %broadcast_in_dim.8), calls=%async_computation.2 | async-start | bytes 1572864 | tf_op jit(solution)/shard_map/all_to_all | solution.py:230
  54.9 0.0 all-gather.2.cloned.1.call-start
  54.9 0.7 all-gather.2.cloned.1.call-update
  55.6 0.0 collective-permute-done.1.refs_4_
  55.6 0.0 collective-permute-done.refs_1_
  55.6 0.0 copy-start.2
  55.7 2.7 %collective-permute-start.3 = (bf16[2064,128]{1,0:T(8,128)(2,1)S(1)}, bf16[2064,128]{1,0:T(8,128)(2,1)S(1)}, u32[]{:S(2)}, u32[]{:S(2)}) collective-permute-start(bf16[2064,128]{1,0:T(8,128)(2,1)S(1)} %slice.15), channel_id=1, source_target_pairs={{0,384},{64,448},{128,0},{192,64},{256,128},{320,192},{384,256},{4... | collective-permute-start | bytes 1585160 | tf_op jit(solution)/shard_map/ppermute | solution.py:221
  58.4 1.1 slice.14
  59.5 4.3 %collective-permute-start.2 = (bf16[2048,128]{1,0:T(8,128)(2,1)S(1)}, bf16[2048,128]{1,0:T(8,128)(2,1)S(1)}, u32[]{:S(2)}, u32[]{:S(2)}) collective-permute-start(bf16[2048,128]{1,0:T(8,128)(2,1)S(1)} %slice.14), channel_id=1, source_target_pairs={{0,128},{64,192},{128,256},{192,320},{256,384},{320,448},{384,0},{... | collective-permute-start | bytes 1572872 | tf_op jit(solution)/shard_map/ppermute | solution.py:220
  63.8 1.9 %collective-permute-start.4 = (bf16[4112,128]{1,0:T(8,128)(2,1)S(1)}, bf16[4112,128]{1,0:T(8,128)(2,1)}, u32[]{:S(2)}, u32[]{:S(2)}) collective-permute-start(bf16[4112,128]{1,0:T(8,128)(2,1)S(1)} %fusion.1.refs_0_), channel_id=1, source_target_pairs={{0,64},{64,0},{128,192},{192,128},{256,320},{320,256},{384,448},{4... | collective-permute-start | bytes 3158024 | tf_op jit(solution)/shard_map/ppermute | solution.py:225
  65.8 2.4 %collective-permute-start.8 = (bf16[4112,128]{1,0:T(8,128)(2,1)}, bf16[4112,128]{1,0:T(8,128)(2,1)}, u32[]{:S(2)}, u32[]{:S(2)}) collective-permute-start(bf16[4112,128]{1,0:T(8,128)(2,1)} %collective-permute-done.1.refs_4_), channel_id=1, source_target_pairs={{0,64},{64,0},{128,192},{192,128},{256,320},{320,256},{384,448},{4... | collective-permute-start | bytes 3158024 | tf_op jit(solution)/shard_map/ppermute | solution.py:225
  68.2 1.9 %collective-permute-start.5 = (bf16[4112,128]{1,0:T(8,128)(2,1)S(1)}, bf16[4112,128]{1,0:T(8,128)(2,1)}, u32[]{:S(2)}, u32[]{:S(2)}) collective-permute-start(bf16[4112,128]{1,0:T(8,128)(2,1)S(1)} %collective-permute-done.refs_1_), channel_id=1, source_target_pairs={{0,64},{64,0},{128,192},{192,128},{256,320},{320,256},{384,448},{4... | collective-permute-start | bytes 3158024 | tf_op jit(solution)/shard_map/ppermute | solution.py:225
  70.1 3.2 %collective-permute-done.2.refs_2_ = bf16[2048,128]{1,0:T(8,128)(2,1)S(1)} collective-permute-done((bf16[2048,128]{1,0:T(8,128)(2,1)S(1)}, bf16[2048,128]{1,0:T(8,128)(2,1)S(1)}, u32[]{:S(2)}, u32[]{:S(2)}) %collective-permute-start.2) | collective-permute-done | bytes 524320 | tf_op jit(solution)/shard_map/ppermute | solution.py:220
  73.4 0.0 copy-start.4
  73.4 0.8 copy-done.4
  74.2 0.0 collective-permute-done.3.refs_3_
  74.2 0.0 copy-start.3
  74.2 2.6 %all-to-all-done.2.rest = bf16[8,8,48,128]{3,2,1,0:T(8,128)(2,1)S(1)} async-done(((bf16[8,8,48,128]{3,2,1,0:T(8,128)(2,1)}), bf16[8,8,48,128]{3,2,1,0:T(8,128)(2,1)S(1)}, u32[]{:S(2)}, u32[]{:S(2)}) %all-to-all-start.2) | async-done | bytes 786464 | tf_op jit(solution)/shard_map/all_to_all | solution.py:230
  76.7 0.0 copy-start
  76.7 1.9 %collective-permute-start.7 = (bf16[2064,128]{1,0:T(8,128)(2,1)S(1)}, bf16[2064,128]{1,0:T(8,128)(2,1)}, u32[]{:S(2)}, u32[]{:S(2)}) collective-permute-start(bf16[2064,128]{1,0:T(8,128)(2,1)S(1)} %collective-permute-done.3.refs_3_), channel_id=1, source_target_pairs={{0,64},{64,0},{128,192},{192,128},{256,320},{320,256},{384,448},{4... | collective-permute-start | bytes 1585160 | tf_op jit(solution)/shard_map/ppermute | solution.py:225
  78.7 2.4 %collective-permute-start.6 = (bf16[2048,128]{1,0:T(8,128)(2,1)}, bf16[2048,128]{1,0:T(8,128)(2,1)}, u32[]{:S(2)}, u32[]{:S(2)}) collective-permute-start(bf16[2048,128]{1,0:T(8,128)(2,1)} %copy-done.4), channel_id=1, source_target_pairs={{0,64},{64,0},{128,192},{192,128},{256,320},{320,256},{384,448},{4... | collective-permute-start | bytes 1572872 | tf_op jit(solution)/shard_map/ppermute | solution.py:225
  81.1 2.5 %shard_map.56 = (s32[128]{0:T(128)S(1)}, s32[128]{0:T(128)S(1)}) custom-call(bf16[8,8,48,128]{3,2,1,0:T(8,128)(2,1)S(1)} %all-to-all-done.2.rest), custom_call_target="tpu_custom_call" | custom-call | bytes 1048576 | tf_op jit(solution)/shard_map/pallas_call | solution.py:115
  83.6 0.0 collective-permute-done.4.refs_5_
  83.6 0.0 collective-permute-done.8.refs_9_
  83.6 0.0 collective-permute-done.5.refs_6_
  83.6 0.0 collective-permute-done.6.refs_7_
  83.6 0.0 collective-permute-done.7.refs_8_
  83.7 0.0 copy-done.1
  83.7 0.0 copy-done.2
  83.7 0.0 copy-start.5
  83.7 1.0 copy-done.5
  84.7 4.1 %shard_map.55.table = s32[512]{0:T(512)S(1)} custom-call(s32[1]{0:T(128)} %bitcast.place, bf16[4112,128]{1,0:T(8,128)(2,1)S(1)} %fusion.1.refs_0_, bf16[4112,128]{1,0:T(8,128)(2,1)S(1)} %collective-permute-done.refs_1_, bf16[2048,128]{1,0:T(8,128)(2,1)S(1)} %copy-done.5, bf16[2064,128]{1,0:T(8,128)(2,1)S(1)} %collective-permute-done.3.refs_3_, ...), custom_call_target="tpu_custom_call" | custom-call | flops 51539607552 | bytes 1048576 | tf_op jit(solution)/shard_map/pallas_call | solution.py:72
  88.8 0.0 copy-done.3
  88.8 0.0 copy-done
  88.8 18.4 %all-gather.2.cloned.1.call-done.left = bf16[64,224,128]{2,1,0:T(8,128)(2,1)} async-done(((bf16[8,224,128]{2,1,0:T(8,128)(2,1)}), bf16[64,224,128]{2,1,0:T(8,128)(2,1)}) %all-gather.2.cloned.1.call-update) | async-done | bytes 3670032 | tf_op jit(solution)/shard_map/all_gather | solution.py:237
  107.3 12.3 %shard_map.57 = bf16[1024,1024]{1,0:T(8,128)(2,1)} custom-call(s32[512]{0:T(512)S(1)} %shard_map.55.table, s32[128]{0:T(128)S(1)} %get-tuple-element.17.spots, s32[128]{0:T(128)S(1)} %get-tuple-element.18.inner, bf16[64,224,128]{2,1,0:T(8,128)(2,1)} %all-gather.2.cloned.1.call-done.left, bf16[8,8,48,128]{3,2,1,0:T(8,128)(2,1)} %copy-done, ...), custom_call_target="tpu_custom_call" | custom-call | flops 4294967296 | bytes 14680064 | tf_op jit(solution)/shard_map/pallas_call | solution.py:195
  (5 shorter events, 0.1 us)
Async XLA Ops:
  6.5 8.8 %copy-start.8 = (s32[8,4]{0,1:T(4,128)S(1)}, s32[8,4]{0,1:T(4,128)}, u32[]{:S(2)}) copy-start(s32[8,4]{0,1:T(4,128)} %param.9) | copy-start | bytes 388
  6.5 9.0 %copy-start.7 = (bf16[8,4,128,128]{3,2,1,0:T(8,128)(2,1)S(1)}, bf16[8,4,128,128]{3,2,1,0:T(8,128)(2,1)}, u32[]{:S(2)}) copy-start(bf16[8,4,128,128]{3,2,1,0:T(8,128)(2,1)} %param.8) | copy-start | bytes 3145732
  8.3 23.2 %all-to-all-start = ((bf16[8,224,128]{2,1,0:T(8,128)(2,1)}), bf16[8,224,128]{2,1,0:T(8,128)(2,1)S(1)}, u32[]{:S(2)}, u32[]{:S(2)}) async-start(bf16[8,224,128]{2,1,0:T(8,128)(2,1)} %broadcast_in_dim.6), calls=%async_computation | async-start | bytes 917504 | tf_op jit(solution)/shard_map/all_to_all | solution.py:230
  15.6 6.9 %copy-start.9 = (s32[2]{0:T(128)S(1)}, s32[2]{0:T(128)}, u32[]{:S(2)}) copy-start(s32[2]{0:T(128)} %param.7) | copy-start | bytes 28
  15.6 6.9 %copy-start.10 = (s32[2]{0:T(128)S(1)}, s32[2]{0:T(128)}, u32[]{:S(2)}) copy-start(s32[2]{0:T(128)} %param.6) | copy-start | bytes 28
  15.7 68.0 %copy-start.1 = (bf16[4112,128]{1,0:T(8,128)(2,1)}, bf16[4112,128]{1,0:T(8,128)(2,1)S(1)}, u32[]{:S(2)}) copy-start(bf16[4112,128]{1,0:T(8,128)(2,1)S(1)} %fusion.1.refs_0_) | copy-start | bytes 3158020
  15.7 39.9 %collective-permute-start.1 = (bf16[4112,128]{1,0:T(8,128)(2,1)S(1)}, bf16[4112,128]{1,0:T(8,128)(2,1)}, u32[]{:S(2)}, u32[]{:S(2)}) collective-permute-start(bf16[4112,128]{1,0:T(8,128)(2,1)S(1)} %fusion.1.refs_0_), channel_id=1, source_target_pairs={{0,128},{64,192},{128,256},{192,320},{256,384},{320,448},{384,0},{... | collective-permute-start | bytes 3158024 | tf_op jit(solution)/shard_map/ppermute | solution.py:218
  19.9 35.8 %collective-permute-start = (bf16[4112,128]{1,0:T(8,128)(2,1)S(1)}, bf16[4112,128]{1,0:T(8,128)(2,1)S(1)}, u32[]{:S(2)}, u32[]{:S(2)}) collective-permute-start(bf16[4112,128]{1,0:T(8,128)(2,1)S(1)} %fusion.1.refs_0_), channel_id=1, source_target_pairs={{0,384},{64,448},{128,0},{192,64},{256,128},{320,192},{384,256},{4... | collective-permute-start | bytes 3158024 | tf_op jit(solution)/shard_map/ppermute | solution.py:217
  31.5 19.8 %copy-start.6 = (bf16[8,224,128]{2,1,0:T(8,128)(2,1)}, bf16[8,224,128]{2,1,0:T(8,128)(2,1)S(1)}, u32[]{:S(2)}) copy-start(bf16[8,224,128]{2,1,0:T(8,128)(2,1)S(1)} %all-to-all-done) | copy-start | bytes 1376260
  51.3 25.4 %all-to-all-start.2 = ((bf16[8,8,48,128]{3,2,1,0:T(8,128)(2,1)}), bf16[8,8,48,128]{3,2,1,0:T(8,128)(2,1)S(1)}, u32[]{:S(2)}, u32[]{:S(2)}) async-start(bf16[8,8,48,128]{3,2,1,0:T(8,128)(2,1)} %broadcast_in_dim.8), calls=%async_computation.2 | async-start | bytes 1572864 | tf_op jit(solution)/shard_map/all_to_all | solution.py:230
  54.9 52.4 %all-gather.2.cloned.1.call-start = ((), (), s32[]{:S(2)}) async-start(), calls=%async_computation.3 | async-start | bytes 4128768 | tf_op jit(solution)/shard_map/all_gather | solution.py:237
  55.6 28.0 %copy-start.2 = (bf16[4112,128]{1,0:T(8,128)(2,1)}, bf16[4112,128]{1,0:T(8,128)(2,1)S(1)}, u32[]{:S(2)}) copy-start(bf16[4112,128]{1,0:T(8,128)(2,1)S(1)} %collective-permute-done.refs_1_) | copy-start | bytes 3158020
  55.7 18.5 %collective-permute-start.3 = (bf16[2064,128]{1,0:T(8,128)(2,1)S(1)}, bf16[2064,128]{1,0:T(8,128)(2,1)S(1)}, u32[]{:S(2)}, u32[]{:S(2)}) collective-permute-start(bf16[2064,128]{1,0:T(8,128)(2,1)S(1)} %slice.15), channel_id=1, source_target_pairs={{0,384},{64,448},{128,0},{192,64},{256,128},{320,192},{384,256},{4... | collective-permute-start | bytes 1585160 | tf_op jit(solution)/shard_map/ppermute | solution.py:221
  59.5 13.8 %collective-permute-start.2 = (bf16[2048,128]{1,0:T(8,128)(2,1)S(1)}, bf16[2048,128]{1,0:T(8,128)(2,1)S(1)}, u32[]{:S(2)}, u32[]{:S(2)}) collective-permute-start(bf16[2048,128]{1,0:T(8,128)(2,1)S(1)} %slice.14), channel_id=1, source_target_pairs={{0,128},{64,192},{128,256},{192,320},{256,384},{320,448},{384,0},{... | collective-permute-start | bytes 1572872 | tf_op jit(solution)/shard_map/ppermute | solution.py:220
  63.8 19.8 %collective-permute-start.4 = (bf16[4112,128]{1,0:T(8,128)(2,1)S(1)}, bf16[4112,128]{1,0:T(8,128)(2,1)}, u32[]{:S(2)}, u32[]{:S(2)}) collective-permute-start(bf16[4112,128]{1,0:T(8,128)(2,1)S(1)} %fusion.1.refs_0_), channel_id=1, source_target_pairs={{0,64},{64,0},{128,192},{192,128},{256,320},{320,256},{384,448},{4... | collective-permute-start | bytes 3158024 | tf_op jit(solution)/shard_map/ppermute | solution.py:225
  65.8 17.8 %collective-permute-start.8 = (bf16[4112,128]{1,0:T(8,128)(2,1)}, bf16[4112,128]{1,0:T(8,128)(2,1)}, u32[]{:S(2)}, u32[]{:S(2)}) collective-permute-start(bf16[4112,128]{1,0:T(8,128)(2,1)} %collective-permute-done.1.refs_4_), channel_id=1, source_target_pairs={{0,64},{64,0},{128,192},{192,128},{256,320},{320,256},{384,448},{4... | collective-permute-start | bytes 3158024 | tf_op jit(solution)/shard_map/ppermute | solution.py:225
  68.2 15.4 %collective-permute-start.5 = (bf16[4112,128]{1,0:T(8,128)(2,1)S(1)}, bf16[4112,128]{1,0:T(8,128)(2,1)}, u32[]{:S(2)}, u32[]{:S(2)}) collective-permute-start(bf16[4112,128]{1,0:T(8,128)(2,1)S(1)} %collective-permute-done.refs_1_), channel_id=1, source_target_pairs={{0,64},{64,0},{128,192},{192,128},{256,320},{320,256},{384,448},{4... | collective-permute-start | bytes 3158024 | tf_op jit(solution)/shard_map/ppermute | solution.py:225
  73.4 0.8 copy-start.4
  74.2 14.6 %copy-start.3 = (bf16[2064,128]{1,0:T(8,128)(2,1)}, bf16[2064,128]{1,0:T(8,128)(2,1)S(1)}, u32[]{:S(2)}) copy-start(bf16[2064,128]{1,0:T(8,128)(2,1)S(1)} %collective-permute-done.3.refs_3_) | copy-start | bytes 1585156
  76.7 12.1 %copy-start = (bf16[8,8,48,128]{3,2,1,0:T(8,128)(2,1)}, bf16[8,8,48,128]{3,2,1,0:T(8,128)(2,1)S(1)}, u32[]{:S(2)}) copy-start(bf16[8,8,48,128]{3,2,1,0:T(8,128)(2,1)S(1)} %all-to-all-done.2.rest) | copy-start | bytes 2359300
  76.7 6.9 %collective-permute-start.7 = (bf16[2064,128]{1,0:T(8,128)(2,1)S(1)}, bf16[2064,128]{1,0:T(8,128)(2,1)}, u32[]{:S(2)}, u32[]{:S(2)}) collective-permute-start(bf16[2064,128]{1,0:T(8,128)(2,1)S(1)} %collective-permute-done.3.refs_3_), channel_id=1, source_target_pairs={{0,64},{64,0},{128,192},{192,128},{256,320},{320,256},{384,448},{4... | collective-permute-start | bytes 1585160 | tf_op jit(solution)/shard_map/ppermute | solution.py:225
  78.7 5.0 %collective-permute-start.6 = (bf16[2048,128]{1,0:T(8,128)(2,1)}, bf16[2048,128]{1,0:T(8,128)(2,1)}, u32[]{:S(2)}, u32[]{:S(2)}) collective-permute-start(bf16[2048,128]{1,0:T(8,128)(2,1)} %copy-done.4), channel_id=1, source_target_pairs={{0,64},{64,0},{128,192},{192,128},{256,320},{320,256},{384,448},{4... | collective-permute-start | bytes 1572872 | tf_op jit(solution)/shard_map/ppermute | solution.py:225
  83.7 1.0 copy-start.5
Sparse Core Ops, SparseCore 0:
  57.8 49.4 all-gather.1

commit v8 on v7

--- a/solution.py
+++ b/solution.py
@@ -81,7 +81,7 @@
             pltpu.SemaphoreType.DMA((N_GRP,)),
         ],
         compiler_params=pltpu.CompilerParams(vmem_limit_bytes=2 * 2**20),
-        cost_estimate=pl.CostEstimate(flops=48 * 2**30, bytes_accessed=2**20, transcendentals=0),
+        cost_estimate=pl.CostEstimate(flops=40 * 2**30, bytes_accessed=2**20, transcendentals=0),
     )(place, *pieces)
 
 
@@ -125,7 +125,7 @@
             pltpu.SemaphoreType.DMA((1,)),
         ],
         compiler_params=pltpu.CompilerParams(vmem_limit_bytes=2 * 2**20),
-        cost_estimate=pl.CostEstimate(flops=0 * 2**30, bytes_accessed=2**20, transcendentals=0),
+        cost_estimate=pl.CostEstimate(flops=0, bytes_accessed=2**20, transcendentals=0),
     )(rest)
 
 

time: 128 us -> 111 us (0.87)
  waiting for transfers between devices: 33.8 us -> 16.1 us
    all_gather x1, waiting for transfers between devices: 18.4 us -> 0.02 us  [body(): lax.all_gather(line, 'col', axis=0, tiled=True, axis_index_groups=Z_LINES)]
    all_to_all x2, waiting for transfers between devices: 11.5 us -> 12.9 us  [spread(): return lax.all_to_all(copies, 'col', 0, 0, axis_index_groups=lines)]
  transfers between devices with their start and end apart: 12 -> 12, of which waited for: 4 -> 3; matrix products, arithmetic and copies ran while one was open for 2% -> 3% of each run, Pallas kernels for 5% -> 6%
where the time goes in v8:
time: 111 us; the launch traced here: 110 us
  starting transfers between devices  34.4 us (31%)
  blocking collectives  19 us (17%)
  Pallas kernels  18.8 us (17%)
  waiting for transfers between devices  16.1 us (15%)
  between operations  13.7 us (12%)
  local copies, waits for them, and re-layouts  7.41 us (7%)
    all_to_all x1, blocking collectives, spread(): return lax.all_to_all(copies, 'col', 0, 0, axis_index_groups=lines)  19 us
    all_to_all x2, waiting for transfers between devices, spread(): return lax.all_to_all(copies, 'col', 0, 0, axis_index_groups=lines)  12.9 us
    pallas_call x1, Pallas kernels, multiply(): pl.pallas_call(multiply_kernel, grid=(RG,), out_shape=jax.ShapeDtypeStruc...  12.2 us
    all_to_all x2, starting transfers between devices, spread(): return lax.all_to_all(copies, 'col', 0, 0, axis_index_groups=lines)  10.7 us
    ppermute x5, starting transfers between devices, gather_right(): return mine + [lax.ppermute(v, 'grp', SWAP_CORES) for v in others]  10.6 us
    ppermute x1, starting transfers between devices, gather_right(): far_head = lax.ppermute(onward[:R_ROWS // 2], 'grp', shift_x(1))  4.31 us
    ppermute x1, starting transfers between devices, gather_right(): before = lax.ppermute(own, 'grp', shift_x(1))  4.15 us
    pallas_call x1, Pallas kernels, make_table(): pl.pallas_call(table_kernel, out_shape=jax.ShapeDtypeStruct((KS * JB,), j...  4.1 us
  transfers between devices with their start and end apart: 12, of which 3 were waited for; matrix products, arithmetic and copies ran while one was open for 3% of the time, Pallas kernels for 6%

profile of v8, /device:TPU:6, one launch (start us, length us, event | category | flops | bytes accessed | tf_op | source)
XLA Modules:
  0.0 109.6 jit_solution(11281296559955715907)
XLA Ops:
  6.5 0.0 copy-start.8
  6.5 0.0 copy-start.7
  6.5 0.9 slice.17
  7.5 0.8 broadcast_in_dim.6
  8.3 7.1 %all-to-all-start = ((bf16[8,224,128]{2,1,0:T(8,128)(2,1)}), bf16[8,224,128]{2,1,0:T(8,128)(2,1)S(1)}, u32[]{:S(2)}, u32[]{:S(2)}) async-start(bf16[8,224,128]{2,1,0:T(8,128)(2,1)} %broadcast_in_dim.6), calls=%async_computation | async-start | bytes 917504 | tf_op jit(solution)/shard_map/all_to_all | solution.py:230
  15.4 0.0 all-gather.2.cloned.1.call-start
  15.4 0.0 copy-done.8
  15.4 0.1 copy.8
  15.5 0.1 reshape.49
  15.6 0.0 copy-done.7
  15.6 0.0 copy-start.9
  15.6 0.0 copy-start.10
  15.7 0.1 fusion.1.refs_0_
  15.7 0.0 copy-start.1
  15.7 4.1 %collective-permute-start.1 = (bf16[4112,128]{1,0:T(8,128)(2,1)S(1)}, bf16[4112,128]{1,0:T(8,128)(2,1)}, u32[]{:S(2)}, u32[]{:S(2)}) collective-permute-start(bf16[4112,128]{1,0:T(8,128)(2,1)S(1)} %fusion.1.refs_0_), channel_id=1, source_target_pairs={{0,128},{64,192},{128,256},{192,320},{256,384},{320,448},{384,0},{... | collective-permute-start | bytes 3158024 | tf_op jit(solution)/shard_map/ppermute | solution.py:218
  19.9 1.9 %collective-permute-start = (bf16[4112,128]{1,0:T(8,128)(2,1)S(1)}, bf16[4112,128]{1,0:T(8,128)(2,1)S(1)}, u32[]{:S(2)}, u32[]{:S(2)}) collective-permute-start(bf16[4112,128]{1,0:T(8,128)(2,1)S(1)} %fusion.1.refs_0_), channel_id=1, source_target_pairs={{0,384},{64,448},{128,0},{192,64},{256,128},{320,192},{384,256},{4... | collective-permute-start | bytes 3158024 | tf_op jit(solution)/shard_map/ppermute | solution.py:217
  21.8 9.6 %all-to-all-done = bf16[8,224,128]{2,1,0:T(8,128)(2,1)S(1)} async-done(((bf16[8,224,128]{2,1,0:T(8,128)(2,1)}), bf16[8,224,128]{2,1,0:T(8,128)(2,1)S(1)}, u32[]{:S(2)}, u32[]{:S(2)}) %all-to-all-start) | async-done | bytes 458784 | tf_op jit(solution)/shard_map/all_to_all | solution.py:230
  31.5 0.0 copy-start.6
  31.5 0.8 copy-done.6
  32.3 0.0 all-gather.2.cloned.1.call-update
  32.3 0.0 copy-done.9
  32.3 0.0 copy-done.10
  32.3 0.7 slice.16
  33.0 0.1 fusion.7
  33.1 19.0 %all_to_all.15 = bf16[8,48,128]{2,1,0:T(8,128)(2,1)S(1)} all-to-all(bf16[8,48,128]{2,1,0:T(8,128)(2,1)S(1)} %broadcast_in_dim.7), channel_id=1, replica_groups={{0,8,16,24,32,40,48,56},{1,9,17,25,33,41,49,57},{2,10,18,26,34,42,50,58..., dimensions={0} | all-to-all | bytes 196608 | tf_op jit(solution)/shard_map/all_to_all | solution.py:230
  52.1 1.0 broadcast_in_dim.8
  53.1 3.5 %all-to-all-start.2 = ((bf16[8,8,48,128]{3,2,1,0:T(8,128)(2,1)}), bf16[8,8,48,128]{3,2,1,0:T(8,128)(2,1)S(1)}, u32[]{:S(2)}, u32[]{:S(2)}) async-start(bf16[8,8,48,128]{3,2,1,0:T(8,128)(2,1)} %broadcast_in_dim.8), calls=%async_computation.2 | async-start | bytes 1572864 | tf_op jit(solution)/shard_map/all_to_all | solution.py:230
  56.6 0.0 collective-permute-done.1.refs_4_
  56.6 0.0 collective-permute-done.refs_1_
  56.6 0.0 copy-start.2
  56.7 2.7 %collective-permute-start.3 = (bf16[2064,128]{1,0:T(8,128)(2,1)S(1)}, bf16[2064,128]{1,0:T(8,128)(2,1)S(1)}, u32[]{:S(2)}, u32[]{:S(2)}) collective-permute-start(bf16[2064,128]{1,0:T(8,128)(2,1)S(1)} %slice.15), channel_id=1, source_target_pairs={{0,384},{64,448},{128,0},{192,64},{256,128},{320,192},{384,256},{4... | collective-permute-start | bytes 1585160 | tf_op jit(solution)/shard_map/ppermute | solution.py:221
  59.4 1.1 slice.14
  60.5 4.3 %collective-permute-start.2 = (bf16[2048,128]{1,0:T(8,128)(2,1)S(1)}, bf16[2048,128]{1,0:T(8,128)(2,1)S(1)}, u32[]{:S(2)}, u32[]{:S(2)}) collective-permute-start(bf16[2048,128]{1,0:T(8,128)(2,1)S(1)} %slice.14), channel_id=1, source_target_pairs={{0,128},{64,192},{128,256},{192,320},{256,384},{320,448},{384,0},{... | collective-permute-start | bytes 1572872 | tf_op jit(solution)/shard_map/ppermute | solution.py:220
  64.8 1.9 %collective-permute-start.4 = (bf16[4112,128]{1,0:T(8,128)(2,1)S(1)}, bf16[4112,128]{1,0:T(8,128)(2,1)}, u32[]{:S(2)}, u32[]{:S(2)}) collective-permute-start(bf16[4112,128]{1,0:T(8,128)(2,1)S(1)} %fusion.1.refs_0_), channel_id=1, source_target_pairs={{0,64},{64,0},{128,192},{192,128},{256,320},{320,256},{384,448},{4... | collective-permute-start | bytes 3158024 | tf_op jit(solution)/shard_map/ppermute | solution.py:225
  66.8 2.4 %collective-permute-start.8 = (bf16[4112,128]{1,0:T(8,128)(2,1)}, bf16[4112,128]{1,0:T(8,128)(2,1)}, u32[]{:S(2)}, u32[]{:S(2)}) collective-permute-start(bf16[4112,128]{1,0:T(8,128)(2,1)} %collective-permute-done.1.refs_4_), channel_id=1, source_target_pairs={{0,64},{64,0},{128,192},{192,128},{256,320},{320,256},{384,448},{4... | collective-permute-start | bytes 3158024 | tf_op jit(solution)/shard_map/ppermute | solution.py:225
  69.2 1.9 %collective-permute-start.5 = (bf16[4112,128]{1,0:T(8,128)(2,1)S(1)}, bf16[4112,128]{1,0:T(8,128)(2,1)}, u32[]{:S(2)}, u32[]{:S(2)}) collective-permute-start(bf16[4112,128]{1,0:T(8,128)(2,1)S(1)} %collective-permute-done.refs_1_), channel_id=1, source_target_pairs={{0,64},{64,0},{128,192},{192,128},{256,320},{320,256},{384,448},{4... | collective-permute-start | bytes 3158024 | tf_op jit(solution)/shard_map/ppermute | solution.py:225
  71.1 3.1 %collective-permute-done.2.refs_2_ = bf16[2048,128]{1,0:T(8,128)(2,1)S(1)} collective-permute-done((bf16[2048,128]{1,0:T(8,128)(2,1)S(1)}, bf16[2048,128]{1,0:T(8,128)(2,1)S(1)}, u32[]{:S(2)}, u32[]{:S(2)}) %collective-permute-start.2) | collective-permute-done | bytes 524320 | tf_op jit(solution)/shard_map/ppermute | solution.py:220
  74.3 0.0 copy-start.4
  74.3 0.8 copy-done.4
  75.1 0.0 collective-permute-done.3.refs_3_
  75.1 0.0 copy-start.3
  75.1 3.3 %all-to-all-done.2.rest = bf16[8,8,48,128]{3,2,1,0:T(8,128)(2,1)S(1)} async-done(((bf16[8,8,48,128]{3,2,1,0:T(8,128)(2,1)}), bf16[8,8,48,128]{3,2,1,0:T(8,128)(2,1)S(1)}, u32[]{:S(2)}, u32[]{:S(2)}) %all-to-all-start.2) | async-done | bytes 786464 | tf_op jit(solution)/shard_map/all_to_all | solution.py:230
  78.4 0.0 copy-start
  78.4 1.9 %collective-permute-start.7 = (bf16[2064,128]{1,0:T(8,128)(2,1)S(1)}, bf16[2064,128]{1,0:T(8,128)(2,1)}, u32[]{:S(2)}, u32[]{:S(2)}) collective-permute-start(bf16[2064,128]{1,0:T(8,128)(2,1)S(1)} %collective-permute-done.3.refs_3_), channel_id=1, source_target_pairs={{0,64},{64,0},{128,192},{192,128},{256,320},{320,256},{384,448},{4... | collective-permute-start | bytes 1585160 | tf_op jit(solution)/shard_map/ppermute | solution.py:225
  80.3 2.4 %collective-permute-start.6 = (bf16[2048,128]{1,0:T(8,128)(2,1)}, bf16[2048,128]{1,0:T(8,128)(2,1)}, u32[]{:S(2)}, u32[]{:S(2)}) collective-permute-start(bf16[2048,128]{1,0:T(8,128)(2,1)} %copy-done.4), channel_id=1, source_target_pairs={{0,64},{64,0},{128,192},{192,128},{256,320},{320,256},{384,448},{4... | collective-permute-start | bytes 1572872 | tf_op jit(solution)/shard_map/ppermute | solution.py:225
  82.7 2.5 %shard_map.56 = (s32[128]{0:T(128)S(1)}, s32[128]{0:T(128)S(1)}) custom-call(bf16[8,8,48,128]{3,2,1,0:T(8,128)(2,1)S(1)} %all-to-all-done.2.rest), custom_call_target="tpu_custom_call" | custom-call | bytes 1048576 | tf_op jit(solution)/shard_map/pallas_call | solution.py:115
  85.2 0.0 collective-permute-done.4.refs_5_
  85.2 0.0 collective-permute-done.8.refs_9_
  85.3 0.0 collective-permute-done.5.refs_6_
  85.3 0.0 collective-permute-done.6.refs_7_
  85.3 0.0 collective-permute-done.7.refs_8_
  85.3 0.0 copy-done.1
  85.3 0.0 copy-done.2
  85.3 0.0 copy-start.5
  85.3 1.0 copy-done.5
  86.4 4.1 %shard_map.55.table = s32[512]{0:T(512)S(1)} custom-call(s32[1]{0:T(128)} %bitcast.place, bf16[4112,128]{1,0:T(8,128)(2,1)S(1)} %fusion.1.refs_0_, bf16[4112,128]{1,0:T(8,128)(2,1)S(1)} %collective-permute-done.refs_1_, bf16[2048,128]{1,0:T(8,128)(2,1)S(1)} %copy-done.5, bf16[2064,128]{1,0:T(8,128)(2,1)S(1)} %collective-permute-done.3.refs_3_, ...), custom_call_target="tpu_custom_call" | custom-call | flops 42949672960 | bytes 1048576 | tf_op jit(solution)/shard_map/pallas_call | solution.py:72
  90.5 0.0 copy-done.3
  90.5 0.0 copy-done
  90.5 0.0 all-gather.2.cloned.1.call-done.left
  90.5 12.2 %shard_map.57 = bf16[1024,1024]{1,0:T(8,128)(2,1)} custom-call(s32[512]{0:T(512)S(1)} %shard_map.55.table, s32[128]{0:T(128)S(1)} %get-tuple-element.17.spots, s32[128]{0:T(128)S(1)} %get-tuple-element.18.inner, bf16[64,224,128]{2,1,0:T(8,128)(2,1)} %all-gather.2.cloned.1.call-done.left, bf16[8,8,48,128]{3,2,1,0:T(8,128)(2,1)} %copy-done, ...), custom_call_target="tpu_custom_call" | custom-call | flops 4294967296 | bytes 14680064 | tf_op jit(solution)/shard_map/pallas_call | solution.py:195
  (5 shorter events, 0.1 us)
Async XLA Ops:
  6.5 8.9 %copy-start.8 = (s32[8,4]{0,1:T(4,128)S(1)}, s32[8,4]{0,1:T(4,128)}, u32[]{:S(2)}) copy-start(s32[8,4]{0,1:T(4,128)} %param.9) | copy-start | bytes 388
  6.5 9.1 %copy-start.7 = (bf16[8,4,128,128]{3,2,1,0:T(8,128)(2,1)S(1)}, bf16[8,4,128,128]{3,2,1,0:T(8,128)(2,1)}, u32[]{:S(2)}) copy-start(bf16[8,4,128,128]{3,2,1,0:T(8,128)(2,1)} %param.8) | copy-start | bytes 3145732
  8.3 23.2 %all-to-all-start = ((bf16[8,224,128]{2,1,0:T(8,128)(2,1)}), bf16[8,224,128]{2,1,0:T(8,128)(2,1)S(1)}, u32[]{:S(2)}, u32[]{:S(2)}) async-start(bf16[8,224,128]{2,1,0:T(8,128)(2,1)} %broadcast_in_dim.6), calls=%async_computation | async-start | bytes 917504 | tf_op jit(solution)/shard_map/all_to_all | solution.py:230
  15.4 75.1 %all-gather.2.cloned.1.call-start = ((), (), s32[]{:S(2)}) async-start(), calls=%async_computation.3 | async-start | bytes 4128768 | tf_op jit(solution)/shard_map/all_gather | solution.py:237
  15.6 16.7 %copy-start.9 = (s32[2]{0:T(128)S(1)}, s32[2]{0:T(128)}, u32[]{:S(2)}) copy-start(s32[2]{0:T(128)} %param.7) | copy-start | bytes 28
  15.6 16.6 %copy-start.10 = (s32[2]{0:T(128)S(1)}, s32[2]{0:T(128)}, u32[]{:S(2)}) copy-start(s32[2]{0:T(128)} %param.6) | copy-start | bytes 28
  15.7 69.6 %copy-start.1 = (bf16[4112,128]{1,0:T(8,128)(2,1)}, bf16[4112,128]{1,0:T(8,128)(2,1)S(1)}, u32[]{:S(2)}) copy-start(bf16[4112,128]{1,0:T(8,128)(2,1)S(1)} %fusion.1.refs_0_) | copy-start | bytes 3158020
  15.7 40.9 %collective-permute-start.1 = (bf16[4112,128]{1,0:T(8,128)(2,1)S(1)}, bf16[4112,128]{1,0:T(8,128)(2,1)}, u32[]{:S(2)}, u32[]{:S(2)}) collective-permute-start(bf16[4112,128]{1,0:T(8,128)(2,1)S(1)} %fusion.1.refs_0_), channel_id=1, source_target_pairs={{0,128},{64,192},{128,256},{192,320},{256,384},{320,448},{384,0},{... | collective-permute-start | bytes 3158024 | tf_op jit(solution)/shard_map/ppermute | solution.py:218
  19.9 36.7 %collective-permute-start = (bf16[4112,128]{1,0:T(8,128)(2,1)S(1)}, bf16[4112,128]{1,0:T(8,128)(2,1)S(1)}, u32[]{:S(2)}, u32[]{:S(2)}) collective-permute-start(bf16[4112,128]{1,0:T(8,128)(2,1)S(1)} %fusion.1.refs_0_), channel_id=1, source_target_pairs={{0,384},{64,448},{128,0},{192,64},{256,128},{320,192},{384,256},{4... | collective-permute-start | bytes 3158024 | tf_op jit(solution)/shard_map/ppermute | solution.py:217
  31.5 0.8 copy-start.6
  53.1 25.3 %all-to-all-start.2 = ((bf16[8,8,48,128]{3,2,1,0:T(8,128)(2,1)}), bf16[8,8,48,128]{3,2,1,0:T(8,128)(2,1)S(1)}, u32[]{:S(2)}, u32[]{:S(2)}) async-start(bf16[8,8,48,128]{3,2,1,0:T(8,128)(2,1)} %broadcast_in_dim.8), calls=%async_computation.2 | async-start | bytes 1572864 | tf_op jit(solution)/shard_map/all_to_all | solution.py:230
  56.6 28.7 %copy-start.2 = (bf16[4112,128]{1,0:T(8,128)(2,1)}, bf16[4112,128]{1,0:T(8,128)(2,1)S(1)}, u32[]{:S(2)}) copy-start(bf16[4112,128]{1,0:T(8,128)(2,1)S(1)} %collective-permute-done.refs_1_) | copy-start | bytes 3158020
  56.7 18.4 %collective-permute-start.3 = (bf16[2064,128]{1,0:T(8,128)(2,1)S(1)}, bf16[2064,128]{1,0:T(8,128)(2,1)S(1)}, u32[]{:S(2)}, u32[]{:S(2)}) collective-permute-start(bf16[2064,128]{1,0:T(8,128)(2,1)S(1)} %slice.15), channel_id=1, source_target_pairs={{0,384},{64,448},{128,0},{192,64},{256,128},{320,192},{384,256},{4... | collective-permute-start | bytes 1585160 | tf_op jit(solution)/shard_map/ppermute | solution.py:221
  60.5 13.7 %collective-permute-start.2 = (bf16[2048,128]{1,0:T(8,128)(2,1)S(1)}, bf16[2048,128]{1,0:T(8,128)(2,1)S(1)}, u32[]{:S(2)}, u32[]{:S(2)}) collective-permute-start(bf16[2048,128]{1,0:T(8,128)(2,1)S(1)} %slice.14), channel_id=1, source_target_pairs={{0,128},{64,192},{128,256},{192,320},{256,384},{320,448},{384,0},{... | collective-permute-start | bytes 1572872 | tf_op jit(solution)/shard_map/ppermute | solution.py:220
  64.8 20.4 %collective-permute-start.4 = (bf16[4112,128]{1,0:T(8,128)(2,1)S(1)}, bf16[4112,128]{1,0:T(8,128)(2,1)}, u32[]{:S(2)}, u32[]{:S(2)}) collective-permute-start(bf16[4112,128]{1,0:T(8,128)(2,1)S(1)} %fusion.1.refs_0_), channel_id=1, source_target_pairs={{0,64},{64,0},{128,192},{192,128},{256,320},{320,256},{384,448},{4... | collective-permute-start | bytes 3158024 | tf_op jit(solution)/shard_map/ppermute | solution.py:225
  66.8 18.5 %collective-permute-start.8 = (bf16[4112,128]{1,0:T(8,128)(2,1)}, bf16[4112,128]{1,0:T(8,128)(2,1)}, u32[]{:S(2)}, u32[]{:S(2)}) collective-permute-start(bf16[4112,128]{1,0:T(8,128)(2,1)} %collective-permute-done.1.refs_4_), channel_id=1, source_target_pairs={{0,64},{64,0},{128,192},{192,128},{256,320},{320,256},{384,448},{4... | collective-permute-start | bytes 3158024 | tf_op jit(solution)/shard_map/ppermute | solution.py:225
  69.2 16.1 %collective-permute-start.5 = (bf16[4112,128]{1,0:T(8,128)(2,1)S(1)}, bf16[4112,128]{1,0:T(8,128)(2,1)}, u32[]{:S(2)}, u32[]{:S(2)}) collective-permute-start(bf16[4112,128]{1,0:T(8,128)(2,1)S(1)} %collective-permute-done.refs_1_), channel_id=1, source_target_pairs={{0,64},{64,0},{128,192},{192,128},{256,320},{320,256},{384,448},{4... | collective-permute-start | bytes 3158024 | tf_op jit(solution)/shard_map/ppermute | solution.py:225
  74.3 0.8 copy-start.4
  75.1 15.4 %copy-start.3 = (bf16[2064,128]{1,0:T(8,128)(2,1)}, bf16[2064,128]{1,0:T(8,128)(2,1)S(1)}, u32[]{:S(2)}) copy-start(bf16[2064,128]{1,0:T(8,128)(2,1)S(1)} %collective-permute-done.3.refs_3_) | copy-start | bytes 1585156
  78.4 12.1 %copy-start = (bf16[8,8,48,128]{3,2,1,0:T(8,128)(2,1)}, bf16[8,8,48,128]{3,2,1,0:T(8,128)(2,1)S(1)}, u32[]{:S(2)}) copy-start(bf16[8,8,48,128]{3,2,1,0:T(8,128)(2,1)S(1)} %all-to-all-done.2.rest) | copy-start | bytes 2359300
  78.4 6.9 %collective-permute-start.7 = (bf16[2064,128]{1,0:T(8,128)(2,1)S(1)}, bf16[2064,128]{1,0:T(8,128)(2,1)}, u32[]{:S(2)}, u32[]{:S(2)}) collective-permute-start(bf16[2064,128]{1,0:T(8,128)(2,1)S(1)} %collective-permute-done.3.refs_3_), channel_id=1, source_target_pairs={{0,64},{64,0},{128,192},{192,128},{256,320},{320,256},{384,448},{4... | collective-permute-start | bytes 1585160 | tf_op jit(solution)/shard_map/ppermute | solution.py:225
  80.3 5.0 %collective-permute-start.6 = (bf16[2048,128]{1,0:T(8,128)(2,1)}, bf16[2048,128]{1,0:T(8,128)(2,1)}, u32[]{:S(2)}, u32[]{:S(2)}) collective-permute-start(bf16[2048,128]{1,0:T(8,128)(2,1)} %copy-done.4), channel_id=1, source_target_pairs={{0,64},{64,0},{128,192},{192,128},{256,320},{320,256},{384,448},{4... | collective-permute-start | bytes 1572872 | tf_op jit(solution)/shard_map/ppermute | solution.py:225
  85.3 1.0 copy-start.5
Sparse Core Ops, SparseCore 0:
  32.4 53.0 all-gather.1

commit v9 on v8

--- a/solution.py
+++ b/solution.py
@@ -33,8 +33,8 @@
 Z_LINES = [[z * N_Y + y for z in range(N_Z)] for y in range(N_Y)]
 
 
-def table_kernel(place, *refs):
-    pieces, (table, tiles, values, columns, sem) = refs[:10], refs[10:]
+def columns_kernel(*refs):
+    pieces, (columns, tiles, values, sem) = refs[:10], refs[10:]
     pieces = [piece for piece in pieces if piece.shape[0] % BS]
     heads = [
         pltpu.make_async_copy(piece.at[pl.ds(piece.shape[0] - PAD, PAD)], tiles.at[n], sem.at[n])
@@ -47,42 +47,25 @@
     values[...] = tiles[:, 0, :].astype(jnp.float32).astype(jnp.int32)
     copy = pltpu.make_async_copy(values, columns, sem.at[0])
     copy.start()
-    own_x, own_core = place[0] // 2, place[0] % 2
-
-    def clear(i, carry):
-        table[i] = N_RIGHT * BS
-        return carry
-
-    lax.fori_loop(0, KS * JB, clear, 0, unroll=16)
     copy.wait()
 
-    def fill(k, carry):
-        g, i = k // OWN_K, k % OWN_K
-        s = ((g + own_core) % 2) * N_X + (g // 2 + N_X - own_x) % N_X
-        for m in range(NBR):
-            table[k * JB + columns[s, i * NBR + m]] = ((s * OWN_K + i) * NBR + m) * BS
-        return carry
-
-    lax.fori_loop(0, KS, fill, 0, unroll=2)
-
-
-def make_table(place, pieces):
+
+def read_columns(pieces):
     smem = pl.BlockSpec(memory_space=pltpu.SMEM)
     hbm = pl.BlockSpec(memory_space=pl.ANY)
     return pl.pallas_call(
-        table_kernel,
-        out_shape=jax.ShapeDtypeStruct((KS * JB,), jnp.int32),
-        in_specs=[smem] + [hbm] * len(pieces),
+        columns_kernel,
+        out_shape=jax.ShapeDtypeStruct((N_GRP, BS), jnp.int32),
+        in_specs=[hbm] * len(pieces),
         out_specs=smem,
         scratch_shapes=[
             pltpu.VMEM((N_GRP, PAD, BS), jnp.bfloat16),
             pltpu.VMEM((N_GRP, BS), jnp.int32),
-            pltpu.SMEM((N_GRP, BS), jnp.int32),
             pltpu.SemaphoreType.DMA((N_GRP,)),
         ],
         compiler_params=pltpu.CompilerParams(vmem_limit_bytes=2 * 2**20),
         cost_estimate=pl.CostEstimate(flops=40 * 2**30, bytes_accessed=2**20, transcendentals=0),
-    )(place, *pieces)
+    )(*pieces)
 
 
 def list_kernel(rest, spots, inner, tiles, values, ids, filled, sem):
@@ -129,8 +112,8 @@
     )(rest)
 
 
-def multiply_kernel(table, spots, inner, left, rest, *refs):
-    pieces, (out, held, strips, sem) = refs[:10], refs[10:]
+def multiply_kernel(place, columns, spots, inner, left, rest, *refs):
+    pieces, (out, held, strips, table, sem) = refs[:10], refs[10:]
     row = pl.program_id(0)
 
     @pl.when(row == 0)
@@ -168,6 +151,22 @@
             return carry
 
         lax.fori_loop(0, N_LEFT // 2, list_row, 0, unroll=2)
+        own_x, own_core = place[0] // 2, place[0] % 2
+
+        def clear(i, carry):
+            table[i] = N_RIGHT * BS
+            return carry
+
+        lax.fori_loop(0, KS * JB, clear, 0, unroll=16)
+
+        def fill(k, carry):
+            g, i = k // OWN_K, k % OWN_K
+            s = ((g + own_core) % 2) * N_X + (g // 2 + N_X - own_x) % N_X
+            for m in range(NBR):
+                table[k * JB + columns[s, i * NBR + m]] = ((s * OWN_K + i) * NBR + m) * BS
+            return carry
+
+        lax.fori_loop(0, KS, fill, 0, unroll=2)
         for copy in copies:
             copy.wait()
 
@@ -190,22 +189,23 @@
         ).astype(out.dtype)
 
 
-def multiply(table, lists, left, rest, pieces):
+def multiply(place, columns, lists, left, rest, pieces):
     hbm = pl.BlockSpec(memory_space=pl.ANY)
     return pl.pallas_call(
         multiply_kernel,
         grid=(RG,),
         out_shape=jax.ShapeDtypeStruct((RG * BS, JB * BS), jnp.bfloat16),
-        in_specs=[pl.BlockSpec(memory_space=pltpu.SMEM)] * 3 + [hbm] * (2 + len(pieces)),
+        in_specs=[pl.BlockSpec(memory_space=pltpu.SMEM)] * 4 + [hbm] * (2 + len(pieces)),
         out_specs=pl.BlockSpec((BS, JB * BS), lambda r: (r, 0)),
         scratch_shapes=[
             pltpu.VMEM(((N_RIGHT + 1) * BS, BS), jnp.bfloat16),
             pltpu.VMEM((RG, BS, PER_ROW * BS), jnp.bfloat16),
+            pltpu.SMEM((KS * JB,), jnp.int32),
             pltpu.SemaphoreType.DMA((RG + len(pieces),)),
         ],
         compiler_params=pltpu.CompilerParams(vmem_limit_bytes=24 * 2**20),
         cost_estimate=pl.CostEstimate(flops=4 * 2**30, bytes_accessed=14 * 2**20, transcendentals=0),
-    )(table, *lists, *(pltpu.with_memory_space_constraint(v, pltpu.HBM) for v in [left, rest, *pieces]))
+    )(place, columns, *lists, *(pltpu.with_memory_space_constraint(v, pltpu.HBM) for v in [left, rest, *pieces]))
 
 
 def tail(values):
@@ -241,8 +241,8 @@
     rest = spread(strip, Y_LINES)
     pieces = gather_right(right, strip, rest)
     place = lax.axis_index("grp").reshape(1)
-    table = make_table(place, pieces)
-    return multiply(table, make_lists(rest), lefts, rest, pieces)
+    columns = read_columns(pieces)
+    return multiply(place, columns, make_lists(rest), lefts, rest, pieces)
 
 
 def solution(mesh):

time: 111 us -> 109 us (0.982)
  Pallas kernels: 18.8 us -> 16.9 us
    pallas_call x1, Pallas kernels: 4.1 us -> 2.03 us  [read_columns(): pl.pallas_call(columns_kernel, out_shape=jax.ShapeDtypeStruct((N_GRP, BS)...]
  transfers between devices with their start and end apart: 12 -> 12, of which waited for: 3 -> 3; matrix products, arithmetic and copies ran while one was open for 3% -> 3% of each run, Pallas kernels for 6% -> 4%
where the time goes in v9:
time: 109 us; the launch traced here: 108 us
  starting transfers between devices  34.4 us (32%)
  blocking collectives  19 us (17%)
  Pallas kernels  16.9 us (16%)
  waiting for transfers between devices  16.1 us (15%)
  between operations  13.7 us (13%)
  local copies, waits for them, and re-layouts  7.41 us (7%)
    all_to_all x1, blocking collectives, spread(): return lax.all_to_all(copies, 'col', 0, 0, axis_index_groups=lines)  19 us
    all_to_all x2, waiting for transfers between devices, spread(): return lax.all_to_all(copies, 'col', 0, 0, axis_index_groups=lines)  12.9 us
    pallas_call x1, Pallas kernels, multiply(): pl.pallas_call(multiply_kernel, grid=(RG,), out_shape=jax.ShapeDtypeStruc...  12.3 us
    all_to_all x2, starting transfers between devices, spread(): return lax.all_to_all(copies, 'col', 0, 0, axis_index_groups=lines)  10.7 us
    ppermute x5, starting transfers between devices, gather_right(): return mine + [lax.ppermute(v, 'grp', SWAP_CORES) for v in others]  10.6 us
    ppermute x1, starting transfers between devices, gather_right(): far_head = lax.ppermute(onward[:R_ROWS // 2], 'grp', shift_x(1))  4.31 us
    ppermute x1, starting transfers between devices, gather_right(): before = lax.ppermute(own, 'grp', shift_x(1))  4.15 us
    ppermute x1, waiting for transfers between devices, gather_right(): far_head = lax.ppermute(onward[:R_ROWS // 2], 'grp', shift_x(1))  3.14 us
  transfers between devices with their start and end apart: 12, of which 3 were waited for; matrix products, arithmetic and copies ran while one was open for 3% of the time, Pallas kernels for 4%

profile of v9, /device:TPU:6, one launch (start us, length us, event | category | flops | bytes accessed | tf_op | source)
XLA Modules:
  0.0 107.6 jit_solution(9022935761790215471)
XLA Ops:
  6.5 0.0 copy-start.8
  6.5 0.0 copy-start.7
  6.5 0.9 slice.17
  7.5 0.8 broadcast_in_dim.6
  8.3 7.1 %all-to-all-start = ((bf16[8,224,128]{2,1,0:T(8,128)(2,1)}), bf16[8,224,128]{2,1,0:T(8,128)(2,1)S(1)}, u32[]{:S(2)}, u32[]{:S(2)}) async-start(bf16[8,224,128]{2,1,0:T(8,128)(2,1)} %broadcast_in_dim.6), calls=%async_computation | async-start | bytes 917504 | tf_op jit(solution)/shard_map/all_to_all | solution.py:230
  15.4 0.0 all-gather.2.cloned.1.call-start
  15.4 0.0 copy-done.8
  15.4 0.1 copy.8
  15.5 0.1 reshape.49
  15.6 0.0 copy-done.7
  15.6 0.0 copy-start.9
  15.6 0.0 copy-start.10
  15.7 0.1 fusion.1.refs_0_
  15.7 0.0 copy-start.1
  15.7 4.1 %collective-permute-start.1 = (bf16[4112,128]{1,0:T(8,128)(2,1)S(1)}, bf16[4112,128]{1,0:T(8,128)(2,1)}, u32[]{:S(2)}, u32[]{:S(2)}) collective-permute-start(bf16[4112,128]{1,0:T(8,128)(2,1)S(1)} %fusion.1.refs_0_), channel_id=1, source_target_pairs={{0,128},{64,192},{128,256},{192,320},{256,384},{320,448},{384,0},{... | collective-permute-start | bytes 3158024 | tf_op jit(solution)/shard_map/ppermute | solution.py:218
  19.9 1.9 %collective-permute-start = (bf16[4112,128]{1,0:T(8,128)(2,1)S(1)}, bf16[4112,128]{1,0:T(8,128)(2,1)S(1)}, u32[]{:S(2)}, u32[]{:S(2)}) collective-permute-start(bf16[4112,128]{1,0:T(8,128)(2,1)S(1)} %fusion.1.refs_0_), channel_id=1, source_target_pairs={{0,384},{64,448},{128,0},{192,64},{256,128},{320,192},{384,256},{4... | collective-permute-start | bytes 3158024 | tf_op jit(solution)/shard_map/ppermute | solution.py:217
  21.8 9.6 %all-to-all-done = bf16[8,224,128]{2,1,0:T(8,128)(2,1)S(1)} async-done(((bf16[8,224,128]{2,1,0:T(8,128)(2,1)}), bf16[8,224,128]{2,1,0:T(8,128)(2,1)S(1)}, u32[]{:S(2)}, u32[]{:S(2)}) %all-to-all-start) | async-done | bytes 458784 | tf_op jit(solution)/shard_map/all_to_all | solution.py:230
  31.5 0.0 copy-start.6
  31.5 0.8 copy-done.6
  32.3 0.0 all-gather.2.cloned.1.call-update
  32.3 0.0 copy-done.9
  32.3 0.0 copy-done.10
  32.3 0.7 slice.16
  33.0 0.1 fusion.7
  33.1 19.0 %all_to_all.15 = bf16[8,48,128]{2,1,0:T(8,128)(2,1)S(1)} all-to-all(bf16[8,48,128]{2,1,0:T(8,128)(2,1)S(1)} %broadcast_in_dim.7), channel_id=1, replica_groups={{0,8,16,24,32,40,48,56},{1,9,17,25,33,41,49,57},{2,10,18,26,34,42,50,58..., dimensions={0} | all-to-all | bytes 196608 | tf_op jit(solution)/shard_map/all_to_all | solution.py:230
  52.1 1.0 broadcast_in_dim.8
  53.1 3.5 %all-to-all-start.2 = ((bf16[8,8,48,128]{3,2,1,0:T(8,128)(2,1)}), bf16[8,8,48,128]{3,2,1,0:T(8,128)(2,1)S(1)}, u32[]{:S(2)}, u32[]{:S(2)}) async-start(bf16[8,8,48,128]{3,2,1,0:T(8,128)(2,1)} %broadcast_in_dim.8), calls=%async_computation.2 | async-start | bytes 1572864 | tf_op jit(solution)/shard_map/all_to_all | solution.py:230
  56.6 0.0 collective-permute-done.1.refs_4_
  56.6 0.0 collective-permute-done.refs_1_
  56.6 0.0 copy-start.2
  56.7 2.7 %collective-permute-start.3 = (bf16[2064,128]{1,0:T(8,128)(2,1)S(1)}, bf16[2064,128]{1,0:T(8,128)(2,1)S(1)}, u32[]{:S(2)}, u32[]{:S(2)}) collective-permute-start(bf16[2064,128]{1,0:T(8,128)(2,1)S(1)} %slice.15), channel_id=1, source_target_pairs={{0,384},{64,448},{128,0},{192,64},{256,128},{320,192},{384,256},{4... | collective-permute-start | bytes 1585160 | tf_op jit(solution)/shard_map/ppermute | solution.py:221
  59.4 1.1 %slice.14 = bf16[2048,128]{1,0:T(8,128)(2,1)S(1)} slice(bf16[4112,128]{1,0:T(8,128)(2,1)} %collective-permute-done.1.refs_4_), slice={[0:2048], [0:128]} | slice | bytes 1048576 | tf_op jit(solution)/shard_map/slice | solution.py:220
  60.5 4.3 %collective-permute-start.2 = (bf16[2048,128]{1,0:T(8,128)(2,1)S(1)}, bf16[2048,128]{1,0:T(8,128)(2,1)S(1)}, u32[]{:S(2)}, u32[]{:S(2)}) collective-permute-start(bf16[2048,128]{1,0:T(8,128)(2,1)S(1)} %slice.14), channel_id=1, source_target_pairs={{0,128},{64,192},{128,256},{192,320},{256,384},{320,448},{384,0},{... | collective-permute-start | bytes 1572872 | tf_op jit(solution)/shard_map/ppermute | solution.py:220
  64.8 1.9 %collective-permute-start.4 = (bf16[4112,128]{1,0:T(8,128)(2,1)S(1)}, bf16[4112,128]{1,0:T(8,128)(2,1)}, u32[]{:S(2)}, u32[]{:S(2)}) collective-permute-start(bf16[4112,128]{1,0:T(8,128)(2,1)S(1)} %fusion.1.refs_0_), channel_id=1, source_target_pairs={{0,64},{64,0},{128,192},{192,128},{256,320},{320,256},{384,448},{4... | collective-permute-start | bytes 3158024 | tf_op jit(solution)/shard_map/ppermute | solution.py:225
  66.8 2.4 %collective-permute-start.8 = (bf16[4112,128]{1,0:T(8,128)(2,1)}, bf16[4112,128]{1,0:T(8,128)(2,1)}, u32[]{:S(2)}, u32[]{:S(2)}) collective-permute-start(bf16[4112,128]{1,0:T(8,128)(2,1)} %collective-permute-done.1.refs_4_), channel_id=1, source_target_pairs={{0,64},{64,0},{128,192},{192,128},{256,320},{320,256},{384,448},{4... | collective-permute-start | bytes 3158024 | tf_op jit(solution)/shard_map/ppermute | solution.py:225
  69.2 1.9 %collective-permute-start.5 = (bf16[4112,128]{1,0:T(8,128)(2,1)S(1)}, bf16[4112,128]{1,0:T(8,128)(2,1)}, u32[]{:S(2)}, u32[]{:S(2)}) collective-permute-start(bf16[4112,128]{1,0:T(8,128)(2,1)S(1)} %collective-permute-done.refs_1_), channel_id=1, source_target_pairs={{0,64},{64,0},{128,192},{192,128},{256,320},{320,256},{384,448},{4... | collective-permute-start | bytes 3158024 | tf_op jit(solution)/shard_map/ppermute | solution.py:225
  71.1 3.1 %collective-permute-done.2.refs_2_ = bf16[2048,128]{1,0:T(8,128)(2,1)S(1)} collective-permute-done((bf16[2048,128]{1,0:T(8,128)(2,1)S(1)}, bf16[2048,128]{1,0:T(8,128)(2,1)S(1)}, u32[]{:S(2)}, u32[]{:S(2)}) %collective-permute-start.2) | collective-permute-done | bytes 524320 | tf_op jit(solution)/shard_map/ppermute | solution.py:220
  74.3 0.0 copy-start.4
  74.3 0.8 copy-done.4
  75.1 0.0 collective-permute-done.3.refs_3_
  75.1 0.0 copy-start.3
  75.1 3.3 %all-to-all-done.2.rest = bf16[8,8,48,128]{3,2,1,0:T(8,128)(2,1)S(1)} async-done(((bf16[8,8,48,128]{3,2,1,0:T(8,128)(2,1)}), bf16[8,8,48,128]{3,2,1,0:T(8,128)(2,1)S(1)}, u32[]{:S(2)}, u32[]{:S(2)}) %all-to-all-start.2) | async-done | bytes 786464 | tf_op jit(solution)/shard_map/all_to_all | solution.py:230
  78.4 0.0 copy-start
  78.4 1.9 %collective-permute-start.7 = (bf16[2064,128]{1,0:T(8,128)(2,1)S(1)}, bf16[2064,128]{1,0:T(8,128)(2,1)}, u32[]{:S(2)}, u32[]{:S(2)}) collective-permute-start(bf16[2064,128]{1,0:T(8,128)(2,1)S(1)} %collective-permute-done.3.refs_3_), channel_id=1, source_target_pairs={{0,64},{64,0},{128,192},{192,128},{256,320},{320,256},{384,448},{4... | collective-permute-start | bytes 1585160 | tf_op jit(solution)/shard_map/ppermute | solution.py:225
  80.3 2.4 %collective-permute-start.6 = (bf16[2048,128]{1,0:T(8,128)(2,1)}, bf16[2048,128]{1,0:T(8,128)(2,1)}, u32[]{:S(2)}, u32[]{:S(2)}) collective-permute-start(bf16[2048,128]{1,0:T(8,128)(2,1)} %copy-done.4), channel_id=1, source_target_pairs={{0,64},{64,0},{128,192},{192,128},{256,320},{320,256},{384,448},{4... | collective-permute-start | bytes 1572872 | tf_op jit(solution)/shard_map/ppermute | solution.py:225
  82.7 2.5 %shard_map.56 = (s32[128]{0:T(128)S(1)}, s32[128]{0:T(128)S(1)}) custom-call(bf16[8,8,48,128]{3,2,1,0:T(8,128)(2,1)S(1)} %all-to-all-done.2.rest), custom_call_target="tpu_custom_call" | custom-call | bytes 1048576 | tf_op jit(solution)/shard_map/pallas_call | solution.py:98
  85.2 0.0 collective-permute-done.4.refs_5_
  85.2 0.0 collective-permute-done.8.refs_9_
  85.3 0.0 collective-permute-done.5.refs_6_
  85.3 0.0 collective-permute-done.6.refs_7_
  85.3 0.0 collective-permute-done.7.refs_8_
  85.3 0.0 copy-done.1
  85.3 0.0 copy-done.2
  85.3 0.0 copy-start.5
  85.3 1.0 copy-done.5
  86.4 2.0 %shard_map.55.columns = s32[8,128]{1,0:T(8,128)S(1)} custom-call(bf16[4112,128]{1,0:T(8,128)(2,1)S(1)} %fusion.1.refs_0_, bf16[4112,128]{1,0:T(8,128)(2,1)S(1)} %collective-permute-done.refs_1_, bf16[2048,128]{1,0:T(8,128)(2,1)S(1)} %copy-done.5, bf16[2064,128]{1,0:T(8,128)(2,1)S(1)} %collective-permute-done.3.refs_3_, ...), custom_call_target="tpu_custom_call" | custom-call | flops 42949672960 | bytes 1048576 | tf_op jit(solution)/shard_map/pallas_call | solution.py:56
  88.4 0.0 copy-done.3
  88.4 0.0 copy-done
  88.4 0.0 all-gather.2.cloned.1.call-done.left
  88.4 12.3 %shard_map.57 = bf16[1024,1024]{1,0:T(8,128)(2,1)} custom-call(s32[1]{0:T(128)} %bitcast.place, s32[8,128]{1,0:T(8,128)S(1)} %shard_map.55.columns, s32[128]{0:T(128)S(1)} %get-tuple-element.17.spots, s32[128]{0:T(128)S(1)} %get-tuple-element.18.inner, bf16[64,224,128]{2,1,0:T(8,128)(2,1)} %all-gather.2.cloned.1.call-done.left, ...), custom_call_target="tpu_custom_call" | custom-call | flops 4294967296 | bytes 14680064 | tf_op jit(solution)/shard_map/pallas_call | solution.py:194
  (5 shorter events, 0.1 us)
Async XLA Ops:
  6.5 8.9 %copy-start.8 = (s32[8,4]{0,1:T(4,128)S(1)}, s32[8,4]{0,1:T(4,128)}, u32[]{:S(2)}) copy-start(s32[8,4]{0,1:T(4,128)} %param.9) | copy-start | bytes 388
  6.5 9.1 %copy-start.7 = (bf16[8,4,128,128]{3,2,1,0:T(8,128)(2,1)S(1)}, bf16[8,4,128,128]{3,2,1,0:T(8,128)(2,1)}, u32[]{:S(2)}) copy-start(bf16[8,4,128,128]{3,2,1,0:T(8,128)(2,1)} %param.8) | copy-start | bytes 3145732
  8.3 23.2 %all-to-all-start = ((bf16[8,224,128]{2,1,0:T(8,128)(2,1)}), bf16[8,224,128]{2,1,0:T(8,128)(2,1)S(1)}, u32[]{:S(2)}, u32[]{:S(2)}) async-start(bf16[8,224,128]{2,1,0:T(8,128)(2,1)} %broadcast_in_dim.6), calls=%async_computation | async-start | bytes 917504 | tf_op jit(solution)/shard_map/all_to_all | solution.py:230
  15.4 73.0 %all-gather.2.cloned.1.call-start = ((), (), s32[]{:S(2)}) async-start(), calls=%async_computation.3 | async-start | bytes 4128768 | tf_op jit(solution)/shard_map/all_gather | solution.py:237
  15.6 16.7 %copy-start.9 = (s32[2]{0:T(128)S(1)}, s32[2]{0:T(128)}, u32[]{:S(2)}) copy-start(s32[2]{0:T(128)} %param.7) | copy-start | bytes 28
  15.6 16.6 %copy-start.10 = (s32[2]{0:T(128)S(1)}, s32[2]{0:T(128)}, u32[]{:S(2)}) copy-start(s32[2]{0:T(128)} %param.6) | copy-start | bytes 28
  15.7 69.6 %copy-start.1 = (bf16[4112,128]{1,0:T(8,128)(2,1)}, bf16[4112,128]{1,0:T(8,128)(2,1)S(1)}, u32[]{:S(2)}) copy-start(bf16[4112,128]{1,0:T(8,128)(2,1)S(1)} %fusion.1.refs_0_) | copy-start | bytes 3158020
  15.7 40.9 %collective-permute-start.1 = (bf16[4112,128]{1,0:T(8,128)(2,1)S(1)}, bf16[4112,128]{1,0:T(8,128)(2,1)}, u32[]{:S(2)}, u32[]{:S(2)}) collective-permute-start(bf16[4112,128]{1,0:T(8,128)(2,1)S(1)} %fusion.1.refs_0_), channel_id=1, source_target_pairs={{0,128},{64,192},{128,256},{192,320},{256,384},{320,448},{384,0},{... | collective-permute-start | bytes 3158024 | tf_op jit(solution)/shard_map/ppermute | solution.py:218
  19.9 36.7 %collective-permute-start = (bf16[4112,128]{1,0:T(8,128)(2,1)S(1)}, bf16[4112,128]{1,0:T(8,128)(2,1)S(1)}, u32[]{:S(2)}, u32[]{:S(2)}) collective-permute-start(bf16[4112,128]{1,0:T(8,128)(2,1)S(1)} %fusion.1.refs_0_), channel_id=1, source_target_pairs={{0,384},{64,448},{128,0},{192,64},{256,128},{320,192},{384,256},{4... | collective-permute-start | bytes 3158024 | tf_op jit(solution)/shard_map/ppermute | solution.py:217
  31.5 0.8 copy-start.6
  53.1 25.3 %all-to-all-start.2 = ((bf16[8,8,48,128]{3,2,1,0:T(8,128)(2,1)}), bf16[8,8,48,128]{3,2,1,0:T(8,128)(2,1)S(1)}, u32[]{:S(2)}, u32[]{:S(2)}) async-start(bf16[8,8,48,128]{3,2,1,0:T(8,128)(2,1)} %broadcast_in_dim.8), calls=%async_computation.2 | async-start | bytes 1572864 | tf_op jit(solution)/shard_map/all_to_all | solution.py:230
  56.6 28.7 %copy-start.2 = (bf16[4112,128]{1,0:T(8,128)(2,1)}, bf16[4112,128]{1,0:T(8,128)(2,1)S(1)}, u32[]{:S(2)}) copy-start(bf16[4112,128]{1,0:T(8,128)(2,1)S(1)} %collective-permute-done.refs_1_) | copy-start | bytes 3158020
  56.7 18.4 %collective-permute-start.3 = (bf16[2064,128]{1,0:T(8,128)(2,1)S(1)}, bf16[2064,128]{1,0:T(8,128)(2,1)S(1)}, u32[]{:S(2)}, u32[]{:S(2)}) collective-permute-start(bf16[2064,128]{1,0:T(8,128)(2,1)S(1)} %slice.15), channel_id=1, source_target_pairs={{0,384},{64,448},{128,0},{192,64},{256,128},{320,192},{384,256},{4... | collective-permute-start | bytes 1585160 | tf_op jit(solution)/shard_map/ppermute | solution.py:221
  60.5 13.7 %collective-permute-start.2 = (bf16[2048,128]{1,0:T(8,128)(2,1)S(1)}, bf16[2048,128]{1,0:T(8,128)(2,1)S(1)}, u32[]{:S(2)}, u32[]{:S(2)}) collective-permute-start(bf16[2048,128]{1,0:T(8,128)(2,1)S(1)} %slice.14), channel_id=1, source_target_pairs={{0,128},{64,192},{128,256},{192,320},{256,384},{320,448},{384,0},{... | collective-permute-start | bytes 1572872 | tf_op jit(solution)/shard_map/ppermute | solution.py:220
  64.8 20.4 %collective-permute-start.4 = (bf16[4112,128]{1,0:T(8,128)(2,1)S(1)}, bf16[4112,128]{1,0:T(8,128)(2,1)}, u32[]{:S(2)}, u32[]{:S(2)}) collective-permute-start(bf16[4112,128]{1,0:T(8,128)(2,1)S(1)} %fusion.1.refs_0_), channel_id=1, source_target_pairs={{0,64},{64,0},{128,192},{192,128},{256,320},{320,256},{384,448},{4... | collective-permute-start | bytes 3158024 | tf_op jit(solution)/shard_map/ppermute | solution.py:225
  66.8 18.5 %collective-permute-start.8 = (bf16[4112,128]{1,0:T(8,128)(2,1)}, bf16[4112,128]{1,0:T(8,128)(2,1)}, u32[]{:S(2)}, u32[]{:S(2)}) collective-permute-start(bf16[4112,128]{1,0:T(8,128)(2,1)} %collective-permute-done.1.refs_4_), channel_id=1, source_target_pairs={{0,64},{64,0},{128,192},{192,128},{256,320},{320,256},{384,448},{4... | collective-permute-start | bytes 3158024 | tf_op jit(solution)/shard_map/ppermute | solution.py:225
  69.2 16.1 %collective-permute-start.5 = (bf16[4112,128]{1,0:T(8,128)(2,1)S(1)}, bf16[4112,128]{1,0:T(8,128)(2,1)}, u32[]{:S(2)}, u32[]{:S(2)}) collective-permute-start(bf16[4112,128]{1,0:T(8,128)(2,1)S(1)} %collective-permute-done.refs_1_), channel_id=1, source_target_pairs={{0,64},{64,0},{128,192},{192,128},{256,320},{320,256},{384,448},{4... | collective-permute-start | bytes 3158024 | tf_op jit(solution)/shard_map/ppermute | solution.py:225
  74.3 0.8 copy-start.4
  75.1 13.3 %copy-start.3 = (bf16[2064,128]{1,0:T(8,128)(2,1)}, bf16[2064,128]{1,0:T(8,128)(2,1)S(1)}, u32[]{:S(2)}) copy-start(bf16[2064,128]{1,0:T(8,128)(2,1)S(1)} %collective-permute-done.3.refs_3_) | copy-start | bytes 1585156
  78.4 10.0 %copy-start = (bf16[8,8,48,128]{3,2,1,0:T(8,128)(2,1)}, bf16[8,8,48,128]{3,2,1,0:T(8,128)(2,1)S(1)}, u32[]{:S(2)}) copy-start(bf16[8,8,48,128]{3,2,1,0:T(8,128)(2,1)S(1)} %all-to-all-done.2.rest) | copy-start | bytes 2359300
  78.4 6.9 %collective-permute-start.7 = (bf16[2064,128]{1,0:T(8,128)(2,1)S(1)}, bf16[2064,128]{1,0:T(8,128)(2,1)}, u32[]{:S(2)}, u32[]{:S(2)}) collective-permute-start(bf16[2064,128]{1,0:T(8,128)(2,1)S(1)} %collective-permute-done.3.refs_3_), channel_id=1, source_target_pairs={{0,64},{64,0},{128,192},{192,128},{256,320},{320,256},{384,448},{4... | collective-permute-start | bytes 1585160 | tf_op jit(solution)/shard_map/ppermute | solution.py:225
  80.3 5.0 %collective-permute-start.6 = (bf16[2048,128]{1,0:T(8,128)(2,1)}, bf16[2048,128]{1,0:T(8,128)(2,1)}, u32[]{:S(2)}, u32[]{:S(2)}) collective-permute-start(bf16[2048,128]{1,0:T(8,128)(2,1)} %copy-done.4), channel_id=1, source_target_pairs={{0,64},{64,0},{128,192},{192,128},{256,320},{320,256},{384,448},{4... | collective-permute-start | bytes 1572872 | tf_op jit(solution)/shard_map/ppermute | solution.py:225
  85.3 1.0 copy-start.5
Sparse Core Ops, SparseCore 0:
  32.4 53.0 all-gather.1
